TPU v7x, 32 devices: a whole 2x2x4 slice. The times are simulated.
32 devices in a mesh: grp: 2 (over y), op: 4 (over z), blk: 2 (over x), rep: 2 (over core).
Axes of the slice: x: 2, y: 2, z: 4, core: 2. Of those that a mesh axis runs over, the one named last changes fastest.
Arguments:
- wavefunction: bfloat16 [96, 128, 128], P(('grp', 'blk', 'rep')), parts along dimension 0, may hold values from -1 to 1
- left_env: bfloat16 [256, 128, 128], P(('grp', 'op')), parts along dimension 0, may hold values from -0.5 to 0.5
- right_env: bfloat16 [256, 128, 128], P(('grp', 'op')), parts along dimension 0, may hold values from -0.5 to 0.5
- slot_table: int32 [3, 4, 2, 2, 2, 64], P(None, 'op', 'blk'), may hold values from 0 to 31, as said below
Outputs:
- sigma_tiles: float32 [128, 96, 128], P(('op', 'rep'), ('grp', 'blk')), parts along dimension 1
There are 2 independent parts, one for each index of `grp`. A program takes and returns all parts, laid end to end along the dimension named above; an argument that names none is the same for every part. Nothing has to cross between parts.
Inputs may be any that keep to these rules, and one draw needn't show every extreme that they name: `slot_table`: at [0, o, b, r, b2, c] a term index below 32 among the terms of op index o; at [1, ...] a target block below 24 of tile group b, or 24 for an empty slot; at [2, ...] a source block below 12 of the wavefunction shard of tile group b2 and sector subset r. Each list of 64 slots has at least one non-empty slot, and in every draw all lists of some op index are full.
All inputs are finite; a program needn't handle non-finite values.
Results may differ from a plain program's by a relative error of at most 0.0029.
Values may be sent and summed in bfloat16 or wider, within the bound.
No kernel may reach another device: no remote copies, remote signals or barrier semaphores. Data moves between devices by JAX's collectives and lax.ppermute only.
A program may use at most 64 MiB of HBM per device.

v0:
```python
import jax
import jax.numpy as jnp
from jax import lax
from jax.sharding import PartitionSpec as P


def partial_sigma(row_env, right_env, gathered, slot_terms, slot_targets, slot_sources, tiles_blk):
    block_width = right_env.shape[2]
    row_total = row_env.shape[1]

    def one_group(running, slot_group):
        terms_now, targets_now, sources_now = slot_group
        left_rows = row_env[terms_now]
        tile_rows = gathered[sources_now]
        inner_prod = jnp.einsum(
            "cik,ckj->cij", left_rows, tile_rows, preferred_element_type=jnp.float32
        ).astype(jnp.bfloat16)
        outer_prod = jnp.einsum(
            "cik,cjk->cij", inner_prod, right_env[terms_now], preferred_element_type=jnp.float32
        )
        onehot = (targets_now[None, :] == lax.iota(jnp.int32, tiles_blk)[:, None]).astype(
            jnp.float32
        )
        running = running + jnp.einsum(
            "tc,cij->itj", onehot, outer_prod, precision=lax.Precision.HIGHEST
        )
        return (running, None)

    zero_term = jnp.zeros((row_total, tiles_blk, block_width), jnp.float32)
    running, _ = lax.scan(one_group, zero_term, (slot_terms, slot_targets, slot_sources))
    return running


def shards(wavefunction, left_env, right_env, slot_table):
    tiles_dev = wavefunction.shape[0]
    blk_count = lax.axis_size("blk")
    rep_count = lax.axis_size("rep")
    tiles_blk = tiles_dev * rep_count
    own_slots = slot_table[:, 0, 0]
    fields = lax.dynamic_index_in_dim(own_slots, lax.axis_index("rep"), 1, keepdims=False)
    offsets = tiles_dev * lax.iota(jnp.int32, blk_count)[:, None]
    gathered = lax.all_gather(wavefunction, "blk", axis=0, tiled=True)
    partial_sum = partial_sigma(
        left_env, right_env, gathered, fields[0], fields[1], fields[2] + offsets, tiles_blk
    )
    return lax.psum_scatter(partial_sum, ("op", "rep"), scatter_dimension=0, tiled=True)


def solution(mesh):
    placed = (
        P(("grp", "blk", "rep"), None, None),
        P(("grp", "op"), None, None),
        P(("grp", "op"), None, None),
        P(None, "op", "blk", None, None, None),
    )
    return jax.shard_map(
        shards,
        mesh=mesh,
        in_specs=placed,
        out_specs=P(("op", "rep"), ("grp", "blk"), None),
        check_vma=False,
    )
```

profile of v0, /device:TPU:0, one launch (start us, length us, event | category | flops | bytes accessed | tf_op | source)
XLA Modules:
  0.0 106.5 jit_solution(14097505922691722471)
XLA Ops:
  6.5 0.0 reduce-scatter.2.cloned.1.call-start
  6.5 13.0 %all_gather.3 = bf16[24,128,128]{2,1,0:T(8,128)(2,1)S(1)} all-gather(bf16[12,128,128]{2,1,0:T(8,128)(2,1)} %param.6), channel_id=1, replica_groups=mesh['grp'=2,'op'=4,'blk'=2,'rep'=2] {'blk'}, dimensions={0}, use_global_device_ids=true | all-gather | bytes 1179648 | tf_op jit(solution)/shard_map/all_gather | solution.py:42
  19.5 0.7 dynamic-slice_bitcast_fusion
  20.2 0.7 fusion.16
  21.0 42.8 %while.11 = (s32[]{:T(128)}, f32[128,24,128]{2,1,0:T(8,128)}, s32[2,64]{1,0:T(2,128)S(1)}, bf16[32,128,128]{2,1,0:T(8,128)(2,1)}, s32[2,64]{1,0:T(2,128)S(1)}, /...) while((s32[]{:T(128)}, f32[128,24,128]{2,1,0:T(8,128)}, ...), condition=%wide.region_1.2_spmd.clone, body=%wide.region_0.1_spmd.clone.sunk | while | flops 840699776 | bytes 30420084 | solution.py:30
  21.0 2.2 %gather_fusion.1 = bf16[64,128,128]{2,1,0:T(8,128)(2,1)S(1)} fusion(bf16[32,128,128]{2,1,0:T(8,128)(2,1)} %get-tuple-element.171, s32[1024]{0:T(1024)S(1)} %pad_clamp_fusion.4), kind=kCustom, calls=%fused_computation.clone.clone.1 | custom fusion | bytes 4194560 | tf_op jit(solution)/shard_map/while/body/eval_jaxpr/gather | solution.py:13
  23.2 3.4 %gather_fusion = bf16[64,128,128]{2,1,0:T(8,128)(2,1)} fusion(bf16[32,128,128]{2,1,0:T(8,128)(2,1)} %get-tuple-element.174, s32[1024]{0:T(1024)S(1)} %pad_clamp_fusion.4), kind=kCustom, calls=%fused_computation.2.clone.clone.1 | custom fusion | bytes 4194560 | tf_op jit(solution)/shard_map/while/body/eval_jaxpr/gather | solution.py:19
  26.5 2.2 %gather_fusion.2 = bf16[64,128,128]{2,1,0:T(8,128)(2,1)} fusion(bf16[24,128,128]{2,1,0:T(8,128)(2,1)S(1)} %get-tuple-element.173, s32[1024]{0:T(1024)S(1)} %pad_clamp_fusion.5), kind=kCustom, calls=%fused_computation.1.clone.clone.1 | custom fusion | bytes 4194560 | tf_op jit(solution)/shard_map/while/body/eval_jaxpr/gather | solution.py:14
  28.7 6.3 %fusion.36 = f32[64,128,128]{2,1,0:T(8,128)} fusion(bf16[64,128,128]{2,1,0:T(8,128)(2,1)} %gather_fusion, bf16[64,128,128]{2,1,0:T(8,128)(2,1)S(1)} %gather_fusion.1, bf16[64,128,128]{2,1,0:T(8,128)(2,1)} %gather_fusion.2), kind=kOutput, calls=%fused_computation.5.clone.1 | convolution fusion | flops 537919488 | bytes 10485760 | tf_op jit(solution)/shard_map/while/body/eval_jaxpr/cik,cjk->cij/dot_general | solution.py:18
  35.0 7.1 %bitcast_add_fusion.2 = f32[128,24,128]{2,1,0:T(8,128)} fusion(f32[128,24,128]{2,1,0:T(8,128)} %get-tuple-element.159, f32[64,128,128]{2,1,0:T(8,128)} %fusion.36, pred[]{:T(512)S(6)} %compare.3, s32[64]{0:T(128)S(1)} %fusion.37), kind=kOutput, calls=%fused_computation.8.clone.1 | convolution fusion | flops 302777856 | bytes 7340289 | tf_op jit(solution)/shard_map/while/body/eval_jaxpr/tc,cij->itj/dot_general | solution.py:24
  42.1 2.2 %gather_fusion.1 = bf16[64,128,128]{2,1,0:T(8,128)(2,1)S(1)} fusion(bf16[32,128,128]{2,1,0:T(8,128)(2,1)} %get-tuple-element.171, s32[1024]{0:T(1024)S(1)} %pad_clamp_fusion.4), kind=kCustom, calls=%fused_computation.clone.clone.1 | custom fusion | bytes 4194560 | tf_op jit(solution)/shard_map/while/body/eval_jaxpr/gather | solution.py:13
  44.3 3.4 %gather_fusion = bf16[64,128,128]{2,1,0:T(8,128)(2,1)} fusion(bf16[32,128,128]{2,1,0:T(8,128)(2,1)} %get-tuple-element.174, s32[1024]{0:T(1024)S(1)} %pad_clamp_fusion.4), kind=kCustom, calls=%fused_computation.2.clone.clone.1 | custom fusion | bytes 4194560 | tf_op jit(solution)/shard_map/while/body/eval_jaxpr/gather | solution.py:19
  47.7 2.2 %gather_fusion.2 = bf16[64,128,128]{2,1,0:T(8,128)(2,1)} fusion(bf16[24,128,128]{2,1,0:T(8,128)(2,1)S(1)} %get-tuple-element.173, s32[1024]{0:T(1024)S(1)} %pad_clamp_fusion.5), kind=kCustom, calls=%fused_computation.1.clone.clone.1 | custom fusion | bytes 4194560 | tf_op jit(solution)/shard_map/while/body/eval_jaxpr/gather | solution.py:14
  49.8 6.3 %fusion.36 = f32[64,128,128]{2,1,0:T(8,128)} fusion(bf16[64,128,128]{2,1,0:T(8,128)(2,1)} %gather_fusion, bf16[64,128,128]{2,1,0:T(8,128)(2,1)S(1)} %gather_fusion.1, bf16[64,128,128]{2,1,0:T(8,128)(2,1)} %gather_fusion.2), kind=kOutput, calls=%fused_computation.5.clone.1 | convolution fusion | flops 537919488 | bytes 10485760 | tf_op jit(solution)/shard_map/while/body/eval_jaxpr/cik,cjk->cij/dot_general | solution.py:18
  56.1 7.6 %bitcast_add_fusion.2 = f32[128,24,128]{2,1,0:T(8,128)} fusion(f32[128,24,128]{2,1,0:T(8,128)} %get-tuple-element.159, f32[64,128,128]{2,1,0:T(8,128)} %fusion.36, pred[]{:T(512)S(6)} %compare.3, s32[64]{0:T(128)S(1)} %fusion.37), kind=kOutput, calls=%fused_computation.8.clone.1 | convolution fusion | flops 302777856 | bytes 7340289 | tf_op jit(solution)/shard_map/while/body/eval_jaxpr/tc,cij->itj/dot_general | solution.py:24
  63.7 0.0 reduce-scatter.2.cloned.1.call-update
  63.8 35.9 %reduce-scatter.2.cloned.1.call-done = f32[16,24,128]{2,1,0:T(8,128)} async-done(((f32[128,24,128]{2,1,0:T(8,128)}), f32[16,24,128]{2,1,0:T(8,128)}) %reduce-scatter.2.cloned.1.call-update) | async-done | bytes 196624 | tf_op jit(solution)/shard_map/reduce_scatter | solution.py:46
  (10 shorter events, 0.1 us)
Async XLA Ops:
  6.5 93.2 %reduce-scatter.2.cloned.1.call-start = ((), (), s32[]{:S(2)}) async-start(), calls=%async_computation.1 | async-start | bytes 1769472 | tf_op jit(solution)/shard_map/reduce_scatter | solution.py:46
Sparse Core Ops, SparseCore 0:
  63.9 35.7 reduce-scatter.1
where the time goes:
time: 107 us
  waiting for transfers between devices  36 us (34%)
  matrix products  27.3 us (26%)
  local copies, waits for them, and re-layouts  16.1 us (15%)
  between operations  13.4 us (13%)
  blocking collectives  13 us (12%)
    reduce_scatter x1, waiting for transfers between devices, shards(): lax.psum_scatter(partial_sum, ('op', 'rep'), scatter_dimension=0, tiled=T...  35.9 us
    dot_general x2, matrix products, one_group(): jnp.einsum('tc,cij->itj', onehot, outer_prod, precision=lax.Precision.HIG...  14.7 us
    all_gather x1, blocking collectives, shards(): gathered = lax.all_gather(wavefunction, 'blk', axis=0, tiled=True)  13 us
    dot_general x2, matrix products, one_group(): jnp.einsum('cik,cjk->cij', inner_prod, right_env[terms_now], preferred_el...  12.6 us
    gather x2, local copies, waits for them, and re-layouts, one_group(): right_env[terms_now]  6.7 us
    gather x2, local copies, waits for them, and re-layouts, one_group(): left_rows = row_env[terms_now]  4.35 us
    gather x2, local copies, waits for them, and re-layouts, one_group(): tile_rows = gathered[sources_now]  4.31 us
  transfers between devices with their start and end apart: 1, of which 1 were waited for; matrix products, arithmetic and copies ran while one was open for 0% of the time, Pallas kernels for 0%

commit v1 on v0

v1 whole, which is shorter than its diff:
```python
import functools

import jax
import jax.numpy as jnp
from jax import lax
from jax.experimental import pallas as pl
from jax.experimental.pallas import tpu as pltpu
from jax.sharding import PartitionSpec as P

VMEM = pl.BlockSpec(memory_space=pltpu.VMEM)
SMEM = pl.BlockSpec(memory_space=pltpu.SMEM)
LINK = jnp.bfloat16


def params():
    return pltpu.CompilerParams(vmem_limit_bytes=24 << 20)


def add_list(table, rep, src, left, right, wave, acc, unroll):
    caps = table.shape[-1]

    def body(step, carry):
        base = step * unroll
        slots = [base + q for q in range(unroll)]
        terms = [table[0, 0, 0, rep, src, c] for c in slots]
        inner = [
            jnp.dot(
                left[terms[q]],
                wave[table[2, 0, 0, rep, src, slots[q]]],
                preferred_element_type=jnp.float32,
            ).astype(jnp.bfloat16)
            for q in range(unroll)
        ]
        outer = [
            lax.dot_general(
                inner[q],
                right[terms[q]],
                (((1,), (1,)), ((), ())),
                preferred_element_type=jnp.float32,
            )
            for q in range(unroll)
        ]
        for q in range(unroll):
            acc[table[1, 0, 0, rep, src, slots[q]]] += outer[q]
        return carry

    lax.fori_loop(0, caps // unroll, body, 0)


def unroll_of(caps):
    return next(u for u in (16, 8, 4, 2, 1) if caps % u == 0)


def own_kernel(where, table, left, right, wave, acc):
    acc[...] = jnp.zeros_like(acc)
    add_list(table, where[0], where[1], left, right, wave, acc, unroll_of(table.shape[-1]))


def other_kernel(where, table, left, right, wave, start, acc):
    acc[...] = start[...]
    add_list(table, where[0], where[1], left, right, wave, acc, unroll_of(table.shape[-1]))


def last_kernel(where, table, left, right, wave, start, keep, send, acc):
    acc[...] = start[...]
    rep = where[0]
    add_list(table, rep, where[1], left, right, wave, acc, unroll_of(table.shape[-1]))
    groups, tiles, rows, _ = keep.shape
    reps = 2
    for g in range(groups):
        mine = pl.multiple_of((g * reps + rep) * rows, rows)
        theirs = pl.multiple_of((g * reps + 1 - rep) * rows, rows)
        keep[g] = acc[pl.ds(0, tiles), pl.ds(mine, rows), :]
        send[g] = acc[pl.ds(0, tiles), pl.ds(theirs, rows), :].astype(LINK)


def pair_kernel(where, keep, got, own, *sends):
    op = where[2]
    own[...] = keep[op] + got[op].astype(jnp.float32)
    for s, out in enumerate(sends):
        to = jnp.bitwise_xor(op, s + 1)
        out[...] = (keep[to] + got[to].astype(jnp.float32)).astype(LINK)


def final_kernel(own, *rest):
    got, out = rest[:-1], rest[-1]
    total = own[...]
    for g in got:
        total = total + g[...].astype(jnp.float32)
    for t in range(total.shape[0]):
        out[:, t, :] = total[t]


def shards(wavefunction, left_env, right_env, slot_table):
    tiles_dev, width, _ = wavefunction.shape
    blk_count = lax.axis_size("blk")
    rep_count = lax.axis_size("rep")
    op_count = lax.axis_size("op")
    tiles_blk = tiles_dev * rep_count
    rep, blk, op = (lax.axis_index(a) for a in ("rep", "blk", "op"))
    row_total = left_env.shape[1]
    rows = row_total // (op_count * rep_count)
    acc_shape = jax.ShapeDtypeStruct((tiles_blk + 1, row_total, width), jnp.float32)

    others = [
        lax.ppermute(wavefunction, "blk", [((i + s) % blk_count, i) for i in range(blk_count)])
        for s in range(1, blk_count)
    ]
    wheres = [
        jnp.stack([rep, (blk + s) % blk_count, op]).astype(jnp.int32) for s in range(blk_count)
    ]
    acc = pl.pallas_call(
        own_kernel,
        out_shape=acc_shape,
        in_specs=[SMEM, SMEM, VMEM, VMEM, VMEM],
        out_specs=VMEM,
        compiler_params=params(),
    )(wheres[0], slot_table, left_env, right_env, wavefunction)

    fast = rep_count == 2 and rows % 16 == 0 and op_count & (op_count - 1) == 0
    middle = others[:-1] if fast else others
    for s, wave in enumerate(middle):
        acc = pl.pallas_call(
            other_kernel,
            out_shape=acc_shape,
            in_specs=[SMEM, SMEM, VMEM, VMEM, VMEM, VMEM],
            out_specs=VMEM,
            compiler_params=params(),
        )(wheres[s + 1], slot_table, left_env, right_env, wave, acc)
    if not fast:
        partial = jnp.swapaxes(acc[:tiles_blk], 0, 1)
        return lax.psum_scatter(partial, ("op", "rep"), scatter_dimension=0, tiled=True)

    part = (op_count, tiles_blk, rows, width)
    keep, send = pl.pallas_call(
        last_kernel,
        out_shape=(
            jax.ShapeDtypeStruct(part, jnp.float32),
            jax.ShapeDtypeStruct(part, LINK),
        ),
        in_specs=[SMEM, SMEM, VMEM, VMEM, VMEM, VMEM],
        out_specs=(VMEM, VMEM),
        scratch_shapes=[pltpu.VMEM(acc_shape.shape, jnp.float32)],
        compiler_params=params(),
    )(wheres[-1], slot_table, left_env, right_env, others[-1], acc)
    got = lax.ppermute(send, "rep", [(0, 1), (1, 0)])
    tile_rows = part[1:]
    own, *sends = pl.pallas_call(
        pair_kernel,
        out_shape=(jax.ShapeDtypeStruct(tile_rows, jnp.float32),)
        + (jax.ShapeDtypeStruct(tile_rows, LINK),) * (op_count - 1),
        in_specs=[SMEM, VMEM, VMEM],
        out_specs=(VMEM,) * op_count,
        compiler_params=params(),
    )(wheres[0], keep, got)
    arrived = [
        lax.ppermute(x, "op", [(i, i ^ (s + 1)) for i in range(op_count)])
        for s, x in enumerate(sends)
    ]
    return pl.pallas_call(
        final_kernel,
        out_shape=jax.ShapeDtypeStruct((rows, tiles_blk, width), jnp.float32),
        in_specs=[VMEM] * op_count,
        out_specs=VMEM,
        compiler_params=params(),
    )(own, *arrived)


def solution(mesh):
    placed = (
        P(("grp", "blk", "rep"), None, None),
        P(("grp", "op"), None, None),
        P(("grp", "op"), None, None),
        P(None, "op", "blk", None, None, None),
    )
    return jax.shard_map(
        shards,
        mesh=mesh,
        in_specs=placed,
        out_specs=P(("op", "rep"), ("grp", "blk"), None),
        check_vma=False,
    )
```

time: 107 us -> 31.9 us (0.30)
  matrix products: 27.3 us -> 0 us
  waiting for transfers between devices: 36 us -> 11.4 us
  between operations: 13.4 us -> 0.04 us
  blocking collectives: 13 us -> 0 us
  local copies, waits for them, and re-layouts: 16.1 us -> 4.14 us
  Pallas kernels: 0 us -> 8.43 us
  starting transfers between devices: 0.01 us -> 7.53 us
    reduce_scatter x1 -> x0, waiting for transfers between devices: 35.9 us -> none  [shards(): lax.psum_scatter(partial_sum, ('op', 'rep'), scatter_dimension=0, tiled=T...]
    dot_general x4 -> x0, matrix products: 27.3 us -> none  [the longest x2 14.7 us: one_group(): jnp.einsum('tc,cij->itj', onehot, outer_prod, precision=lax.Precision.HIG...]
    gather x6 -> x0, local copies, waits for them, and re-layouts: 15.4 us -> none  [the longest x2 6.7 us: one_group(): right_env[terms_now]]
    all_gather x1 -> x0, blocking collectives: 13 us -> none  [shards(): gathered = lax.all_gather(wavefunction, 'blk', axis=0, tiled=True)]
    ppermute x0 -> x5, waiting for transfers between devices: none -> 11.4 us  [the longest x3 8.08 us: shards(): lax.ppermute(x, 'op', [(i, i ^ s + 1) for i in range(op_count)])]
    pallas_call x0 -> x4, Pallas kernels: none -> 8.43 us  [the longest x1 3.54 us: shards(): pl.pallas_call(last_kernel, out_shape=(jax.ShapeDtypeStruct(part, jnp.flo...]
    ppermute x0 -> x5, starting transfers between devices: none -> 7.53 us  [the longest x3 4.52 us: shards(): lax.ppermute(x, 'op', [(i, i ^ s + 1) for i in range(op_count)])]
    unnamed x0 -> x10, local copies, waits for them, and re-layouts: none -> 4.14 us
  transfers between devices with their start and end apart: 1 -> 5, of which waited for: 1 -> 4; matrix products, arithmetic and copies ran while one was open for 0% -> 0% of each run, Pallas kernels for 0% -> 11%
where the time goes in v1:
time: 31.9 us; the launch traced here: 31.7 us
  waiting for transfers between devices  11.4 us (36%)
  Pallas kernels  8.43 us (26%)
  starting transfers between devices  7.53 us (24%)
  local copies, waits for them, and re-layouts  4.14 us (13%)
    ppermute x3, waiting for transfers between devices, shards(): lax.ppermute(x, 'op', [(i, i ^ s + 1) for i in range(op_count)])  8.08 us
    ppermute x3, starting transfers between devices, shards(): lax.ppermute(x, 'op', [(i, i ^ s + 1) for i in range(op_count)])  4.52 us
    unnamed x10, local copies, waits for them, and re-layouts  4.14 us
    pallas_call x1, Pallas kernels, shards(): pl.pallas_call(last_kernel, out_shape=(jax.ShapeDtypeStruct(part, jnp.flo...  3.54 us
    pallas_call x1, Pallas kernels, shards(): pl.pallas_call(own_kernel, out_shape=acc_shape, in_specs=[SMEM, SMEM, VME...  3.44 us
    ppermute x1, starting transfers between devices, shards(): lax.ppermute(wavefunction, 'blk', [((i + s) % blk_count, i) for i in rang...  2.94 us
    ppermute x1, waiting for transfers between devices, shards(): got = lax.ppermute(send, 'rep', [(0, 1), (1, 0)])  1.71 us
    ppermute x1, waiting for transfers between devices, shards(): lax.ppermute(wavefunction, 'blk', [((i + s) % blk_count, i) for i in rang...  1.66 us
  transfers between devices with their start and end apart: 5, of which 4 were waited for; matrix products, arithmetic and copies ran while one was open for 0% of the time, Pallas kernels for 11%

profile of v1, /device:TPU:0, one launch (start us, length us, event | category | flops | bytes accessed | tf_op | source)
XLA Modules:
  0.0 31.7 jit_solution(15546751031718884839)
XLA Ops:
  0.0 2.9 %collective-permute-start = (bf16[12,128,128]{2,1,0:T(8,128)(2,1)}, bf16[12,128,128]{2,1,0:T(8,128)(2,1)S(1)}, u32[]{:S(2)}, u32[]{:S(2)}) collective-permute-start(bf16[12,128,128]{2,1,0:T(8,128)(2,1)} %wave.1), channel_id=1, source_target_pairs={{2,0},{0,2},{3,1},{1,3},{6,4},{4,6},{7,5},{5,7},{10,8},{8,10},{11,... | collective-permute-start | bytes 1179656 | tf_op jit(solution)/shard_map/ppermute | solution.py:106
  2.9 0.1 add_add_fusion
  3.0 0.0 copy-start
  3.0 1.2 %copy-done = bf16[32,128,128]{2,1,0:T(8,128)(2,1)S(1)} copy-done((bf16[32,128,128]{2,1,0:T(8,128)(2,1)S(1)}, bf16[32,128,128]{2,1,0:T(8,128)(2,1)}, u32[]{:S(2)}) %copy-start) | copy-done | bytes 1048600
  4.2 0.0 copy-start.2
  4.2 1.2 %copy-done.2 = bf16[32,128,128]{2,1,0:T(8,128)(2,1)S(1)} copy-done((bf16[32,128,128]{2,1,0:T(8,128)(2,1)S(1)}, bf16[32,128,128]{2,1,0:T(8,128)(2,1)}, u32[]{:S(2)}) %copy-start.2) | copy-done | bytes 1048600
  5.5 0.0 copy-start.3
  5.5 1.0 %copy-done.3 = bf16[12,128,128]{2,1,0:T(8,128)(2,1)S(1)} copy-done((bf16[12,128,128]{2,1,0:T(8,128)(2,1)S(1)}, bf16[12,128,128]{2,1,0:T(8,128)(2,1)}, u32[]{:S(2)}) %copy-start.3) | copy-done | bytes 393240
  6.5 0.0 copy-start.4
  6.5 0.7 %copy-done.4 = s32[3,1,1,2,2,64]{5,4,3,2,1,0:T(2,128)S(1)} copy-done((s32[3,1,1,2,2,64]{5,4,3,2,1,0:T(2,128)S(1)}, s32[3,1,1,2,2,64]{5,4,3,2,1,0:T(2,128)}, u32[]{:S(2)}) %copy-start.4) | copy-done | bytes 3096
  7.2 0.0 copy-start.1
  7.2 3.4 %shard_map.46.start = f32[25,128,128]{2,1,0:T(8,128)S(1)} custom-call(s32[3]{0:T(128)S(1)} %get-tuple-element.17.where, s32[3,1,1,2,2,64]{5,4,3,2,1,0:T(2,128)S(1)} %copy-done.4, bf16[32,128,128]{2,1,0:T(8,128)(2,1)S(1)} %copy-done, bf16[32,128,128]{2,1,0:T(8,128)(2,1)S(1)} %copy-done.2, bf16[12,128,128]{2,1,0:T(8,128)(2,1)S(1)} %copy-done.3), custom_call_target="tpu_custom_call" | custom-call | tf_op jit(solution)/shard_map/pallas_call | solution.py:112
  10.6 1.7 %collective-permute-done.wave = bf16[12,128,128]{2,1,0:T(8,128)(2,1)S(1)} collective-permute-done((bf16[12,128,128]{2,1,0:T(8,128)(2,1)}, bf16[12,128,128]{2,1,0:T(8,128)(2,1)S(1)}, u32[]{:S(2)}, u32[]{:S(2)}) %collective-permute-start) | collective-permute-done | bytes 393248 | tf_op jit(solution)/shard_map/ppermute | solution.py:106
  12.3 0.0 copy-done.1
  12.3 3.5 %shard_map.47 = (f32[4,24,16,128]{3,2,1,0:T(8,128)S(1)}, bf16[4,24,16,128]{3,2,1,0:T(8,128)(2,1)S(1)}) custom-call(s32[3]{0:T(128)S(1)} %get-tuple-element.18.where, s32[3,1,1,2,2,64]{5,4,3,2,1,0:T(2,128)S(1)} %copy-done.4, bf16[32,128,128]{2,1,0:T(8,128)(2,1)S(1)} %copy-done.1, bf16[32,128,128]{2,1,0:T(8,128)(2,1)S(1)} %copy-done.2, ...), custom_call_target="tpu_custom_call" | custom-call | tf_op jit(solution)/shard_map/pallas_call | solution.py:135
  15.8 0.1 collective-permute-start.1
  15.9 1.7 %collective-permute-done.1.got = bf16[4,24,16,128]{3,2,1,0:T(8,128)(2,1)S(1)} collective-permute-done((bf16[4,24,16,128]{3,2,1,0:T(8,128)(2,1)S(1)}, bf16[4,24,16,128]{3,2,1,0:T(8,128)(2,1)S(1)}, u32[]{:S(2)}, u32[]{:S(2)}) %collective-permute-start.1) | collective-permute-done | bytes 393248 | tf_op jit(solution)/shard_map/ppermute | solution.py:146
  17.6 0.6 %shard_map.48 = (f32[24,16,128]{2,1,0:T(8,128)S(1)}, bf16[24,16,128]{2,1,0:T(8,128)(2,1)S(1)}, bf16[24,16,128]{2,1,0:T(8,128)(2,1)S(1)}, bf16[24,16,128]{2,1,0:T(8,128)(2,1)S(1)}) custom-call(s32[3]{0:T(128)S(1)} %get-tuple-element.17.where, f32[4,24,16,128]{3,2,1,0:T(8,128)S(1)} %get-tuple-element.11.keep, ...), custom_call_target="tpu_custom_call" | custom-call | tf_op jit(solution)/shard_map/pallas_call | solution.py:148
  18.2 1.9 %collective-permute-start.2 = (bf16[24,16,128]{2,1,0:T(8,128)(2,1)S(1)}, bf16[24,16,128]{2,1,0:T(8,128)(2,1)S(1)}, u32[]{:S(2)}, u32[]{:S(2)}) collective-permute-start(bf16[24,16,128]{2,1,0:T(8,128)(2,1)S(1)} %get-tuple-element.14), channel_id=1, source_target_pairs={{0,4},{4,0},{8,12},{12,8},{1,5},{5,1},{9,13},{13,9},{2,6},{6,2},{1... | collective-permute-start | bytes 294920 | tf_op jit(solution)/shard_map/ppermute | solution.py:157
  20.2 2.6 %collective-permute-start.3 = (bf16[24,16,128]{2,1,0:T(8,128)(2,1)S(1)}, bf16[24,16,128]{2,1,0:T(8,128)(2,1)S(1)}, u32[]{:S(2)}, u32[]{:S(2)}) collective-permute-start(bf16[24,16,128]{2,1,0:T(8,128)(2,1)S(1)} %get-tuple-element.15), channel_id=1, source_target_pairs={{0,8},{4,12},{8,0},{12,4},{1,9},{5,13},{9,1},{13,5},{2,10},{6,14},... | collective-permute-start | bytes 294920 | tf_op jit(solution)/shard_map/ppermute | solution.py:157
  22.8 0.0 collective-permute-start.4
  22.8 0.5 %collective-permute-done.2.rest_0_ = bf16[24,16,128]{2,1,0:T(8,128)(2,1)S(1)} collective-permute-done((bf16[24,16,128]{2,1,0:T(8,128)(2,1)S(1)}, bf16[24,16,128]{2,1,0:T(8,128)(2,1)S(1)}, u32[]{:S(2)}, u32[]{:S(2)}) %collective-permute-start.2) | collective-permute-done | bytes 98336 | tf_op jit(solution)/shard_map/ppermute | solution.py:157
  23.3 7.6 %collective-permute-done.3.rest_1_ = bf16[24,16,128]{2,1,0:T(8,128)(2,1)S(1)} collective-permute-done((bf16[24,16,128]{2,1,0:T(8,128)(2,1)S(1)}, bf16[24,16,128]{2,1,0:T(8,128)(2,1)S(1)}, u32[]{:S(2)}, u32[]{:S(2)}) %collective-permute-start.3) | collective-permute-done | bytes 98336 | tf_op jit(solution)/shard_map/ppermute | solution.py:157
  30.8 0.0 collective-permute-done.4.rest_2_
  30.9 0.8 %shard_map.49 = f32[16,24,128]{2,1,0:T(8,128)} custom-call(f32[24,16,128]{2,1,0:T(8,128)S(1)} %get-tuple-element.13.own, bf16[24,16,128]{2,1,0:T(8,128)(2,1)S(1)} %collective-permute-done.2.rest_0_, bf16[24,16,128]{2,1,0:T(8,128)(2,1)S(1)} %collective-permute-done.3.rest_1_, bf16[24,16,128]{2,1,0:T(8,128)(2,1)S(1)} %collective-permute-done.4.rest_2_), custom_call_target="tpu_custom_call" | custom-call | tf_op jit(solution)/shard_map/pallas_call | solution.py:160
Async XLA Ops:
  0.0 12.3 %collective-permute-start = (bf16[12,128,128]{2,1,0:T(8,128)(2,1)}, bf16[12,128,128]{2,1,0:T(8,128)(2,1)S(1)}, u32[]{:S(2)}, u32[]{:S(2)}) collective-permute-start(bf16[12,128,128]{2,1,0:T(8,128)(2,1)} %wave.1), channel_id=1, source_target_pairs={{2,0},{0,2},{3,1},{1,3},{6,4},{4,6},{7,5},{5,7},{10,8},{8,10},{11,... | collective-permute-start | bytes 1179656 | tf_op jit(solution)/shard_map/ppermute | solution.py:106
  3.0 1.2 %copy-start = (bf16[32,128,128]{2,1,0:T(8,128)(2,1)S(1)}, bf16[32,128,128]{2,1,0:T(8,128)(2,1)}, u32[]{:S(2)}) copy-start(bf16[32,128,128]{2,1,0:T(8,128)(2,1)} %left.3) | copy-start | bytes 3145732
  4.2 1.2 %copy-start.2 = (bf16[32,128,128]{2,1,0:T(8,128)(2,1)S(1)}, bf16[32,128,128]{2,1,0:T(8,128)(2,1)}, u32[]{:S(2)}) copy-start(bf16[32,128,128]{2,1,0:T(8,128)(2,1)} %right.3) | copy-start | bytes 3145732
  5.5 1.0 %copy-start.3 = (bf16[12,128,128]{2,1,0:T(8,128)(2,1)S(1)}, bf16[12,128,128]{2,1,0:T(8,128)(2,1)}, u32[]{:S(2)}) copy-start(bf16[12,128,128]{2,1,0:T(8,128)(2,1)} %wave.1) | copy-start | bytes 1179652
  6.5 0.7 %copy-start.4 = (s32[3,1,1,2,2,64]{5,4,3,2,1,0:T(2,128)S(1)}, s32[3,1,1,2,2,64]{5,4,3,2,1,0:T(2,128)}, u32[]{:S(2)}) copy-start(s32[3,1,1,2,2,64]{5,4,3,2,1,0:T(2,128)} %table.3) | copy-start | bytes 9220
  7.2 5.1 %copy-start.1 = (bf16[32,128,128]{2,1,0:T(8,128)(2,1)S(1)}, bf16[32,128,128]{2,1,0:T(8,128)(2,1)}, u32[]{:S(2)}) copy-start(bf16[32,128,128]{2,1,0:T(8,128)(2,1)} %left.3) | copy-start | bytes 3145732
  15.8 1.8 %collective-permute-start.1 = (bf16[4,24,16,128]{3,2,1,0:T(8,128)(2,1)S(1)}, bf16[4,24,16,128]{3,2,1,0:T(8,128)(2,1)S(1)}, u32[]{:S(2)}, u32[]{:S(2)}) collective-permute-start(bf16[4,24,16,128]{3,2,1,0:T(8,128)(2,1)S(1)} %get-tuple-element.12), channel_id=1, source_target_pairs={{0,1},{1,0},{2,3},{3,2},{4,5},{5,4},{6,7},{7,6},{8,9},{9,8},{10,11... | collective-permute-start | bytes 1179656 | tf_op jit(solution)/shard_map/ppermute | solution.py:146
  18.2 5.0 %collective-permute-start.2 = (bf16[24,16,128]{2,1,0:T(8,128)(2,1)S(1)}, bf16[24,16,128]{2,1,0:T(8,128)(2,1)S(1)}, u32[]{:S(2)}, u32[]{:S(2)}) collective-permute-start(bf16[24,16,128]{2,1,0:T(8,128)(2,1)S(1)} %get-tuple-element.14), channel_id=1, source_target_pairs={{0,4},{4,0},{8,12},{12,8},{1,5},{5,1},{9,13},{13,9},{2,6},{6,2},{1... | collective-permute-start | bytes 294920 | tf_op jit(solution)/shard_map/ppermute | solution.py:157
  20.2 10.7 %collective-permute-start.3 = (bf16[24,16,128]{2,1,0:T(8,128)(2,1)S(1)}, bf16[24,16,128]{2,1,0:T(8,128)(2,1)S(1)}, u32[]{:S(2)}, u32[]{:S(2)}) collective-permute-start(bf16[24,16,128]{2,1,0:T(8,128)(2,1)S(1)} %get-tuple-element.15), channel_id=1, source_target_pairs={{0,8},{4,12},{8,0},{12,4},{1,9},{5,13},{9,1},{13,5},{2,10},{6,14},... | collective-permute-start | bytes 294920 | tf_op jit(solution)/shard_map/ppermute | solution.py:157
  22.8 8.1 %collective-permute-start.4 = (bf16[24,16,128]{2,1,0:T(8,128)(2,1)S(1)}, bf16[24,16,128]{2,1,0:T(8,128)(2,1)S(1)}, u32[]{:S(2)}, u32[]{:S(2)}) collective-permute-start(bf16[24,16,128]{2,1,0:T(8,128)(2,1)S(1)} %get-tuple-element.16), channel_id=1, source_target_pairs={{0,12},{4,8},{8,4},{12,0},{1,13},{5,9},{9,5},{13,1},{2,14},{6,10},... | collective-permute-start | bytes 294920 | tf_op jit(solution)/shard_map/ppermute | solution.py:157

commit v2 on v1

--- a/solution.py
+++ b/solution.py
@@ -9,6 +9,7 @@
 
 VMEM = pl.BlockSpec(memory_space=pltpu.VMEM)
 SMEM = pl.BlockSpec(memory_space=pltpu.SMEM)
+ANY = pl.BlockSpec(memory_space=pl.ANY)
 LINK = jnp.bfloat16
 
 
@@ -61,25 +62,23 @@
     add_list(table, where[0], where[1], left, right, wave, acc, unroll_of(table.shape[-1]))
 
 
-def last_kernel(where, table, left, right, wave, start, keep, send, acc):
-    acc[...] = start[...]
-    rep = where[0]
+def last_kernel(where, table, left, right, wave, start, acc, keep_far, keep_near, send_far, send_near):
+    rep, op = where[0], where[2]
     add_list(table, rep, where[1], left, right, wave, acc, unroll_of(table.shape[-1]))
-    groups, tiles, rows, _ = keep.shape
-    reps = 2
-    for g in range(groups):
-        mine = pl.multiple_of((g * reps + rep) * rows, rows)
-        theirs = pl.multiple_of((g * reps + 1 - rep) * rows, rows)
-        keep[g] = acc[pl.ds(0, tiles), pl.ds(mine, rows), :]
-        send[g] = acc[pl.ds(0, tiles), pl.ds(theirs, rows), :].astype(LINK)
+    half, tiles, rows, _ = keep_far.shape
+    for keep, send, first in ((keep_far, send_far, half), (keep_near, send_near, 0)):
+        for g in range(half):
+            to = 2 * jnp.bitwise_xor(op, first + g)
+            mine = pl.multiple_of((to + rep) * rows, rows)
+            theirs = pl.multiple_of((to + 1 - rep) * rows, rows)
+            keep[g] = acc[pl.ds(0, tiles), pl.ds(mine, rows), :]
+            send[g] = acc[pl.ds(0, tiles), pl.ds(theirs, rows), :].astype(LINK)
 
 
-def pair_kernel(where, keep, got, own, *sends):
-    op = where[2]
-    own[...] = keep[op] + got[op].astype(jnp.float32)
-    for s, out in enumerate(sends):
-        to = jnp.bitwise_xor(op, s + 1)
-        out[...] = (keep[to] + got[to].astype(jnp.float32)).astype(LINK)
+def pair_kernel(skip, *refs):
+    keep, got = refs[skip : skip + 2]
+    for g, out in enumerate(refs[2 * skip + 2 :]):
+        out[...] = (keep[g] + got[g].astype(jnp.float32)).astype(out.dtype)
 
 
 def final_kernel(own, *rest):
@@ -117,7 +116,7 @@
         compiler_params=params(),
     )(wheres[0], slot_table, left_env, right_env, wavefunction)
 
-    fast = rep_count == 2 and rows % 16 == 0 and op_count & (op_count - 1) == 0
+    fast = rep_count == 2 and rows % 16 == 0 and op_count > 1 and op_count & (op_count - 1) == 0
     middle = others[:-1] if fast else others
     for s, wave in enumerate(middle):
         acc = pl.pallas_call(
@@ -131,32 +130,39 @@
         partial = jnp.swapaxes(acc[:tiles_blk], 0, 1)
         return lax.psum_scatter(partial, ("op", "rep"), scatter_dimension=0, tiled=True)
 
-    part = (op_count, tiles_blk, rows, width)
-    keep, send = pl.pallas_call(
+    half = op_count // 2
+    part = (half, tiles_blk, rows, width)
+    kept = jax.ShapeDtypeStruct(part, jnp.float32)
+    sent = jax.ShapeDtypeStruct(part, LINK)
+    _, keep_far, keep_near, send_far, send_near = pl.pallas_call(
         last_kernel,
-        out_shape=(
-            jax.ShapeDtypeStruct(part, jnp.float32),
-            jax.ShapeDtypeStruct(part, LINK),
-        ),
+        out_shape=(acc_shape, kept, kept, sent, sent),
         in_specs=[SMEM, SMEM, VMEM, VMEM, VMEM, VMEM],
-        out_specs=(VMEM, VMEM),
-        scratch_shapes=[pltpu.VMEM(acc_shape.shape, jnp.float32)],
+        out_specs=(VMEM,) * 5,
+        input_output_aliases={5: 0},
         compiler_params=params(),
     )(wheres[-1], slot_table, left_env, right_env, others[-1], acc)
-    got = lax.ppermute(send, "rep", [(0, 1), (1, 0)])
-    tile_rows = part[1:]
-    own, *sends = pl.pallas_call(
-        pair_kernel,
-        out_shape=(jax.ShapeDtypeStruct(tile_rows, jnp.float32),)
-        + (jax.ShapeDtypeStruct(tile_rows, LINK),) * (op_count - 1),
-        in_specs=[SMEM, VMEM, VMEM],
-        out_specs=(VMEM,) * op_count,
-        compiler_params=params(),
-    )(wheres[0], keep, got)
-    arrived = [
-        lax.ppermute(x, "op", [(i, i ^ (s + 1)) for i in range(op_count)])
-        for s, x in enumerate(sends)
-    ]
+
+    def pair_sum(keep, got, dtypes, later=()):
+        out = tuple(jax.ShapeDtypeStruct(part[1:], d) for d in dtypes)
+        return pl.pallas_call(
+            functools.partial(pair_kernel, len(later)),
+            out_shape=tuple(sent for _ in later) + out,
+            in_specs=[ANY] * len(later) + [VMEM, VMEM],
+            out_specs=(ANY,) * len(later) + (VMEM,) * half,
+            input_output_aliases={i: i for i in range(len(later))},
+            compiler_params=params(),
+        )(*later, keep, got)
+
+    def to_op(x, s):
+        return lax.ppermute(x, "op", [(i, i ^ s) for i in range(op_count)])
+
+    got_far = lax.ppermute(send_far, "rep", [(0, 1), (1, 0)])
+    send_near, *far = pair_sum(keep_far, got_far, (LINK,) * half, (send_near,))
+    arrived = [to_op(x, half + g) for g, x in enumerate(far)]
+    got_near = lax.ppermute(send_near, "rep", [(0, 1), (1, 0)])
+    own, *near = pair_sum(keep_near, got_near, (jnp.float32,) + (LINK,) * (half - 1))
+    arrived = [to_op(x, g + 1) for g, x in enumerate(near)] + arrived
     return pl.pallas_call(
         final_kernel,
         out_shape=jax.ShapeDtypeStruct((rows, tiles_blk, width), jnp.float32),

time: 31.9 us -> 30.4 us (0.953)
  waiting for transfers between devices: 11.4 us -> 10.4 us
  Pallas kernels: 8.43 us -> 7.77 us
    ppermute x4 -> x5, waiting for transfers between devices: 9.79 us -> 8.74 us  [the longest x3 7.31 us: to_op(): return lax.ppermute(x, 'op', [(i, i ^ s) for i in range(op_count)])]
    pallas_call x2 -> x3, Pallas kernels: 4.18 us -> 3.53 us  [the longest x1 3.44 us: shards(): pl.pallas_call(last_kernel, out_shape=(acc_shape, kept, kept, sent, sent)...]
    ppermute x4 -> x5, starting transfers between devices: 4.59 us -> 4.79 us  [the longest x3 4.51 us: to_op(): return lax.ppermute(x, 'op', [(i, i ^ s) for i in range(op_count)])]
  transfers between devices with their start and end apart: 5 -> 6, of which waited for: 4 -> 4; matrix products, arithmetic and copies ran while one was open for 0% -> 0% of each run, Pallas kernels for 11% -> 12%
where the time goes in v2:
time: 30.4 us; the launch traced here: 30.1 us
  waiting for transfers between devices  10.4 us (34%)
  Pallas kernels  7.77 us (26%)
  starting transfers between devices  7.72 us (25%)
  local copies, waits for them, and re-layouts  4.14 us (14%)
    ppermute x3, waiting for transfers between devices, to_op(): return lax.ppermute(x, 'op', [(i, i ^ s) for i in range(op_count)])  7.31 us
    ppermute x3, starting transfers between devices, to_op(): return lax.ppermute(x, 'op', [(i, i ^ s) for i in range(op_count)])  4.51 us
    unnamed x10, local copies, waits for them, and re-layouts  4.14 us
    pallas_call x1, Pallas kernels, shards(): pl.pallas_call(own_kernel, out_shape=acc_shape, in_specs=[SMEM, SMEM, VME...  3.44 us
    pallas_call x1, Pallas kernels, shards(): pl.pallas_call(last_kernel, out_shape=(acc_shape, kept, kept, sent, sent)...  3.44 us
    ppermute x1, starting transfers between devices, shards(): lax.ppermute(wavefunction, 'blk', [((i + s) % blk_count, i) for i in rang...  2.94 us
    ppermute x1, waiting for transfers between devices, shards(): lax.ppermute(wavefunction, 'blk', [((i + s) % blk_count, i) for i in rang...  1.66 us
    ppermute x1, waiting for transfers between devices, shards(): got_far = lax.ppermute(send_far, 'rep', [(0, 1), (1, 0)])  1.43 us
  transfers between devices with their start and end apart: 6, of which 4 were waited for; matrix products, arithmetic and copies ran while one was open for 0% of the time, Pallas kernels for 12%

profile of v2, /device:TPU:0, one launch (start us, length us, event | category | flops | bytes accessed | tf_op | source)
XLA Modules:
  0.0 30.1 jit_solution(11140794784033224247)
XLA Ops:
  0.0 2.9 %collective-permute-start = (bf16[12,128,128]{2,1,0:T(8,128)(2,1)}, bf16[12,128,128]{2,1,0:T(8,128)(2,1)S(1)}, u32[]{:S(2)}, u32[]{:S(2)}) collective-permute-start(bf16[12,128,128]{2,1,0:T(8,128)(2,1)} %wave.1), channel_id=1, source_target_pairs={{2,0},{0,2},{3,1},{1,3},{6,4},{4,6},{7,5},{5,7},{10,8},{8,10},{11,... | collective-permute-start | bytes 1179656 | tf_op jit(solution)/shard_map/ppermute | solution.py:105
  2.9 0.1 add_add_fusion
  3.0 0.0 copy-start
  3.0 1.2 %copy-done = bf16[32,128,128]{2,1,0:T(8,128)(2,1)S(1)} copy-done((bf16[32,128,128]{2,1,0:T(8,128)(2,1)S(1)}, bf16[32,128,128]{2,1,0:T(8,128)(2,1)}, u32[]{:S(2)}) %copy-start) | copy-done | bytes 1048600
  4.2 0.0 copy-start.2
  4.2 1.2 %copy-done.2 = bf16[32,128,128]{2,1,0:T(8,128)(2,1)S(1)} copy-done((bf16[32,128,128]{2,1,0:T(8,128)(2,1)S(1)}, bf16[32,128,128]{2,1,0:T(8,128)(2,1)}, u32[]{:S(2)}) %copy-start.2) | copy-done | bytes 1048600
  5.5 0.0 copy-start.3
  5.5 1.0 %copy-done.3 = bf16[12,128,128]{2,1,0:T(8,128)(2,1)S(1)} copy-done((bf16[12,128,128]{2,1,0:T(8,128)(2,1)S(1)}, bf16[12,128,128]{2,1,0:T(8,128)(2,1)}, u32[]{:S(2)}) %copy-start.3) | copy-done | bytes 393240
  6.5 0.0 copy-start.4
  6.5 0.7 %copy-done.4 = s32[3,1,1,2,2,64]{5,4,3,2,1,0:T(2,128)S(1)} copy-done((s32[3,1,1,2,2,64]{5,4,3,2,1,0:T(2,128)S(1)}, s32[3,1,1,2,2,64]{5,4,3,2,1,0:T(2,128)}, u32[]{:S(2)}) %copy-start.4) | copy-done | bytes 3096
  7.2 0.0 copy-start.1
  7.2 3.4 %shard_map.46.start = f32[25,128,128]{2,1,0:T(8,128)S(1)} custom-call(s32[3]{0:T(128)S(1)} %get-tuple-element.24.where, s32[3,1,1,2,2,64]{5,4,3,2,1,0:T(2,128)S(1)} %copy-done.4, bf16[32,128,128]{2,1,0:T(8,128)(2,1)S(1)} %copy-done, bf16[32,128,128]{2,1,0:T(8,128)(2,1)S(1)} %copy-done.2, bf16[12,128,128]{2,1,0:T(8,128)(2,1)S(1)} %copy-done.3), custom_call_target="tpu_custom_call" | custom-call | tf_op jit(solution)/shard_map/pallas_call | solution.py:111
  10.6 1.7 %collective-permute-done.wave = bf16[12,128,128]{2,1,0:T(8,128)(2,1)S(1)} collective-permute-done((bf16[12,128,128]{2,1,0:T(8,128)(2,1)}, bf16[12,128,128]{2,1,0:T(8,128)(2,1)S(1)}, u32[]{:S(2)}, u32[]{:S(2)}) %collective-permute-start) | collective-permute-done | bytes 393248 | tf_op jit(solution)/shard_map/ppermute | solution.py:105
  12.3 0.0 copy-done.1
  12.3 3.4 %shard_map.47 = (f32[25,128,128]{2,1,0:T(8,128)S(1)}, f32[2,24,16,128]{3,2,1,0:T(8,128)S(1)}, f32[2,24,16,128]{3,2,1,0:T(8,128)S(1)}, bf16[2,24,16,128]{3,2,1,0:T(8,128)(2,1)S(1)}, bf16[2,24,16,128]{3,2,1,0:T(8,128)(2,1)S(1)}) custom-call(s32[3]{0:T(128)S(1)} %get-tuple-element.23.where, ...), custom_call_target="tpu_custom_call", output_to_operand_aliasing={{0}: (5, {})} | custom-call | tf_op jit(solution)/shard_map/pallas_call | solution.py:137
  15.7 0.1 collective-permute-start.1
  15.8 1.4 %collective-permute-done.1.refs_2_ = bf16[2,24,16,128]{3,2,1,0:T(8,128)(2,1)S(1)} collective-permute-done((bf16[2,24,16,128]{3,2,1,0:T(8,128)(2,1)S(1)}, bf16[2,24,16,128]{3,2,1,0:T(8,128)(2,1)S(1)}, u32[]{:S(2)}, u32[]{:S(2)}) %collective-permute-start.1) | collective-permute-done | bytes 196640 | tf_op jit(solution)/shard_map/ppermute | solution.py:160
  17.3 0.2 collective-permute-start.2
  17.5 2.9 %collective-permute-start.4 = (bf16[24,16,128]{2,1,0:T(8,128)(2,1)S(1)}, bf16[24,16,128]{2,1,0:T(8,128)(2,1)S(1)}, u32[]{:S(2)}, u32[]{:S(2)}) collective-permute-start(bf16[24,16,128]{2,1,0:T(8,128)(2,1)S(1)} %get-tuple-element.21), channel_id=1, source_target_pairs={{0,8},{4,12},{8,0},{12,4},{1,9},{5,13},{9,1},{13,5},{2,10},{6,14},... | collective-permute-start | bytes 294920 | tf_op jit(solution)/shard_map/ppermute | solution.py:158
  20.3 1.3 %collective-permute-start.5 = (bf16[24,16,128]{2,1,0:T(8,128)(2,1)S(1)}, bf16[24,16,128]{2,1,0:T(8,128)(2,1)S(1)}, u32[]{:S(2)}, u32[]{:S(2)}) collective-permute-start(bf16[24,16,128]{2,1,0:T(8,128)(2,1)S(1)} %get-tuple-element.22), channel_id=1, source_target_pairs={{0,12},{4,8},{8,4},{12,0},{1,13},{5,9},{9,5},{13,1},{2,14},{6,10},... | collective-permute-start | bytes 294920 | tf_op jit(solution)/shard_map/ppermute | solution.py:158
  21.7 0.0 collective-permute-done.2.refs_1_
  21.7 0.3 collective-permute-start.3
  22.0 6.2 %collective-permute-done.4.rest_1_ = bf16[24,16,128]{2,1,0:T(8,128)(2,1)S(1)} collective-permute-done((bf16[24,16,128]{2,1,0:T(8,128)(2,1)S(1)}, bf16[24,16,128]{2,1,0:T(8,128)(2,1)S(1)}, u32[]{:S(2)}, u32[]{:S(2)}) %collective-permute-start.4) | collective-permute-done | bytes 98336 | tf_op jit(solution)/shard_map/ppermute | solution.py:158
  28.2 0.0 collective-permute-done.5.rest_2_
  28.2 1.1 %collective-permute-done.3.rest_0_ = bf16[24,16,128]{2,1,0:T(8,128)(2,1)S(1)} collective-permute-done((bf16[24,16,128]{2,1,0:T(8,128)(2,1)S(1)}, bf16[24,16,128]{2,1,0:T(8,128)(2,1)S(1)}, u32[]{:S(2)}, u32[]{:S(2)}) %collective-permute-start.3) | collective-permute-done | bytes 98336 | tf_op jit(solution)/shard_map/ppermute | solution.py:158
  29.3 0.8 %shard_map.50 = f32[16,24,128]{2,1,0:T(8,128)} custom-call(f32[24,16,128]{2,1,0:T(8,128)S(1)} %get-tuple-element.19.own, bf16[24,16,128]{2,1,0:T(8,128)(2,1)S(1)} %collective-permute-done.3.rest_0_, bf16[24,16,128]{2,1,0:T(8,128)(2,1)S(1)} %collective-permute-done.4.rest_1_, bf16[24,16,128]{2,1,0:T(8,128)(2,1)S(1)} %collective-permute-done.5.rest_2_), custom_call_target="tpu_custom_call" | custom-call | tf_op jit(solution)/shard_map/pallas_call | solution.py:166
  (2 shorter events, 0.1 us)
Async XLA Ops:
  0.0 12.3 %collective-permute-start = (bf16[12,128,128]{2,1,0:T(8,128)(2,1)}, bf16[12,128,128]{2,1,0:T(8,128)(2,1)S(1)}, u32[]{:S(2)}, u32[]{:S(2)}) collective-permute-start(bf16[12,128,128]{2,1,0:T(8,128)(2,1)} %wave.1), channel_id=1, source_target_pairs={{2,0},{0,2},{3,1},{1,3},{6,4},{4,6},{7,5},{5,7},{10,8},{8,10},{11,... | collective-permute-start | bytes 1179656 | tf_op jit(solution)/shard_map/ppermute | solution.py:105
  3.0 1.2 %copy-start = (bf16[32,128,128]{2,1,0:T(8,128)(2,1)S(1)}, bf16[32,128,128]{2,1,0:T(8,128)(2,1)}, u32[]{:S(2)}) copy-start(bf16[32,128,128]{2,1,0:T(8,128)(2,1)} %left.3) | copy-start | bytes 3145732
  4.2 1.2 %copy-start.2 = (bf16[32,128,128]{2,1,0:T(8,128)(2,1)S(1)}, bf16[32,128,128]{2,1,0:T(8,128)(2,1)}, u32[]{:S(2)}) copy-start(bf16[32,128,128]{2,1,0:T(8,128)(2,1)} %right.3) | copy-start | bytes 3145732
  5.5 1.0 %copy-start.3 = (bf16[12,128,128]{2,1,0:T(8,128)(2,1)S(1)}, bf16[12,128,128]{2,1,0:T(8,128)(2,1)}, u32[]{:S(2)}) copy-start(bf16[12,128,128]{2,1,0:T(8,128)(2,1)} %wave.1) | copy-start | bytes 1179652
  6.5 0.7 %copy-start.4 = (s32[3,1,1,2,2,64]{5,4,3,2,1,0:T(2,128)S(1)}, s32[3,1,1,2,2,64]{5,4,3,2,1,0:T(2,128)}, u32[]{:S(2)}) copy-start(s32[3,1,1,2,2,64]{5,4,3,2,1,0:T(2,128)} %table.3) | copy-start | bytes 9220
  7.2 5.1 %copy-start.1 = (bf16[32,128,128]{2,1,0:T(8,128)(2,1)S(1)}, bf16[32,128,128]{2,1,0:T(8,128)(2,1)}, u32[]{:S(2)}) copy-start(bf16[32,128,128]{2,1,0:T(8,128)(2,1)} %left.3) | copy-start | bytes 3145732
  15.7 1.5 %collective-permute-start.1 = (bf16[2,24,16,128]{3,2,1,0:T(8,128)(2,1)S(1)}, bf16[2,24,16,128]{3,2,1,0:T(8,128)(2,1)S(1)}, u32[]{:S(2)}, u32[]{:S(2)}) collective-permute-start(bf16[2,24,16,128]{3,2,1,0:T(8,128)(2,1)S(1)} %get-tuple-element.17), channel_id=1, source_target_pairs={{0,1},{1,0},{2,3},{3,2},{4,5},{5,4},{6,7},{7,6},{8,9},{9,8},{10,11... | collective-permute-start | bytes 589832 | tf_op jit(solution)/shard_map/ppermute | solution.py:160
  17.3 4.4 %collective-permute-start.2 = (bf16[2,24,16,128]{3,2,1,0:T(8,128)(2,1)S(1)}, bf16[2,24,16,128]{3,2,1,0:T(8,128)(2,1)S(1)}, u32[]{:S(2)}, u32[]{:S(2)}) collective-permute-start(bf16[2,24,16,128]{3,2,1,0:T(8,128)(2,1)S(1)} %get-tuple-element.18), channel_id=1, source_target_pairs={{0,1},{1,0},{2,3},{3,2},{4,5},{5,4},{6,7},{7,6},{8,9},{9,8},{10,11... | collective-permute-start | bytes 589832 | tf_op jit(solution)/shard_map/ppermute | solution.py:163
  17.5 10.8 %collective-permute-start.4 = (bf16[24,16,128]{2,1,0:T(8,128)(2,1)S(1)}, bf16[24,16,128]{2,1,0:T(8,128)(2,1)S(1)}, u32[]{:S(2)}, u32[]{:S(2)}) collective-permute-start(bf16[24,16,128]{2,1,0:T(8,128)(2,1)S(1)} %get-tuple-element.21), channel_id=1, source_target_pairs={{0,8},{4,12},{8,0},{12,4},{1,9},{5,13},{9,1},{13,5},{2,10},{6,14},... | collective-permute-start | bytes 294920 | tf_op jit(solution)/shard_map/ppermute | solution.py:158
  20.3 7.9 %collective-permute-start.5 = (bf16[24,16,128]{2,1,0:T(8,128)(2,1)S(1)}, bf16[24,16,128]{2,1,0:T(8,128)(2,1)S(1)}, u32[]{:S(2)}, u32[]{:S(2)}) collective-permute-start(bf16[24,16,128]{2,1,0:T(8,128)(2,1)S(1)} %get-tuple-element.22), channel_id=1, source_target_pairs={{0,12},{4,8},{8,4},{12,0},{1,13},{5,9},{9,5},{13,1},{2,14},{6,10},... | collective-permute-start | bytes 294920 | tf_op jit(solution)/shard_map/ppermute | solution.py:158
  21.7 7.6 %collective-permute-start.3 = (bf16[24,16,128]{2,1,0:T(8,128)(2,1)S(1)}, bf16[24,16,128]{2,1,0:T(8,128)(2,1)S(1)}, u32[]{:S(2)}, u32[]{:S(2)}) collective-permute-start(bf16[24,16,128]{2,1,0:T(8,128)(2,1)S(1)} %get-tuple-element.20), channel_id=1, source_target_pairs={{0,4},{4,0},{8,12},{12,8},{1,5},{5,1},{9,13},{13,9},{2,6},{6,2},{1... | collective-permute-start | bytes 294920 | tf_op jit(solution)/shard_map/ppermute | solution.py:158

commit v3 on v0

v3 whole, which is shorter than its diff:
```python
import functools

import jax
import jax.numpy as jnp
from jax import lax
from jax.experimental import pallas as pl
from jax.experimental.pallas import tpu as pltpu
from jax.sharding import PartitionSpec as P

VMEM = pl.BlockSpec(memory_space=pltpu.VMEM)
SMEM = pl.BlockSpec(memory_space=pltpu.SMEM)
ANY = pl.BlockSpec(memory_space=pl.ANY)
LINK = jnp.bfloat16


def params():
    return pltpu.CompilerParams(vmem_limit_bytes=24 << 20)


def in_hbm(x):
    return pltpu.with_memory_space_constraint(x, pltpu.HBM)


def unroll_of(caps, most):
    return next(u for u in (64, 32, 16, 8, 4, 2, 1) if u <= most and caps % u == 0)


def add_list(table, rep, src, left, right_t, wave, acc):
    caps = table.shape[-1]
    unroll = unroll_of(caps, 32)

    def body(step, carry):
        slots = [step * unroll + q for q in range(unroll)]
        terms = [table[0, 0, 0, rep, src, c] for c in slots]
        inner = [
            jnp.dot(
                left[terms[q]],
                wave[table[2, 0, 0, rep, src, slots[q]]],
                preferred_element_type=jnp.float32,
            ).astype(jnp.bfloat16)
            for q in range(unroll)
        ]
        outer = [
            jnp.dot(inner[q], right_t[terms[q]], preferred_element_type=jnp.float32)
            for q in range(unroll)
        ]
        for q in range(unroll):
            acc[table[1, 0, 0, rep, src, slots[q]]] += outer[q]
        return carry

    lax.fori_loop(0, caps // unroll, body, 0)


def prepare_kernel(
    order, left, right, wave, own, other,
    left_rows, right_t, wave_here, own_here, other_here, right_here, sems,
):
    rep, op = lax.axis_index("rep"), lax.axis_index("op")
    rows = left_rows.shape[1] // len(order)
    moves = [(right, right_here), (wave, wave_here), (own, own_here), (other, other_here)]
    for g, s in enumerate(order):
        first = pl.multiple_of((jnp.bitwise_xor(op, s) * 2 + rep) * rows, rows)
        moves.append((left.at[:, pl.ds(first, rows), :], left_rows.at[:, pl.ds(g * rows, rows), :]))
    copies = [pltpu.make_async_copy(a, b, sems.at[i]) for i, (a, b) in enumerate(moves)]
    for copy in copies:
        copy.start()
    for copy in copies:
        copy.wait()
    for k in range(right_t.shape[0]):
        right_t[k] = right_here[k].T


def add_both(table, left_rows, right_t, wave, wave_pair, acc):
    rep, blk = lax.axis_index("rep"), lax.axis_index("blk")
    acc[...] = jnp.zeros_like(acc)
    add_list(table, rep, blk, left_rows, right_t, wave, acc)
    add_list(table, 1 - rep, blk, left_rows, right_t, wave_pair, acc)


def split_rows(acc, outs):
    for g, out in enumerate(outs):
        tiles, rows, _ = out.shape
        out[...] = acc[0:tiles, g * rows : (g + 1) * rows, :].astype(out.dtype)


def other_kernel(table, left_rows, right_t, wave, wave_pair, acc, *outs):
    add_both(table, left_rows, right_t, wave, wave_pair, acc)
    split_rows(acc, outs)


def own_kernel(table, left_rows, right_t, wave, wave_pair, spare, acc, *outs):
    del spare
    add_both(table, left_rows, right_t, wave, wave_pair, acc)
    split_rows(acc, outs)


def sum_kernel(kept, got, out):
    out[...] = (kept[...] + got[...].astype(jnp.float32)).astype(out.dtype)


def final_kernel(own, *rest):
    got, out = rest[:-1], rest[-1]
    total = own[...]
    for g in got:
        total = total + g[...].astype(jnp.float32)
    for t in range(total.shape[0]):
        out[:, t, :] = total[t]


def call(kernel, out_shape, args, ins, outs, **kwargs):
    return pl.pallas_call(
        kernel, out_shape=out_shape, in_specs=ins, out_specs=outs, compiler_params=params(), **kwargs
    )(*args)


def at_source(wavefunction, left_env, right_env, slot_table):
    tiles_dev, width, _ = wavefunction.shape
    terms, row_total, _ = left_env.shape
    op_count = lax.axis_size("op")
    tiles = 2 * tiles_dev
    rows = row_total // (2 * op_count)
    half = op_count // 2
    order = list(range(half, op_count)) + list(range(half - 1, -1, -1))
    swap = [(0, 1), (1, 0)]
    f32, bf16 = jnp.float32, jnp.bfloat16
    shape = jax.ShapeDtypeStruct
    table_spec = pltpu.SMEM(slot_table.shape, slot_table.dtype)
    block = (tiles, rows, width)

    table_other = lax.ppermute(slot_table, "blk", swap)
    wave_pair = lax.ppermute(wavefunction, "rep", swap)
    left_rows, right_t, wave, own_table, other_table = call(
        functools.partial(prepare_kernel, order),
        (
            shape((terms, op_count * rows, width), left_env.dtype),
            shape(right_env.shape, right_env.dtype),
            shape(wavefunction.shape, wavefunction.dtype),
            table_spec,
            table_spec,
        ),
        [in_hbm(x) for x in (left_env, right_env, wavefunction, slot_table)] + [table_other],
        [ANY] * 5,
        (VMEM, VMEM, VMEM, SMEM, SMEM),
        scratch_shapes=[
            pltpu.VMEM(right_env.shape, right_env.dtype),
            pltpu.SemaphoreType.DMA((4 + op_count,)),
        ],
    )
    acc_shape = shape((tiles + 1, op_count * rows, width), f32)
    blocks = [block] * op_count
    acc, *sends = call(
        other_kernel,
        (acc_shape,) + tuple(shape(b, LINK) for b in blocks),
        (other_table, left_rows, right_t, wave, wave_pair),
        [SMEM] + [VMEM] * 4,
        (VMEM,) * (1 + op_count),
    )
    got = [lax.ppermute(x, "blk", swap) for x in sends]
    _, *kept = call(
        own_kernel,
        (acc_shape,) + tuple(shape(b, f32) for b in blocks),
        (own_table, left_rows, right_t, wave, wave_pair, acc),
        [SMEM] + [VMEM] * 5,
        (VMEM,) * (1 + op_count),
        input_output_aliases={5: 0},
    )

    def to_op(x, s):
        return lax.ppermute(x, "op", [(i, i ^ s) for i in range(op_count)])

    arrived = []
    for g in range(op_count - 1):
        total = call(sum_kernel, shape(block, LINK), (kept[g], got[g]), [VMEM] * 2, VMEM)
        arrived.append(to_op(total, order[g]))
    return call(
        final_kernel,
        shape((rows, tiles, width), f32),
        (kept[-1], got[-1], *arrived),
        [VMEM] * (op_count + 1),
        VMEM,
    )


def list_kernel(where, table, left, right, wave, start, acc):
    acc[...] = start[...]
    add_list(table, where[0], where[1], left, right, wave, acc)


def gathered(wavefunction, left_env, right_env, slot_table):
    tiles_dev, width, _ = wavefunction.shape
    blk_count = lax.axis_size("blk")
    tiles_blk = tiles_dev * lax.axis_size("rep")
    rep, blk = lax.axis_index("rep"), lax.axis_index("blk")
    right_t = jnp.swapaxes(right_env, 1, 2)
    acc = jnp.zeros((tiles_blk + 1, left_env.shape[1], width), jnp.float32)
    for s in range(blk_count):
        pairs = [((i + s) % blk_count, i) for i in range(blk_count)]
        acc = call(
            list_kernel,
            jax.ShapeDtypeStruct(acc.shape, acc.dtype),
            (
                jnp.stack([rep, (blk + s) % blk_count]).astype(jnp.int32),
                slot_table,
                left_env,
                right_t,
                lax.ppermute(wavefunction, "blk", pairs) if s else wavefunction,
                acc,
            ),
            [SMEM] * 2 + [VMEM] * 4,
            VMEM,
        )
    partial = jnp.swapaxes(acc[:tiles_blk], 0, 1)
    return lax.psum_scatter(partial, ("op", "rep"), scatter_dimension=0, tiled=True)


def shards(wavefunction, left_env, right_env, slot_table):
    op_count = lax.axis_size("op")
    rows = left_env.shape[1] // (2 * op_count)
    fits = lax.axis_size("rep") == 2 and lax.axis_size("blk") == 2
    fits = fits and op_count > 1 and op_count & (op_count - 1) == 0
    fits = fits and rows % 16 == 0 and rows * 2 * op_count == left_env.shape[1]
    form = at_source if fits else gathered
    return form(wavefunction, left_env, right_env, slot_table)


def solution(mesh):
    placed = (
        P(("grp", "blk", "rep"), None, None),
        P(("grp", "op"), None, None),
        P(("grp", "op"), None, None),
        P(None, "op", "blk", None, None, None),
    )
    return jax.shard_map(
        shards,
        mesh=mesh,
        in_specs=placed,
        out_specs=P(("op", "rep"), ("grp", "blk"), None),
        check_vma=False,
    )
```

time: 107 us -> 28.3 us (0.26)
  waiting for transfers between devices: 36 us -> 7.6 us
  matrix products: 27.3 us -> 0 us
  local copies, waits for them, and re-layouts: 16.1 us -> 0 us
  between operations: 13.4 us -> 0.08 us
  blocking collectives: 13 us -> 0 us
  starting transfers between devices: 0.01 us -> 12 us
  Pallas kernels: 0 us -> 8.54 us
    reduce_scatter x1 -> x0, waiting for transfers between devices: 35.9 us -> none  [shards(): lax.psum_scatter(partial_sum, ('op', 'rep'), scatter_dimension=0, tiled=T...]
    dot_general x4 -> x0, matrix products: 27.3 us -> none  [the longest x2 14.7 us: one_group(): jnp.einsum('tc,cij->itj', onehot, outer_prod, precision=lax.Precision.HIG...]
    gather x6 -> x0, local copies, waits for them, and re-layouts: 15.4 us -> none  [the longest x2 6.7 us: one_group(): right_env[terms_now]]
    all_gather x1 -> x0, blocking collectives: 13 us -> none  [shards(): gathered = lax.all_gather(wavefunction, 'blk', axis=0, tiled=True)]
    ppermute x0 -> x9, starting transfers between devices: none -> 12 us  [the longest x3 4.86 us: to_op(): return lax.ppermute(x, 'op', [(i, i ^ s) for i in range(op_count)])]
    pallas_call x0 -> x7, Pallas kernels: none -> 8.54 us  [call(): pl.pallas_call(kernel, out_shape=out_shape, in_specs=ins, out_specs=outs,...]
    ppermute x0 -> x9, waiting for transfers between devices: none -> 7.6 us  [the longest x3 5.77 us: to_op(): return lax.ppermute(x, 'op', [(i, i ^ s) for i in range(op_count)])]
  transfers between devices with their start and end apart: 1 -> 9, of which waited for: 1 -> 4; matrix products, arithmetic and copies ran while one was open for 0% -> 0% of each run, Pallas kernels for 0% -> 17%
where the time goes in v3:
time: 28.3 us; the launch traced here: 28.2 us
  starting transfers between devices  12 us (42%)
  Pallas kernels  8.54 us (30%)
  waiting for transfers between devices  7.6 us (27%)
    pallas_call x7, Pallas kernels, call(): pl.pallas_call(kernel, out_shape=out_shape, in_specs=ins, out_specs=outs,...  8.54 us
    ppermute x3, waiting for transfers between devices, to_op(): return lax.ppermute(x, 'op', [(i, i ^ s) for i in range(op_count)])  5.77 us
    ppermute x3, starting transfers between devices, to_op(): return lax.ppermute(x, 'op', [(i, i ^ s) for i in range(op_count)])  4.86 us
    ppermute x4, starting transfers between devices, at_source(): got = [lax.ppermute(x, 'blk', swap) for x in sends]  4.19 us
    ppermute x1, starting transfers between devices, at_source(): table_other = lax.ppermute(slot_table, 'blk', swap)  2.49 us
    ppermute x1, waiting for transfers between devices, at_source(): table_other = lax.ppermute(slot_table, 'blk', swap)  1.82 us
  transfers between devices with their start and end apart: 9, of which 4 were waited for; matrix products, arithmetic and copies ran while one was open for 0% of the time, Pallas kernels for 17%

profile of v3, /device:TPU:0, one launch (start us, length us, event | category | flops | bytes accessed | tf_op | source)
XLA Modules:
  0.0 28.2 jit_solution(13194694806132133103)
XLA Ops:
  0.0 0.5 %collective-permute-start.1 = (bf16[12,128,128]{2,1,0:T(8,128)(2,1)}, bf16[12,128,128]{2,1,0:T(8,128)(2,1)S(1)}, u32[]{:S(2)}, u32[]{:S(2)}) collective-permute-start(bf16[12,128,128]{2,1,0:T(8,128)(2,1)} %wave.1), channel_id=1, source_target_pairs={{0,1},{1,0},{2,3},{3,2},{4,5},{5,4},{6,7},{7,6},{8,9},{9,8},{10,11... | collective-permute-start | bytes 1179656 | tf_op jit(solution)/shard_map/ppermute | solution.py:131
  0.5 2.5 %collective-permute-start = (s32[3,1,1,2,2,64]{5,4,3,2,1,0:T(2,128)}, s32[3,1,1,2,2,64]{5,4,3,2,1,0:T(2,128)S(1)}, u32[]{:S(2)}, u32[]{:S(2)}) collective-permute-start(s32[3,1,1,2,2,64]{5,4,3,2,1,0:T(2,128)} %own.1), channel_id=1, source_target_pairs={{0,2},{2,0},{1,3},{3,1},{4,6},{6,4},{5,7},{7,5},{8,10},{10,8},{9,1... | collective-permute-start | bytes 9224 | tf_op jit(solution)/shard_map/ppermute | solution.py:130
  2.9 1.8 %collective-permute-done.other = s32[3,1,1,2,2,64]{5,4,3,2,1,0:T(2,128)S(1)} collective-permute-done((s32[3,1,1,2,2,64]{5,4,3,2,1,0:T(2,128)}, s32[3,1,1,2,2,64]{5,4,3,2,1,0:T(2,128)S(1)}, u32[]{:S(2)}, u32[]{:S(2)}) %collective-permute-start) | collective-permute-done | bytes 3104 | tf_op jit(solution)/shard_map/ppermute | solution.py:130
  4.8 1.9 %shard_map.46 = (bf16[32,64,128]{2,1,0:T(8,128)(2,1)S(1)}, bf16[32,128,128]{2,1,0:T(8,128)(2,1)S(1)}, bf16[12,128,128]{2,1,0:T(8,128)(2,1)S(1)}, s32[3,1,1,2,2,6...) custom-call(bf16[32,128,128]{2,1,0:T(8,128)(2,1)} %left.1, bf16[32,128,128]{2,1,0:T(8,128)(2,1)} %right.1, ...), custom_call_target="tpu_custom_call" | custom-call | tf_op jit(solution)/shard_map/pallas_call | solution.py:111
  6.6 0.0 collective-permute-done.1.wave_pair
  6.6 2.9 %shard_map.47 = (f32[25,64,128]{2,1,0:T(8,128)S(1)}, bf16[24,16,128]{2,1,0:T(8,128)(2,1)S(1)}, bf16[24,16,128]{2,1,0:T(8,128)(2,1)S(1)}, bf16[24,16,128]{2,1,0:T(8,128)(2,1)S(1)}, bf16[24,16,128]{2,1,0:T(8,128)(2,1)S(1)}) custom-call(s32[3,1,1,2,2,64]{5,4,3,2,1,0:T(2,128)S(4)} %get-tuple-element.23.table, ...), custom_call_target="tpu_custom_call" | custom-call | tf_op jit(solution)/shard_map/pallas_call | solution.py:111
  9.5 2.1 %collective-permute-start.3 = (bf16[24,16,128]{2,1,0:T(8,128)(2,1)S(1)}, bf16[24,16,128]{2,1,0:T(8,128)(2,1)S(1)}, u32[]{:S(2)}, u32[]{:S(2)}) collective-permute-start(bf16[24,16,128]{2,1,0:T(8,128)(2,1)S(1)} %get-tuple-element.28), channel_id=1, source_target_pairs={{0,2},{2,0},{1,3},{3,1},{4,6},{6,4},{5,7},{7,5},{8,10},{10,8},{9,1... | collective-permute-start | bytes 294920 | tf_op jit(solution)/shard_map/ppermute | solution.py:158
  11.6 0.1 collective-permute-start.5
  11.7 1.9 %collective-permute-start.7 = (bf16[24,16,128]{2,1,0:T(8,128)(2,1)S(1)}, bf16[24,16,128]{2,1,0:T(8,128)(2,1)S(1)}, u32[]{:S(2)}, u32[]{:S(2)}) collective-permute-start(bf16[24,16,128]{2,1,0:T(8,128)(2,1)S(1)} %get-tuple-element.32), channel_id=1, source_target_pairs={{0,2},{2,0},{1,3},{3,1},{4,6},{6,4},{5,7},{7,5},{8,10},{10,8},{9,1... | collective-permute-start | bytes 294920 | tf_op jit(solution)/shard_map/ppermute | solution.py:158
  13.7 0.1 collective-permute-start.2
  13.7 2.9 %shard_map.48 = (f32[25,64,128]{2,1,0:T(8,128)S(1)}, f32[24,16,128]{2,1,0:T(8,128)S(1)}, f32[24,16,128]{2,1,0:T(8,128)S(1)}, f32[24,16,128]{2,1,0:T(8,128)S(1)}, f32[24,16,128]{2,1,0:T(8,128)S(1)}) custom-call(s32[3,1,1,2,2,64]{5,4,3,2,1,0:T(2,128)S(4)} %get-tuple-element.19.table, ...), custom_call_target="tpu_custom_call", output_to_operand_aliasing={{0}: (5, {})} | custom-call | tf_op jit(solution)/shard_map/pallas_call | solution.py:111
  16.6 0.0 collective-permute-done.3.got
  16.7 3.1 %collective-permute-start.4 = (bf16[24,16,128]{2,1,0:T(8,128)(2,1)S(1)}, bf16[24,16,128]{2,1,0:T(8,128)(2,1)S(1)}, u32[]{:S(2)}, u32[]{:S(2)}) collective-permute-start(bf16[24,16,128]{2,1,0:T(8,128)(2,1)S(1)} %shard_map.49), channel_id=1, source_target_pairs={{0,8},{4,12},{8,0},{12,4},{1,9},{5,13},{9,1},{13,5},{2,10},{6,14},... | collective-permute-start | bytes 294920 | tf_op jit(solution)/shard_map/ppermute | solution.py:169
  19.8 0.0 collective-permute-done.5.got
  19.8 1.7 %collective-permute-start.6 = (bf16[24,16,128]{2,1,0:T(8,128)(2,1)S(1)}, bf16[24,16,128]{2,1,0:T(8,128)(2,1)S(1)}, u32[]{:S(2)}, u32[]{:S(2)}) collective-permute-start(bf16[24,16,128]{2,1,0:T(8,128)(2,1)S(1)} %shard_map.50), channel_id=1, source_target_pairs={{0,12},{4,8},{8,4},{12,0},{1,13},{5,9},{9,5},{13,1},{2,14},{6,10},... | collective-permute-start | bytes 294920 | tf_op jit(solution)/shard_map/ppermute | solution.py:169
  21.5 0.0 collective-permute-done.7.got
  21.5 0.1 collective-permute-start.8
  21.6 0.0 collective-permute-done.2.rest_0_
  21.6 3.9 %collective-permute-done.4.rest_1_ = bf16[24,16,128]{2,1,0:T(8,128)(2,1)S(1)} collective-permute-done((bf16[24,16,128]{2,1,0:T(8,128)(2,1)S(1)}, bf16[24,16,128]{2,1,0:T(8,128)(2,1)S(1)}, u32[]{:S(2)}, u32[]{:S(2)}) %collective-permute-start.4) | collective-permute-done | bytes 98336 | tf_op jit(solution)/shard_map/ppermute | solution.py:169
  25.5 1.1 %collective-permute-done.6.rest_2_ = bf16[24,16,128]{2,1,0:T(8,128)(2,1)S(1)} collective-permute-done((bf16[24,16,128]{2,1,0:T(8,128)(2,1)S(1)}, bf16[24,16,128]{2,1,0:T(8,128)(2,1)S(1)}, u32[]{:S(2)}, u32[]{:S(2)}) %collective-permute-start.6) | collective-permute-done | bytes 98336 | tf_op jit(solution)/shard_map/ppermute | solution.py:169
  26.6 0.8 %collective-permute-done.8.rest_3_ = bf16[24,16,128]{2,1,0:T(8,128)(2,1)S(1)} collective-permute-done((bf16[24,16,128]{2,1,0:T(8,128)(2,1)S(1)}, bf16[24,16,128]{2,1,0:T(8,128)(2,1)S(1)}, u32[]{:S(2)}, u32[]{:S(2)}) %collective-permute-start.8) | collective-permute-done | bytes 98336 | tf_op jit(solution)/shard_map/ppermute | solution.py:169
  27.4 0.8 %shard_map.52 = f32[16,24,128]{2,1,0:T(8,128)} custom-call(f32[24,16,128]{2,1,0:T(8,128)S(1)} %get-tuple-element.25.own, bf16[24,16,128]{2,1,0:T(8,128)(2,1)S(1)} %collective-permute-done.2.rest_0_, bf16[24,16,128]{2,1,0:T(8,128)(2,1)S(1)} %collective-permute-done.4.rest_1_, bf16[24,16,128]{2,1,0:T(8,128)(2,1)S(1)} %collective-permute-done.6.rest_2_, ...), custom_call_target="tpu_custom_call" | custom-call | tf_op jit(solution)/shard_map/pallas_call | solution.py:111
  (3 shorter events, 0.1 us)
Async XLA Ops:
  0.0 6.6 %collective-permute-start.1 = (bf16[12,128,128]{2,1,0:T(8,128)(2,1)}, bf16[12,128,128]{2,1,0:T(8,128)(2,1)S(1)}, u32[]{:S(2)}, u32[]{:S(2)}) collective-permute-start(bf16[12,128,128]{2,1,0:T(8,128)(2,1)} %wave.1), channel_id=1, source_target_pairs={{0,1},{1,0},{2,3},{3,2},{4,5},{5,4},{6,7},{7,6},{8,9},{9,8},{10,11... | collective-permute-start | bytes 1179656 | tf_op jit(solution)/shard_map/ppermute | solution.py:131
  0.5 4.3 %collective-permute-start = (s32[3,1,1,2,2,64]{5,4,3,2,1,0:T(2,128)}, s32[3,1,1,2,2,64]{5,4,3,2,1,0:T(2,128)S(1)}, u32[]{:S(2)}, u32[]{:S(2)}) collective-permute-start(s32[3,1,1,2,2,64]{5,4,3,2,1,0:T(2,128)} %own.1), channel_id=1, source_target_pairs={{0,2},{2,0},{1,3},{3,1},{4,6},{6,4},{5,7},{7,5},{8,10},{10,8},{9,1... | collective-permute-start | bytes 9224 | tf_op jit(solution)/shard_map/ppermute | solution.py:130
  9.5 7.1 %collective-permute-start.3 = (bf16[24,16,128]{2,1,0:T(8,128)(2,1)S(1)}, bf16[24,16,128]{2,1,0:T(8,128)(2,1)S(1)}, u32[]{:S(2)}, u32[]{:S(2)}) collective-permute-start(bf16[24,16,128]{2,1,0:T(8,128)(2,1)S(1)} %get-tuple-element.28), channel_id=1, source_target_pairs={{0,2},{2,0},{1,3},{3,1},{4,6},{6,4},{5,7},{7,5},{8,10},{10,8},{9,1... | collective-permute-start | bytes 294920 | tf_op jit(solution)/shard_map/ppermute | solution.py:158
  11.6 8.1 %collective-permute-start.5 = (bf16[24,16,128]{2,1,0:T(8,128)(2,1)S(1)}, bf16[24,16,128]{2,1,0:T(8,128)(2,1)S(1)}, u32[]{:S(2)}, u32[]{:S(2)}) collective-permute-start(bf16[24,16,128]{2,1,0:T(8,128)(2,1)S(1)} %get-tuple-element.30), channel_id=1, source_target_pairs={{0,2},{2,0},{1,3},{3,1},{4,6},{6,4},{5,7},{7,5},{8,10},{10,8},{9,1... | collective-permute-start | bytes 294920 | tf_op jit(solution)/shard_map/ppermute | solution.py:158
  11.7 9.8 %collective-permute-start.7 = (bf16[24,16,128]{2,1,0:T(8,128)(2,1)S(1)}, bf16[24,16,128]{2,1,0:T(8,128)(2,1)S(1)}, u32[]{:S(2)}, u32[]{:S(2)}) collective-permute-start(bf16[24,16,128]{2,1,0:T(8,128)(2,1)S(1)} %get-tuple-element.32), channel_id=1, source_target_pairs={{0,2},{2,0},{1,3},{3,1},{4,6},{6,4},{5,7},{7,5},{8,10},{10,8},{9,1... | collective-permute-start | bytes 294920 | tf_op jit(solution)/shard_map/ppermute | solution.py:158
  13.7 8.0 %collective-permute-start.2 = (bf16[24,16,128]{2,1,0:T(8,128)(2,1)S(1)}, bf16[24,16,128]{2,1,0:T(8,128)(2,1)S(1)}, u32[]{:S(2)}, u32[]{:S(2)}) collective-permute-start(bf16[24,16,128]{2,1,0:T(8,128)(2,1)S(1)} %get-tuple-element.26), channel_id=1, source_target_pairs={{0,2},{2,0},{1,3},{3,1},{4,6},{6,4},{5,7},{7,5},{8,10},{10,8},{9,1... | collective-permute-start | bytes 294920 | tf_op jit(solution)/shard_map/ppermute | solution.py:158
  16.7 8.8 %collective-permute-start.4 = (bf16[24,16,128]{2,1,0:T(8,128)(2,1)S(1)}, bf16[24,16,128]{2,1,0:T(8,128)(2,1)S(1)}, u32[]{:S(2)}, u32[]{:S(2)}) collective-permute-start(bf16[24,16,128]{2,1,0:T(8,128)(2,1)S(1)} %shard_map.49), channel_id=1, source_target_pairs={{0,8},{4,12},{8,0},{12,4},{1,9},{5,13},{9,1},{13,5},{2,10},{6,14},... | collective-permute-start | bytes 294920 | tf_op jit(solution)/shard_map/ppermute | solution.py:169
  19.8 6.8 %collective-permute-start.6 = (bf16[24,16,128]{2,1,0:T(8,128)(2,1)S(1)}, bf16[24,16,128]{2,1,0:T(8,128)(2,1)S(1)}, u32[]{:S(2)}, u32[]{:S(2)}) collective-permute-start(bf16[24,16,128]{2,1,0:T(8,128)(2,1)S(1)} %shard_map.50), channel_id=1, source_target_pairs={{0,12},{4,8},{8,4},{12,0},{1,13},{5,9},{9,5},{13,1},{2,14},{6,10},... | collective-permute-start | bytes 294920 | tf_op jit(solution)/shard_map/ppermute | solution.py:169
  21.5 5.9 %collective-permute-start.8 = (bf16[24,16,128]{2,1,0:T(8,128)(2,1)S(1)}, bf16[24,16,128]{2,1,0:T(8,128)(2,1)S(1)}, u32[]{:S(2)}, u32[]{:S(2)}) collective-permute-start(bf16[24,16,128]{2,1,0:T(8,128)(2,1)S(1)} %shard_map.51), channel_id=1, source_target_pairs={{0,4},{4,0},{8,12},{12,8},{1,5},{5,1},{9,13},{13,9},{2,6},{6,2},{1... | collective-permute-start | bytes 294920 | tf_op jit(solution)/shard_map/ppermute | solution.py:169

commit v4 on v3

--- a/solution.py
+++ b/solution.py
@@ -51,46 +51,50 @@
     lax.fori_loop(0, caps // unroll, body, 0)
 
 
-def prepare_kernel(
-    order, left, right, wave, own, other,
-    left_rows, right_t, wave_here, own_here, other_here, right_here, sems,
+def first_kernel(
+    order, left, right, wave, table,
+    left_rows, right_t, wave_here, table_here, acc, right_here, sems,
 ):
-    rep, op = lax.axis_index("rep"), lax.axis_index("op")
+    rep, op, blk = lax.axis_index("rep"), lax.axis_index("op"), lax.axis_index("blk")
     rows = left_rows.shape[1] // len(order)
-    moves = [(right, right_here), (wave, wave_here), (own, own_here), (other, other_here)]
+    moves = [(right, right_here), (wave, wave_here), (table, table_here)]
     for g, s in enumerate(order):
         first = pl.multiple_of((jnp.bitwise_xor(op, s) * 2 + rep) * rows, rows)
         moves.append((left.at[:, pl.ds(first, rows), :], left_rows.at[:, pl.ds(g * rows, rows), :]))
     copies = [pltpu.make_async_copy(a, b, sems.at[i]) for i, (a, b) in enumerate(moves)]
     for copy in copies:
         copy.start()
+    acc[...] = jnp.zeros_like(acc)
     for copy in copies:
         copy.wait()
     for k in range(right_t.shape[0]):
         right_t[k] = right_here[k].T
-
-
-def add_both(table, left_rows, right_t, wave, wave_pair, acc):
+    add_list(table_here, rep, blk, left_rows, right_t, wave_here, acc)
+
+
+def split_rows(acc, outs):
+    for g, out in enumerate(outs):
+        tiles, rows, _ = out.shape
+        out[...] = acc[0:tiles, g * rows : (g + 1) * rows, :].astype(out.dtype)
+
+
+def own_kernel(table, left_rows, right_t, wave_pair, start, table_other, acc, other_here, *outs):
+    del start
+    *outs, sem = outs
+    rep, blk = lax.axis_index("rep"), lax.axis_index("blk")
+    copy = pltpu.make_async_copy(table_other, other_here, sem)
+    copy.start()
+    add_list(table, 1 - rep, blk, left_rows, right_t, wave_pair, acc)
+    split_rows(acc, outs)
+    copy.wait()
+
+
+def other_kernel(table, left_rows, right_t, wave, wave_pair, spare, acc, *outs):
+    del spare
     rep, blk = lax.axis_index("rep"), lax.axis_index("blk")
     acc[...] = jnp.zeros_like(acc)
     add_list(table, rep, blk, left_rows, right_t, wave, acc)
     add_list(table, 1 - rep, blk, left_rows, right_t, wave_pair, acc)
-
-
-def split_rows(acc, outs):
-    for g, out in enumerate(outs):
-        tiles, rows, _ = out.shape
-        out[...] = acc[0:tiles, g * rows : (g + 1) * rows, :].astype(out.dtype)
-
-
-def other_kernel(table, left_rows, right_t, wave, wave_pair, acc, *outs):
-    add_both(table, left_rows, right_t, wave, wave_pair, acc)
-    split_rows(acc, outs)
-
-
-def own_kernel(table, left_rows, right_t, wave, wave_pair, spare, acc, *outs):
-    del spare
-    add_both(table, left_rows, right_t, wave, wave_pair, acc)
     split_rows(acc, outs)
 
 
@@ -122,48 +126,49 @@
     half = op_count // 2
     order = list(range(half, op_count)) + list(range(half - 1, -1, -1))
     swap = [(0, 1), (1, 0)]
-    f32, bf16 = jnp.float32, jnp.bfloat16
+    f32 = jnp.float32
     shape = jax.ShapeDtypeStruct
     table_spec = pltpu.SMEM(slot_table.shape, slot_table.dtype)
     block = (tiles, rows, width)
 
     table_other = lax.ppermute(slot_table, "blk", swap)
     wave_pair = lax.ppermute(wavefunction, "rep", swap)
-    left_rows, right_t, wave, own_table, other_table = call(
-        functools.partial(prepare_kernel, order),
+    acc_shape = shape((tiles + 1, op_count * rows, width), f32)
+    left_rows, right_t, wave, own_table, acc = call(
+        functools.partial(first_kernel, order),
         (
             shape((terms, op_count * rows, width), left_env.dtype),
             shape(right_env.shape, right_env.dtype),
             shape(wavefunction.shape, wavefunction.dtype),
             table_spec,
-            table_spec,
+            acc_shape,
         ),
-        [in_hbm(x) for x in (left_env, right_env, wavefunction, slot_table)] + [table_other],
-        [ANY] * 5,
-        (VMEM, VMEM, VMEM, SMEM, SMEM),
+        [in_hbm(x) for x in (left_env, right_env, wavefunction, slot_table)],
+        [ANY] * 4,
+        (VMEM, VMEM, VMEM, SMEM, VMEM),
         scratch_shapes=[
             pltpu.VMEM(right_env.shape, right_env.dtype),
-            pltpu.SemaphoreType.DMA((4 + op_count,)),
+            pltpu.SemaphoreType.DMA((3 + op_count,)),
         ],
     )
-    acc_shape = shape((tiles + 1, op_count * rows, width), f32)
-    blocks = [block] * op_count
-    acc, *sends = call(
+    acc, other_table, *kept = call(
+        own_kernel,
+        (acc_shape, table_spec) + (shape(block, f32),) * op_count,
+        (own_table, left_rows, right_t, wave_pair, acc, table_other),
+        [SMEM] + [VMEM] * 4 + [ANY],
+        (VMEM, SMEM) + (VMEM,) * op_count,
+        input_output_aliases={4: 0},
+        scratch_shapes=[pltpu.SemaphoreType.DMA],
+    )
+    _, *sends = call(
         other_kernel,
-        (acc_shape,) + tuple(shape(b, LINK) for b in blocks),
-        (other_table, left_rows, right_t, wave, wave_pair),
-        [SMEM] + [VMEM] * 4,
-        (VMEM,) * (1 + op_count),
-    )
-    got = [lax.ppermute(x, "blk", swap) for x in sends]
-    _, *kept = call(
-        own_kernel,
-        (acc_shape,) + tuple(shape(b, f32) for b in blocks),
-        (own_table, left_rows, right_t, wave, wave_pair, acc),
+        (acc_shape,) + (shape(block, LINK),) * op_count,
+        (other_table, left_rows, right_t, wave, wave_pair, acc),
         [SMEM] + [VMEM] * 5,
         (VMEM,) * (1 + op_count),
         input_output_aliases={5: 0},
     )
+    got = [lax.ppermute(x, "blk", swap) for x in sends]
 
     def to_op(x, s):
         return lax.ppermute(x, "op", [(i, i ^ s) for i in range(op_count)])

time: 28.3 us -> 28.3 us (level)
  waiting for transfers between devices: 7.6 us -> 6.61 us
  starting transfers between devices: 12 us -> 12.8 us
    ppermute x1, waiting for transfers between devices: 1.82 us -> 0.01 us  [at_source(): table_other = lax.ppermute(slot_table, 'blk', swap)]
    ppermute x4, waiting for transfers between devices: 0.01 us -> 1.59 us  [at_source(): got = [lax.ppermute(x, 'blk', swap) for x in sends]]
    ppermute x3, starting transfers between devices: 4.86 us -> 5.76 us  [to_op(): return lax.ppermute(x, 'op', [(i, i ^ s) for i in range(op_count)])]
    ppermute x3, waiting for transfers between devices: 5.77 us -> 5.02 us  [to_op(): return lax.ppermute(x, 'op', [(i, i ^ s) for i in range(op_count)])]
  transfers between devices with their start and end apart: 9 -> 9, of which waited for: 4 -> 4; matrix products, arithmetic and copies ran while one was open for 0% -> 0% of each run, Pallas kernels for 17% -> 12%
where the time goes in v4:
time: 28.3 us; the launch traced here: 28.2 us
  starting transfers between devices  12.8 us (45%)
  Pallas kernels  8.66 us (31%)
  waiting for transfers between devices  6.61 us (23%)
    pallas_call x7, Pallas kernels, call(): pl.pallas_call(kernel, out_shape=out_shape, in_specs=ins, out_specs=outs,...  8.66 us
    ppermute x3, starting transfers between devices, to_op(): return lax.ppermute(x, 'op', [(i, i ^ s) for i in range(op_count)])  5.76 us
    ppermute x3, waiting for transfers between devices, to_op(): return lax.ppermute(x, 'op', [(i, i ^ s) for i in range(op_count)])  5.02 us
    ppermute x4, starting transfers between devices, at_source(): got = [lax.ppermute(x, 'blk', swap) for x in sends]  4.12 us
    ppermute x1, starting transfers between devices, at_source(): table_other = lax.ppermute(slot_table, 'blk', swap)  2.49 us
    ppermute x4, waiting for transfers between devices, at_source(): got = [lax.ppermute(x, 'blk', swap) for x in sends]  1.59 us
  transfers between devices with their start and end apart: 9, of which 4 were waited for; matrix products, arithmetic and copies ran while one was open for 0% of the time, Pallas kernels for 12%

profile of v4, /device:TPU:0, one launch (start us, length us, event | category | flops | bytes accessed | tf_op | source)
XLA Modules:
  0.0 28.2 jit_solution(13250548612128574079)
XLA Ops:
  0.0 0.5 %collective-permute-start = (bf16[12,128,128]{2,1,0:T(8,128)(2,1)}, bf16[12,128,128]{2,1,0:T(8,128)(2,1)S(1)}, u32[]{:S(2)}, u32[]{:S(2)}) collective-permute-start(bf16[12,128,128]{2,1,0:T(8,128)(2,1)} %wave.1), channel_id=1, source_target_pairs={{0,1},{1,0},{2,3},{3,2},{4,5},{5,4},{6,7},{7,6},{8,9},{9,8},{10,11... | collective-permute-start | bytes 1179656 | tf_op jit(solution)/shard_map/ppermute | solution.py:135
  0.5 2.5 %collective-permute-start.1 = (s32[3,1,1,2,2,64]{5,4,3,2,1,0:T(2,128)}, s32[3,1,1,2,2,64]{5,4,3,2,1,0:T(2,128)S(1)}, u32[]{:S(2)}, u32[]{:S(2)}) collective-permute-start(s32[3,1,1,2,2,64]{5,4,3,2,1,0:T(2,128)} %table.1), channel_id=1, source_target_pairs={{0,2},{2,0},{1,3},{3,1},{4,6},{6,4},{5,7},{7,5},{8,10},{10,8},{9,1... | collective-permute-start | bytes 9224 | tf_op jit(solution)/shard_map/ppermute | solution.py:134
  2.9 3.3 %shard_map.46 = (bf16[32,64,128]{2,1,0:T(8,128)(2,1)S(1)}, bf16[32,128,128]{2,1,0:T(8,128)(2,1)S(1)}, bf16[12,128,128]{2,1,0:T(8,128)(2,1)S(1)}, s32[3,1,1,2,2,64]{5,4,3,2,1,0:T(2,128)S(4)}, f32[25,64,128]{2,1,0:T(8,128)S(1)}) custom-call(bf16[32,128,128]{2,1,0:T(8,128)(2,1)} %left.1, bf16[32,128,128]{2,1,0:T(8,128)(2,1)} %right.1, ...), custom_call_target="tpu_custom_call" | custom-call | tf_op jit(solution)/shard_map/pallas_call | solution.py:115
  6.2 0.0 collective-permute-done.1.table_other
  6.2 0.0 collective-permute-done.wave_pair
  6.3 1.5 %shard_map.47 = (f32[25,64,128]{2,1,0:T(8,128)S(1)}, s32[3,1,1,2,2,64]{5,4,3,2,1,0:T(2,128)S(4)}, f32[24,16,128]{2,1,0:T(8,128)S(1)}, f32[24,16,128]{2,1,0:T(8,1...) custom-call(s32[3,1,1,2,2,64]{5,4,3,2,1,0:T(2,128)S(4)} %get-tuple-element.20.tab, ...), custom_call_target="tpu_custom_call", output_to_operand_aliasing={{0}: (4, {})} | custom-call | tf_op jit(solution)/shard_map/pallas_call | solution.py:115
  7.8 3.0 %shard_map.48 = (f32[25,64,128]{2,1,0:T(8,128)S(1)}, bf16[24,16,128]{2,1,0:T(8,128)(2,1)S(1)}, bf16[24,16,128]{2,1,0:T(8,128)(2,1)S(1)}, bf16[24,16,128]{2,1,0:T(8,128)(2,1)S(1)}, bf16[24,16,128]{2,1,0:T(8,128)(2,1)S(1)}) custom-call(s32[3,1,1,2,2,64]{5,4,3,2,1,0:T(2,128)S(4)} %get-tuple-element.25.table, ...), custom_call_target="tpu_custom_call", output_to_operand_aliasing={{0}: (5, {})} | custom-call | tf_op jit(solution)/shard_map/pallas_call | solution.py:115
  10.8 0.6 %collective-permute-start.3 = (bf16[24,16,128]{2,1,0:T(8,128)(2,1)S(1)}, bf16[24,16,128]{2,1,0:T(8,128)(2,1)S(1)}, u32[]{:S(2)}, u32[]{:S(2)}) collective-permute-start(bf16[24,16,128]{2,1,0:T(8,128)(2,1)S(1)} %get-tuple-element.30), channel_id=1, source_target_pairs={{0,2},{2,0},{1,3},{3,1},{4,6},{6,4},{5,7},{7,5},{8,10},{10,8},{9,1... | collective-permute-start | bytes 294920 | tf_op jit(solution)/shard_map/ppermute | solution.py:171
  11.3 1.5 %collective-permute-start.5 = (bf16[24,16,128]{2,1,0:T(8,128)(2,1)S(1)}, bf16[24,16,128]{2,1,0:T(8,128)(2,1)S(1)}, u32[]{:S(2)}, u32[]{:S(2)}) collective-permute-start(bf16[24,16,128]{2,1,0:T(8,128)(2,1)S(1)} %get-tuple-element.32), channel_id=1, source_target_pairs={{0,2},{2,0},{1,3},{3,1},{4,6},{6,4},{5,7},{7,5},{8,10},{10,8},{9,1... | collective-permute-start | bytes 294920 | tf_op jit(solution)/shard_map/ppermute | solution.py:171
  12.9 0.5 %collective-permute-start.7 = (bf16[24,16,128]{2,1,0:T(8,128)(2,1)S(1)}, bf16[24,16,128]{2,1,0:T(8,128)(2,1)S(1)}, u32[]{:S(2)}, u32[]{:S(2)}) collective-permute-start(bf16[24,16,128]{2,1,0:T(8,128)(2,1)S(1)} %get-tuple-element.34), channel_id=1, source_target_pairs={{0,2},{2,0},{1,3},{3,1},{4,6},{6,4},{5,7},{7,5},{8,10},{10,8},{9,1... | collective-permute-start | bytes 294920 | tf_op jit(solution)/shard_map/ppermute | solution.py:171
  13.4 1.5 %collective-permute-start.2 = (bf16[24,16,128]{2,1,0:T(8,128)(2,1)S(1)}, bf16[24,16,128]{2,1,0:T(8,128)(2,1)S(1)}, u32[]{:S(2)}, u32[]{:S(2)}) collective-permute-start(bf16[24,16,128]{2,1,0:T(8,128)(2,1)S(1)} %get-tuple-element.28), channel_id=1, source_target_pairs={{0,2},{2,0},{1,3},{3,1},{4,6},{6,4},{5,7},{7,5},{8,10},{10,8},{9,1... | collective-permute-start | bytes 294920 | tf_op jit(solution)/shard_map/ppermute | solution.py:171
  14.9 1.6 %collective-permute-done.3.got = bf16[24,16,128]{2,1,0:T(8,128)(2,1)S(1)} collective-permute-done((bf16[24,16,128]{2,1,0:T(8,128)(2,1)S(1)}, bf16[24,16,128]{2,1,0:T(8,128)(2,1)S(1)}, u32[]{:S(2)}, u32[]{:S(2)}) %collective-permute-start.3) | collective-permute-done | bytes 98336 | tf_op jit(solution)/shard_map/ppermute | solution.py:171
  16.5 2.6 %collective-permute-start.4 = (bf16[24,16,128]{2,1,0:T(8,128)(2,1)S(1)}, bf16[24,16,128]{2,1,0:T(8,128)(2,1)S(1)}, u32[]{:S(2)}, u32[]{:S(2)}) collective-permute-start(bf16[24,16,128]{2,1,0:T(8,128)(2,1)S(1)} %shard_map.49), channel_id=1, source_target_pairs={{0,8},{4,12},{8,0},{12,4},{1,9},{5,13},{9,1},{13,5},{2,10},{6,14},... | collective-permute-start | bytes 294920 | tf_op jit(solution)/shard_map/ppermute | solution.py:174
  19.1 0.0 collective-permute-done.5.got
  19.1 3.1 %collective-permute-start.6 = (bf16[24,16,128]{2,1,0:T(8,128)(2,1)S(1)}, bf16[24,16,128]{2,1,0:T(8,128)(2,1)S(1)}, u32[]{:S(2)}, u32[]{:S(2)}) collective-permute-start(bf16[24,16,128]{2,1,0:T(8,128)(2,1)S(1)} %shard_map.50), channel_id=1, source_target_pairs={{0,12},{4,8},{8,4},{12,0},{1,13},{5,9},{9,5},{13,1},{2,14},{6,10},... | collective-permute-start | bytes 294920 | tf_op jit(solution)/shard_map/ppermute | solution.py:174
  22.2 0.0 collective-permute-done.7.got
  22.2 0.1 collective-permute-start.8
  22.3 0.0 collective-permute-done.2.rest_0_
  22.3 3.1 %collective-permute-done.4.rest_1_ = bf16[24,16,128]{2,1,0:T(8,128)(2,1)S(1)} collective-permute-done((bf16[24,16,128]{2,1,0:T(8,128)(2,1)S(1)}, bf16[24,16,128]{2,1,0:T(8,128)(2,1)S(1)}, u32[]{:S(2)}, u32[]{:S(2)}) %collective-permute-start.4) | collective-permute-done | bytes 98336 | tf_op jit(solution)/shard_map/ppermute | solution.py:174
  25.5 0.8 %collective-permute-done.6.rest_2_ = bf16[24,16,128]{2,1,0:T(8,128)(2,1)S(1)} collective-permute-done((bf16[24,16,128]{2,1,0:T(8,128)(2,1)S(1)}, bf16[24,16,128]{2,1,0:T(8,128)(2,1)S(1)}, u32[]{:S(2)}, u32[]{:S(2)}) %collective-permute-start.6) | collective-permute-done | bytes 98336 | tf_op jit(solution)/shard_map/ppermute | solution.py:174
  26.3 1.1 %collective-permute-done.8.rest_3_ = bf16[24,16,128]{2,1,0:T(8,128)(2,1)S(1)} collective-permute-done((bf16[24,16,128]{2,1,0:T(8,128)(2,1)S(1)}, bf16[24,16,128]{2,1,0:T(8,128)(2,1)S(1)}, u32[]{:S(2)}, u32[]{:S(2)}) %collective-permute-start.8) | collective-permute-done | bytes 98336 | tf_op jit(solution)/shard_map/ppermute | solution.py:174
  27.4 0.8 %shard_map.52 = f32[16,24,128]{2,1,0:T(8,128)} custom-call(f32[24,16,128]{2,1,0:T(8,128)S(1)} %get-tuple-element.24.own, bf16[24,16,128]{2,1,0:T(8,128)(2,1)S(1)} %collective-permute-done.2.rest_0_, bf16[24,16,128]{2,1,0:T(8,128)(2,1)S(1)} %collective-permute-done.4.rest_1_, bf16[24,16,128]{2,1,0:T(8,128)(2,1)S(1)} %collective-permute-done.6.rest_2_, ...), custom_call_target="tpu_custom_call" | custom-call | tf_op jit(solution)/shard_map/pallas_call | solution.py:115
  (3 shorter events, 0.1 us)
Async XLA Ops:
  0.0 6.2 %collective-permute-start = (bf16[12,128,128]{2,1,0:T(8,128)(2,1)}, bf16[12,128,128]{2,1,0:T(8,128)(2,1)S(1)}, u32[]{:S(2)}, u32[]{:S(2)}) collective-permute-start(bf16[12,128,128]{2,1,0:T(8,128)(2,1)} %wave.1), channel_id=1, source_target_pairs={{0,1},{1,0},{2,3},{3,2},{4,5},{5,4},{6,7},{7,6},{8,9},{9,8},{10,11... | collective-permute-start | bytes 1179656 | tf_op jit(solution)/shard_map/ppermute | solution.py:135
  0.5 5.8 %collective-permute-start.1 = (s32[3,1,1,2,2,64]{5,4,3,2,1,0:T(2,128)}, s32[3,1,1,2,2,64]{5,4,3,2,1,0:T(2,128)S(1)}, u32[]{:S(2)}, u32[]{:S(2)}) collective-permute-start(s32[3,1,1,2,2,64]{5,4,3,2,1,0:T(2,128)} %table.1), channel_id=1, source_target_pairs={{0,2},{2,0},{1,3},{3,1},{4,6},{6,4},{5,7},{7,5},{8,10},{10,8},{9,1... | collective-permute-start | bytes 9224 | tf_op jit(solution)/shard_map/ppermute | solution.py:134
  10.8 5.7 %collective-permute-start.3 = (bf16[24,16,128]{2,1,0:T(8,128)(2,1)S(1)}, bf16[24,16,128]{2,1,0:T(8,128)(2,1)S(1)}, u32[]{:S(2)}, u32[]{:S(2)}) collective-permute-start(bf16[24,16,128]{2,1,0:T(8,128)(2,1)S(1)} %get-tuple-element.30), channel_id=1, source_target_pairs={{0,2},{2,0},{1,3},{3,1},{4,6},{6,4},{5,7},{7,5},{8,10},{10,8},{9,1... | collective-permute-start | bytes 294920 | tf_op jit(solution)/shard_map/ppermute | solution.py:171
  11.3 7.7 %collective-permute-start.5 = (bf16[24,16,128]{2,1,0:T(8,128)(2,1)S(1)}, bf16[24,16,128]{2,1,0:T(8,128)(2,1)S(1)}, u32[]{:S(2)}, u32[]{:S(2)}) collective-permute-start(bf16[24,16,128]{2,1,0:T(8,128)(2,1)S(1)} %get-tuple-element.32), channel_id=1, source_target_pairs={{0,2},{2,0},{1,3},{3,1},{4,6},{6,4},{5,7},{7,5},{8,10},{10,8},{9,1... | collective-permute-start | bytes 294920 | tf_op jit(solution)/shard_map/ppermute | solution.py:171
  12.9 9.4 %collective-permute-start.7 = (bf16[24,16,128]{2,1,0:T(8,128)(2,1)S(1)}, bf16[24,16,128]{2,1,0:T(8,128)(2,1)S(1)}, u32[]{:S(2)}, u32[]{:S(2)}) collective-permute-start(bf16[24,16,128]{2,1,0:T(8,128)(2,1)S(1)} %get-tuple-element.34), channel_id=1, source_target_pairs={{0,2},{2,0},{1,3},{3,1},{4,6},{6,4},{5,7},{7,5},{8,10},{10,8},{9,1... | collective-permute-start | bytes 294920 | tf_op jit(solution)/shard_map/ppermute | solution.py:171
  13.4 9.0 %collective-permute-start.2 = (bf16[24,16,128]{2,1,0:T(8,128)(2,1)S(1)}, bf16[24,16,128]{2,1,0:T(8,128)(2,1)S(1)}, u32[]{:S(2)}, u32[]{:S(2)}) collective-permute-start(bf16[24,16,128]{2,1,0:T(8,128)(2,1)S(1)} %get-tuple-element.28), channel_id=1, source_target_pairs={{0,2},{2,0},{1,3},{3,1},{4,6},{6,4},{5,7},{7,5},{8,10},{10,8},{9,1... | collective-permute-start | bytes 294920 | tf_op jit(solution)/shard_map/ppermute | solution.py:171
  16.5 9.0 %collective-permute-start.4 = (bf16[24,16,128]{2,1,0:T(8,128)(2,1)S(1)}, bf16[24,16,128]{2,1,0:T(8,128)(2,1)S(1)}, u32[]{:S(2)}, u32[]{:S(2)}) collective-permute-start(bf16[24,16,128]{2,1,0:T(8,128)(2,1)S(1)} %shard_map.49), channel_id=1, source_target_pairs={{0,8},{4,12},{8,0},{12,4},{1,9},{5,13},{9,1},{13,5},{2,10},{6,14},... | collective-permute-start | bytes 294920 | tf_op jit(solution)/shard_map/ppermute | solution.py:174
  19.1 7.2 %collective-permute-start.6 = (bf16[24,16,128]{2,1,0:T(8,128)(2,1)S(1)}, bf16[24,16,128]{2,1,0:T(8,128)(2,1)S(1)}, u32[]{:S(2)}, u32[]{:S(2)}) collective-permute-start(bf16[24,16,128]{2,1,0:T(8,128)(2,1)S(1)} %shard_map.50), channel_id=1, source_target_pairs={{0,12},{4,8},{8,4},{12,0},{1,13},{5,9},{9,5},{13,1},{2,14},{6,10},... | collective-permute-start | bytes 294920 | tf_op jit(solution)/shard_map/ppermute | solution.py:174
  22.2 5.1 %collective-permute-start.8 = (bf16[24,16,128]{2,1,0:T(8,128)(2,1)S(1)}, bf16[24,16,128]{2,1,0:T(8,128)(2,1)S(1)}, u32[]{:S(2)}, u32[]{:S(2)}) collective-permute-start(bf16[24,16,128]{2,1,0:T(8,128)(2,1)S(1)} %shard_map.51), channel_id=1, source_target_pairs={{0,4},{4,0},{8,12},{12,8},{1,5},{5,1},{9,13},{13,9},{2,6},{6,2},{1... | collective-permute-start | bytes 294920 | tf_op jit(solution)/shard_map/ppermute | solution.py:174

commit v5 on v4

--- a/solution.py
+++ b/solution.py
@@ -11,6 +11,7 @@
 SMEM = pl.BlockSpec(memory_space=pltpu.SMEM)
 ANY = pl.BlockSpec(memory_space=pl.ANY)
 LINK = jnp.bfloat16
+COSTLY = pl.CostEstimate(flops=16 << 30, bytes_accessed=64 << 20, transcendentals=0)
 
 
 def params():
@@ -73,33 +74,46 @@
 
 
 def split_rows(acc, outs):
-    for g, out in enumerate(outs):
-        tiles, rows, _ = out.shape
-        out[...] = acc[0:tiles, g * rows : (g + 1) * rows, :].astype(out.dtype)
-
-
-def own_kernel(table, left_rows, right_t, wave_pair, start, table_other, acc, other_here, *outs):
-    del start
-    *outs, sem = outs
+    first = 0
+    for out in outs:
+        tiles, rows, _ = out.shape[-3:]
+        for g in range(out.shape[0] if len(out.shape) == 4 else 1):
+            block = acc[0:tiles, first : first + rows, :].astype(out.dtype)
+            if len(out.shape) == 4:
+                out[g] = block
+            else:
+                out[...] = block
+            first += rows
+
+
+def other_kernel(table, left_rows, right_t, wave, wave_pair, *refs):
+    *outs, acc, table_here, sem = refs
     rep, blk = lax.axis_index("rep"), lax.axis_index("blk")
-    copy = pltpu.make_async_copy(table_other, other_here, sem)
+    copy = pltpu.make_async_copy(table, table_here, sem)
     copy.start()
+    acc[...] = jnp.zeros_like(acc)
+    copy.wait()
+    add_list(table_here, rep, blk, left_rows, right_t, wave, acc)
+    add_list(table_here, 1 - rep, blk, left_rows, right_t, wave_pair, acc)
+    split_rows(acc, outs)
+
+
+def own_kernel(table, left_rows, right_t, wave_pair, start, later, acc, handed_on, *outs):
+    del start, later, handed_on
+    rep, blk = lax.axis_index("rep"), lax.axis_index("blk")
     add_list(table, 1 - rep, blk, left_rows, right_t, wave_pair, acc)
     split_rows(acc, outs)
-    copy.wait()
-
-
-def other_kernel(table, left_rows, right_t, wave, wave_pair, spare, acc, *outs):
-    del spare
-    rep, blk = lax.axis_index("rep"), lax.axis_index("blk")
-    acc[...] = jnp.zeros_like(acc)
-    add_list(table, rep, blk, left_rows, right_t, wave, acc)
-    add_list(table, 1 - rep, blk, left_rows, right_t, wave_pair, acc)
-    split_rows(acc, outs)
-
-
-def sum_kernel(kept, got, out):
+
+
+def sum_kernel(kept, got, later, out, handed_on):
+    del later, handed_on
     out[...] = (kept[...] + got[...].astype(jnp.float32)).astype(out.dtype)
+
+
+def sums_kernel(kept, got, later, handed_on, *outs):
+    del later, handed_on
+    for g, out in enumerate(outs):
+        out[...] = (kept[g] + got[g].astype(jnp.float32)).astype(out.dtype)
 
 
 def final_kernel(own, *rest):
@@ -151,36 +165,60 @@
             pltpu.SemaphoreType.DMA((3 + op_count,)),
         ],
     )
-    acc, other_table, *kept = call(
-        own_kernel,
-        (acc_shape, table_spec) + (shape(block, f32),) * op_count,
-        (own_table, left_rows, right_t, wave_pair, acc, table_other),
-        [SMEM] + [VMEM] * 4 + [ANY],
-        (VMEM, SMEM) + (VMEM,) * op_count,
-        input_output_aliases={4: 0},
-        scratch_shapes=[pltpu.SemaphoreType.DMA],
-    )
-    _, *sends = call(
+    blocks = (block, (op_count - 2,) + block, block)
+    first, middle, last = call(
         other_kernel,
-        (acc_shape,) + (shape(block, LINK),) * op_count,
-        (other_table, left_rows, right_t, wave, wave_pair, acc),
-        [SMEM] + [VMEM] * 5,
-        (VMEM,) * (1 + op_count),
-        input_output_aliases={5: 0},
-    )
-    got = [lax.ppermute(x, "blk", swap) for x in sends]
+        tuple(shape(b, LINK) for b in blocks),
+        (table_other, left_rows, right_t, wave, wave_pair),
+        [ANY] + [VMEM] * 4,
+        (VMEM,) * 3,
+        scratch_shapes=[
+            pltpu.VMEM(acc_shape.shape, f32),
+            pltpu.SMEM(slot_table.shape, slot_table.dtype),
+            pltpu.SemaphoreType.DMA,
+        ],
+    )
+
+    def to_blk(x):
+        return lax.ppermute(x, "blk", swap)
 
     def to_op(x, s):
         return lax.ppermute(x, "op", [(i, i ^ s) for i in range(op_count)])
 
-    arrived = []
-    for g in range(op_count - 1):
-        total = call(sum_kernel, shape(block, LINK), (kept[g], got[g]), [VMEM] * 2, VMEM)
-        arrived.append(to_op(total, order[g]))
+    got_first = to_blk(first)
+    _, middle, kept_first, kept_middle, kept_last = call(
+        own_kernel,
+        (acc_shape, shape(middle.shape, LINK)) + tuple(shape(b, f32) for b in blocks),
+        (own_table, left_rows, right_t, wave_pair, acc, middle),
+        [SMEM] + [VMEM] * 4 + [ANY],
+        (VMEM, ANY) + (VMEM,) * 3,
+        input_output_aliases={4: 0, 5: 1},
+        cost_estimate=COSTLY,
+    )
+    got_middle = to_blk(middle)
+    total, last = call(
+        sum_kernel,
+        (shape(block, LINK),) * 2,
+        (kept_first, got_first, last),
+        [VMEM] * 2 + [ANY],
+        (VMEM, ANY),
+        input_output_aliases={2: 1},
+        cost_estimate=COSTLY,
+    )
+    arrived = [to_op(total, order[0])]
+    last, *totals = call(
+        sums_kernel,
+        (shape(block, LINK),) * (op_count - 1),
+        (kept_middle, got_middle, last),
+        [VMEM] * 2 + [ANY],
+        (ANY,) + (VMEM,) * (op_count - 2),
+        input_output_aliases={2: 0},
+    )
+    arrived += [to_op(x, s) for x, s in zip(totals, order[1:])]
     return call(
         final_kernel,
         shape((rows, tiles, width), f32),
-        (kept[-1], got[-1], *arrived),
+        (kept_last, to_blk(last), *arrived),
         [VMEM] * (op_count + 1),
         VMEM,
     )
@@ -222,7 +260,7 @@
     op_count = lax.axis_size("op")
     rows = left_env.shape[1] // (2 * op_count)
     fits = lax.axis_size("rep") == 2 and lax.axis_size("blk") == 2
-    fits = fits and op_count > 1 and op_count & (op_count - 1) == 0
+    fits = fits and op_count > 2 and op_count & (op_count - 1) == 0
     fits = fits and rows % 16 == 0 and rows * 2 * op_count == left_env.shape[1]
     form = at_source if fits else gathered
     return form(wavefunction, left_env, right_env, slot_table)

time: 28.3 us -> 29.3 us (1.035)
  waiting for transfers between devices: 6.61 us -> 7.74 us
  starting transfers between devices: 12.8 us -> 12.4 us
  Pallas kernels: 8.66 us -> 9.01 us
    ppermute x4 -> x3, waiting for transfers between devices: 1.59 us -> 3.13 us  [to_blk(): return lax.ppermute(x, 'blk', swap)]
    ppermute x4 -> x3, starting transfers between devices: 4.12 us -> 3.37 us  [to_blk(): return lax.ppermute(x, 'blk', swap)]
    ppermute x3, waiting for transfers between devices: 5.02 us -> 4.61 us  [to_op(): return lax.ppermute(x, 'op', [(i, i ^ s) for i in range(op_count)])]
    pallas_call x7 -> x6, Pallas kernels: 8.66 us -> 9.01 us  [call(): pl.pallas_call(kernel, out_shape=out_shape, in_specs=ins, out_specs=outs,...]
    ppermute x3, starting transfers between devices: 5.76 us -> 6.06 us  [to_op(): return lax.ppermute(x, 'op', [(i, i ^ s) for i in range(op_count)])]
  transfers between devices with their start and end apart: 9 -> 8, of which waited for: 4 -> 4; matrix products, arithmetic and copies ran while one was open for 0% -> 0% of each run, Pallas kernels for 12% -> 16%
where the time goes in v5:
time: 29.3 us; the launch traced here: 29.2 us
  starting transfers between devices  12.4 us (42%)
  Pallas kernels  9.01 us (31%)
  waiting for transfers between devices  7.74 us (26%)
    pallas_call x6, Pallas kernels, call(): pl.pallas_call(kernel, out_shape=out_shape, in_specs=ins, out_specs=outs,...  9.01 us
    ppermute x3, starting transfers between devices, to_op(): return lax.ppermute(x, 'op', [(i, i ^ s) for i in range(op_count)])  6.06 us
    ppermute x3, waiting for transfers between devices, to_op(): return lax.ppermute(x, 'op', [(i, i ^ s) for i in range(op_count)])  4.61 us
    ppermute x3, starting transfers between devices, to_blk(): return lax.ppermute(x, 'blk', swap)  3.37 us
    ppermute x3, waiting for transfers between devices, to_blk(): return lax.ppermute(x, 'blk', swap)  3.13 us
    ppermute x1, starting transfers between devices, at_source(): table_other = lax.ppermute(slot_table, 'blk', swap)  2.49 us
  transfers between devices with their start and end apart: 8, of which 4 were waited for; matrix products, arithmetic and copies ran while one was open for 0% of the time, Pallas kernels for 16%

profile of v5, /device:TPU:0, one launch (start us, length us, event | category | flops | bytes accessed | tf_op | source)
XLA Modules:
  0.0 29.2 jit_solution(7990680689895502040)
XLA Ops:
  0.0 0.5 %collective-permute-start = (bf16[12,128,128]{2,1,0:T(8,128)(2,1)}, bf16[12,128,128]{2,1,0:T(8,128)(2,1)S(1)}, u32[]{:S(2)}, u32[]{:S(2)}) collective-permute-start(bf16[12,128,128]{2,1,0:T(8,128)(2,1)} %wave.1), channel_id=1, source_target_pairs={{0,1},{1,0},{2,3},{3,2},{4,5},{5,4},{6,7},{7,6},{8,9},{9,8},{10,11... | collective-permute-start | bytes 1179656 | tf_op jit(solution)/shard_map/ppermute | solution.py:149
  0.5 2.5 %collective-permute-start.1 = (s32[3,1,1,2,2,64]{5,4,3,2,1,0:T(2,128)}, s32[3,1,1,2,2,64]{5,4,3,2,1,0:T(2,128)S(1)}, u32[]{:S(2)}, u32[]{:S(2)}) collective-permute-start(s32[3,1,1,2,2,64]{5,4,3,2,1,0:T(2,128)} %table.1), channel_id=1, source_target_pairs={{0,2},{2,0},{1,3},{3,1},{4,6},{6,4},{5,7},{7,5},{8,10},{10,8},{9,1... | collective-permute-start | bytes 9224 | tf_op jit(solution)/shard_map/ppermute | solution.py:148
  2.9 3.2 %shard_map.46 = (bf16[32,64,128]{2,1,0:T(8,128)(2,1)S(1)}, bf16[32,128,128]{2,1,0:T(8,128)(2,1)S(1)}, bf16[12,128,128]{2,1,0:T(8,128)(2,1)S(1)}, s32[3,1,1,2,2,64]{5,4,3,2,1,0:T(2,128)S(4)}, f32[25,64,128]{2,1,0:T(8,128)S(1)}) custom-call(bf16[32,128,128]{2,1,0:T(8,128)(2,1)} %left.1, bf16[32,128,128]{2,1,0:T(8,128)(2,1)} %right.1, ...), custom_call_target="tpu_custom_call" | custom-call | tf_op jit(solution)/shard_map/pallas_call | solution.py:129
  6.2 0.0 collective-permute-done.1.table
  6.2 0.0 collective-permute-done.wave_pair
  6.2 3.5 %shard_map.47 = (bf16[24,16,128]{2,1,0:T(8,128)(2,1)S(1)}, bf16[2,24,16,128]{3,2,1,0:T(8,128)(2,1)S(1)}, bf16[24,16,128]{2,1,0:T(8,128)(2,1)S(1)}) custom-call(s32[3,1,1,2,2,64]{5,4,3,2,1,0:T(2,128)S(1)} %collective-permute-done.1.table, bf16[32,64,128]{2,1,0:T(8,128)(2,1)S(1)} %get-tuple-element.23.left_rows, ...), custom_call_target="tpu_custom_call" | custom-call | tf_op jit(solution)/shard_map/pallas_call | solution.py:129
  9.7 0.6 %collective-permute-start.3 = (bf16[24,16,128]{2,1,0:T(8,128)(2,1)S(1)}, bf16[24,16,128]{2,1,0:T(8,128)(2,1)S(1)}, u32[]{:S(2)}, u32[]{:S(2)}) collective-permute-start(bf16[24,16,128]{2,1,0:T(8,128)(2,1)S(1)} %get-tuple-element.32), channel_id=1, source_target_pairs={{0,2},{2,0},{1,3},{3,1},{4,6},{6,4},{5,7},{7,5},{8,10},{10,8},{9,1... | collective-permute-start | bytes 294920 | tf_op jit(solution)/shard_map/ppermute | solution.py:183
  10.3 1.4 %shard_map.48 = (f32[25,64,128]{2,1,0:T(8,128)S(1)}, bf16[2,24,16,128]{3,2,1,0:T(8,128)(2,1)S(1)}, f32[24,16,128]{2,1,0:T(8,128)S(1)}, f32[2,24,16,128]{3,2,1,0:T(8,128)S(1)}, f32[24,16,128]{2,1,0:T(8,128)S(1)}) custom-call(s32[3,1,1,2,2,64]{5,4,3,2,1,0:T(2,128)S(4)} %get-tuple-element.22.table, ...), custom_call_target="tpu_custom_call", output_to_operand_aliasing={{0}: (4, {}), {1}: (5, {})} | custom-call | flops 17179869184 | bytes 67108864 | tf_op jit(solution)/shard_map/pallas_call | solution.py:129
  11.8 1.5 %collective-permute-start.2 = (bf16[2,24,16,128]{3,2,1,0:T(8,128)(2,1)S(1)}, bf16[2,24,16,128]{3,2,1,0:T(8,128)(2,1)S(1)}, u32[]{:S(2)}, u32[]{:S(2)}) collective-permute-start(bf16[2,24,16,128]{3,2,1,0:T(8,128)(2,1)S(1)} %get-tuple-element.30), channel_id=1, source_target_pairs={{0,2},{2,0},{1,3},{3,1},{4,6},{6,4},{5,7},{7,5},{8,10},{10,8},{9,1... | collective-permute-start | bytes 589832 | tf_op jit(solution)/shard_map/ppermute | solution.py:183
  13.3 2.0 %collective-permute-done.3.got = bf16[24,16,128]{2,1,0:T(8,128)(2,1)S(1)} collective-permute-done((bf16[24,16,128]{2,1,0:T(8,128)(2,1)S(1)}, bf16[24,16,128]{2,1,0:T(8,128)(2,1)S(1)}, u32[]{:S(2)}, u32[]{:S(2)}) %collective-permute-start.3) | collective-permute-done | bytes 98336 | tf_op jit(solution)/shard_map/ppermute | solution.py:183
  15.3 2.5 %collective-permute-start.5 = (bf16[24,16,128]{2,1,0:T(8,128)(2,1)S(1)}, bf16[24,16,128]{2,1,0:T(8,128)(2,1)S(1)}, u32[]{:S(2)}, u32[]{:S(2)}) collective-permute-start(bf16[24,16,128]{2,1,0:T(8,128)(2,1)S(1)} %get-tuple-element.36), channel_id=1, source_target_pairs={{0,8},{4,12},{8,0},{12,4},{1,9},{5,13},{9,1},{13,5},{2,10},{6,14},... | collective-permute-start | bytes 294920 | tf_op jit(solution)/shard_map/ppermute | solution.py:186
  17.7 1.2 %collective-permute-done.2.got = bf16[2,24,16,128]{3,2,1,0:T(8,128)(2,1)S(1)} collective-permute-done((bf16[2,24,16,128]{3,2,1,0:T(8,128)(2,1)S(1)}, bf16[2,24,16,128]{3,2,1,0:T(8,128)(2,1)S(1)}, u32[]{:S(2)}, u32[]{:S(2)}) %collective-permute-start.2) | collective-permute-done | bytes 196640 | tf_op jit(solution)/shard_map/ppermute | solution.py:183
  18.9 1.2 %collective-permute-start.4 = (bf16[24,16,128]{2,1,0:T(8,128)(2,1)S(1)}, bf16[24,16,128]{2,1,0:T(8,128)(2,1)S(1)}, u32[]{:S(2)}, u32[]{:S(2)}) collective-permute-start(bf16[24,16,128]{2,1,0:T(8,128)(2,1)S(1)} %get-tuple-element.35), channel_id=1, source_target_pairs={{0,2},{2,0},{1,3},{3,1},{4,6},{6,4},{5,7},{7,5},{8,10},{10,8},{9,1... | collective-permute-start | bytes 294920 | tf_op jit(solution)/shard_map/ppermute | solution.py:183
  20.1 3.6 %collective-permute-start.6 = (bf16[24,16,128]{2,1,0:T(8,128)(2,1)S(1)}, bf16[24,16,128]{2,1,0:T(8,128)(2,1)S(1)}, u32[]{:S(2)}, u32[]{:S(2)}) collective-permute-start(bf16[24,16,128]{2,1,0:T(8,128)(2,1)S(1)} %get-tuple-element.37), channel_id=1, source_target_pairs={{0,12},{4,8},{8,4},{12,0},{1,13},{5,9},{9,5},{13,1},{2,14},{6,10},... | collective-permute-start | bytes 294920 | tf_op jit(solution)/shard_map/ppermute | solution.py:186
  23.7 0.0 collective-permute-start.7
  23.7 0.0 collective-permute-done.5.rest_1_
  23.7 0.0 collective-permute-done.4.rest_0_
  23.8 3.0 %collective-permute-done.6.rest_2_ = bf16[24,16,128]{2,1,0:T(8,128)(2,1)S(1)} collective-permute-done((bf16[24,16,128]{2,1,0:T(8,128)(2,1)S(1)}, bf16[24,16,128]{2,1,0:T(8,128)(2,1)S(1)}, u32[]{:S(2)}, u32[]{:S(2)}) %collective-permute-start.6) | collective-permute-done | bytes 98336 | tf_op jit(solution)/shard_map/ppermute | solution.py:186
  26.8 1.6 %collective-permute-done.7.rest_3_ = bf16[24,16,128]{2,1,0:T(8,128)(2,1)S(1)} collective-permute-done((bf16[24,16,128]{2,1,0:T(8,128)(2,1)S(1)}, bf16[24,16,128]{2,1,0:T(8,128)(2,1)S(1)}, u32[]{:S(2)}, u32[]{:S(2)}) %collective-permute-start.7) | collective-permute-done | bytes 98336 | tf_op jit(solution)/shard_map/ppermute | solution.py:186
  28.4 0.8 %shard_map.51 = f32[16,24,128]{2,1,0:T(8,128)} custom-call(f32[24,16,128]{2,1,0:T(8,128)S(1)} %get-tuple-element.28.own, bf16[24,16,128]{2,1,0:T(8,128)(2,1)S(1)} %collective-permute-done.4.rest_0_, bf16[24,16,128]{2,1,0:T(8,128)(2,1)S(1)} %collective-permute-done.5.rest_1_, bf16[24,16,128]{2,1,0:T(8,128)(2,1)S(1)} %collective-permute-done.6.rest_2_, ...), custom_call_target="tpu_custom_call" | custom-call | tf_op jit(solution)/shard_map/pallas_call | solution.py:129
  (2 shorter events, 0.1 us)
Async XLA Ops:
  0.0 6.2 %collective-permute-start = (bf16[12,128,128]{2,1,0:T(8,128)(2,1)}, bf16[12,128,128]{2,1,0:T(8,128)(2,1)S(1)}, u32[]{:S(2)}, u32[]{:S(2)}) collective-permute-start(bf16[12,128,128]{2,1,0:T(8,128)(2,1)} %wave.1), channel_id=1, source_target_pairs={{0,1},{1,0},{2,3},{3,2},{4,5},{5,4},{6,7},{7,6},{8,9},{9,8},{10,11... | collective-permute-start | bytes 1179656 | tf_op jit(solution)/shard_map/ppermute | solution.py:149
  0.5 5.7 %collective-permute-start.1 = (s32[3,1,1,2,2,64]{5,4,3,2,1,0:T(2,128)}, s32[3,1,1,2,2,64]{5,4,3,2,1,0:T(2,128)S(1)}, u32[]{:S(2)}, u32[]{:S(2)}) collective-permute-start(s32[3,1,1,2,2,64]{5,4,3,2,1,0:T(2,128)} %table.1), channel_id=1, source_target_pairs={{0,2},{2,0},{1,3},{3,1},{4,6},{6,4},{5,7},{7,5},{8,10},{10,8},{9,1... | collective-permute-start | bytes 9224 | tf_op jit(solution)/shard_map/ppermute | solution.py:148
  9.7 5.6 %collective-permute-start.3 = (bf16[24,16,128]{2,1,0:T(8,128)(2,1)S(1)}, bf16[24,16,128]{2,1,0:T(8,128)(2,1)S(1)}, u32[]{:S(2)}, u32[]{:S(2)}) collective-permute-start(bf16[24,16,128]{2,1,0:T(8,128)(2,1)S(1)} %get-tuple-element.32), channel_id=1, source_target_pairs={{0,2},{2,0},{1,3},{3,1},{4,6},{6,4},{5,7},{7,5},{8,10},{10,8},{9,1... | collective-permute-start | bytes 294920 | tf_op jit(solution)/shard_map/ppermute | solution.py:183
  11.8 7.1 %collective-permute-start.2 = (bf16[2,24,16,128]{3,2,1,0:T(8,128)(2,1)S(1)}, bf16[2,24,16,128]{3,2,1,0:T(8,128)(2,1)S(1)}, u32[]{:S(2)}, u32[]{:S(2)}) collective-permute-start(bf16[2,24,16,128]{3,2,1,0:T(8,128)(2,1)S(1)} %get-tuple-element.30), channel_id=1, source_target_pairs={{0,2},{2,0},{1,3},{3,1},{4,6},{6,4},{5,7},{7,5},{8,10},{10,8},{9,1... | collective-permute-start | bytes 589832 | tf_op jit(solution)/shard_map/ppermute | solution.py:183
  15.3 8.5 %collective-permute-start.5 = (bf16[24,16,128]{2,1,0:T(8,128)(2,1)S(1)}, bf16[24,16,128]{2,1,0:T(8,128)(2,1)S(1)}, u32[]{:S(2)}, u32[]{:S(2)}) collective-permute-start(bf16[24,16,128]{2,1,0:T(8,128)(2,1)S(1)} %get-tuple-element.36), channel_id=1, source_target_pairs={{0,8},{4,12},{8,0},{12,4},{1,9},{5,13},{9,1},{13,5},{2,10},{6,14},... | collective-permute-start | bytes 294920 | tf_op jit(solution)/shard_map/ppermute | solution.py:186
  18.9 4.8 %collective-permute-start.4 = (bf16[24,16,128]{2,1,0:T(8,128)(2,1)S(1)}, bf16[24,16,128]{2,1,0:T(8,128)(2,1)S(1)}, u32[]{:S(2)}, u32[]{:S(2)}) collective-permute-start(bf16[24,16,128]{2,1,0:T(8,128)(2,1)S(1)} %get-tuple-element.35), channel_id=1, source_target_pairs={{0,2},{2,0},{1,3},{3,1},{4,6},{6,4},{5,7},{7,5},{8,10},{10,8},{9,1... | collective-permute-start | bytes 294920 | tf_op jit(solution)/shard_map/ppermute | solution.py:183
  20.1 6.6 %collective-permute-start.6 = (bf16[24,16,128]{2,1,0:T(8,128)(2,1)S(1)}, bf16[24,16,128]{2,1,0:T(8,128)(2,1)S(1)}, u32[]{:S(2)}, u32[]{:S(2)}) collective-permute-start(bf16[24,16,128]{2,1,0:T(8,128)(2,1)S(1)} %get-tuple-element.37), channel_id=1, source_target_pairs={{0,12},{4,8},{8,4},{12,0},{1,13},{5,9},{9,5},{13,1},{2,14},{6,10},... | collective-permute-start | bytes 294920 | tf_op jit(solution)/shard_map/ppermute | solution.py:186
  23.7 4.6 %collective-permute-start.7 = (bf16[24,16,128]{2,1,0:T(8,128)(2,1)S(1)}, bf16[24,16,128]{2,1,0:T(8,128)(2,1)S(1)}, u32[]{:S(2)}, u32[]{:S(2)}) collective-permute-start(bf16[24,16,128]{2,1,0:T(8,128)(2,1)S(1)} %get-tuple-element.38), channel_id=1, source_target_pairs={{0,4},{4,0},{8,12},{12,8},{1,5},{5,1},{9,13},{13,9},{2,6},{6,2},{1... | collective-permute-start | bytes 294920 | tf_op jit(solution)/shard_map/ppermute | solution.py:186

commit v6 on v5

--- a/solution.py
+++ b/solution.py
@@ -11,7 +11,9 @@
 SMEM = pl.BlockSpec(memory_space=pltpu.SMEM)
 ANY = pl.BlockSpec(memory_space=pl.ANY)
 LINK = jnp.bfloat16
-COSTLY = pl.CostEstimate(flops=16 << 30, bytes_accessed=64 << 20, transcendentals=0)
+COST_K = None
+COST_S = (pl.CostEstimate(flops=int(10.0e9), bytes_accessed=int(10.0e6), transcendentals=0), pl.CostEstimate(flops=int(10.0e9), bytes_accessed=int(10.0e6), transcendentals=0), None)
+COST_F = None
 
 
 def params():
@@ -23,15 +25,15 @@
 
 
 def unroll_of(caps, most):
-    return next(u for u in (64, 32, 16, 8, 4, 2, 1) if u <= most and caps % u == 0)
-
-
-def add_list(table, rep, src, left, right_t, wave, acc):
-    caps = table.shape[-1]
-    unroll = unroll_of(caps, 32)
+    return next((u for u in (64, 32, 16, 8, 4, 2, 1) if u <= min(most, caps) and caps % u == 0), 0)
+
+
+def add_list(table, rep, src, left, right_t, wave, acc, begin=0, end=None):
+    end = table.shape[-1] if end is None else end
+    unroll = unroll_of(end - begin, 64)
 
     def body(step, carry):
-        slots = [step * unroll + q for q in range(unroll)]
+        slots = [begin + step * unroll + q for q in range(unroll)]
         terms = [table[0, 0, 0, rep, src, c] for c in slots]
         inner = [
             jnp.dot(
@@ -49,14 +51,14 @@
             acc[table[1, 0, 0, rep, src, slots[q]]] += outer[q]
         return carry
 
-    lax.fori_loop(0, caps // unroll, body, 0)
-
-
-def first_kernel(
-    order, left, right, wave, table,
-    left_rows, right_t, wave_here, table_here, acc, right_here, sems,
+    if unroll:
+        lax.fori_loop(0, (end - begin) // unroll, body, 0)
+
+
+def load_kernel(
+    order, early, left, right, wave, table, left_rows, right_t, wave_here, table_here, acc, right_here, sems
 ):
-    rep, op, blk = lax.axis_index("rep"), lax.axis_index("op"), lax.axis_index("blk")
+    rep, op = lax.axis_index("rep"), lax.axis_index("op")
     rows = left_rows.shape[1] // len(order)
     moves = [(right, right_here), (wave, wave_here), (table, table_here)]
     for g, s in enumerate(order):
@@ -70,48 +72,50 @@
         copy.wait()
     for k in range(right_t.shape[0]):
         right_t[k] = right_here[k].T
-    add_list(table_here, rep, blk, left_rows, right_t, wave_here, acc)
+    blk = lax.axis_index("blk")
+    add_list(table_here, rep, blk, left_rows, right_t, wave_here, acc, 0, early)
 
 
 def split_rows(acc, outs):
     first = 0
     for out in outs:
         tiles, rows, _ = out.shape[-3:]
-        for g in range(out.shape[0] if len(out.shape) == 4 else 1):
-            block = acc[0:tiles, first : first + rows, :].astype(out.dtype)
-            if len(out.shape) == 4:
-                out[g] = block
-            else:
-                out[...] = block
+        for to in [out] if len(out.shape) == 3 else [out.at[g] for g in range(out.shape[0])]:
+            to[...] = acc[0:tiles, first : first + rows, :].astype(out.dtype)
             first += rows
 
 
-def other_kernel(table, left_rows, right_t, wave, wave_pair, *refs):
-    *outs, acc, table_here, sem = refs
+def other_kernel(
+    begin, end, other, table, left_rows, right_t, wave, wave_pair, start, own_acc, *refs
+):
+    del start
+    *outs, acc, other_here, sem = refs
     rep, blk = lax.axis_index("rep"), lax.axis_index("blk")
-    copy = pltpu.make_async_copy(table, table_here, sem)
+    copy = pltpu.make_async_copy(other, other_here, sem)
     copy.start()
     acc[...] = jnp.zeros_like(acc)
+    add_list(table, rep, blk, left_rows, right_t, wave, own_acc, begin, end)
     copy.wait()
-    add_list(table_here, rep, blk, left_rows, right_t, wave, acc)
-    add_list(table_here, 1 - rep, blk, left_rows, right_t, wave_pair, acc)
+    add_list(other_here, rep, blk, left_rows, right_t, wave, acc)
+    add_list(other_here, 1 - rep, blk, left_rows, right_t, wave_pair, acc)
     split_rows(acc, outs)
 
 
-def own_kernel(table, left_rows, right_t, wave_pair, start, later, acc, handed_on, *outs):
+def own_kernel(begin, table, left_rows, right_t, wave, wave_pair, start, later, acc, handed_on, *outs):
     del start, later, handed_on
     rep, blk = lax.axis_index("rep"), lax.axis_index("blk")
+    add_list(table, rep, blk, left_rows, right_t, wave, acc, begin)
     add_list(table, 1 - rep, blk, left_rows, right_t, wave_pair, acc)
     split_rows(acc, outs)
 
 
-def sum_kernel(kept, got, later, out, handed_on):
-    del later, handed_on
+def sum_kernel(kept, got, *refs):
+    out = refs[-1]
     out[...] = (kept[...] + got[...].astype(jnp.float32)).astype(out.dtype)
 
 
-def sums_kernel(kept, got, later, handed_on, *outs):
-    del later, handed_on
+def last_sum_kernel(kept, got, before, *outs):
+    del before
     for g, out in enumerate(outs):
         out[...] = (kept[g] + got[g].astype(jnp.float32)).astype(out.dtype)
 
@@ -137,8 +141,7 @@
     op_count = lax.axis_size("op")
     tiles = 2 * tiles_dev
     rows = row_total // (2 * op_count)
-    half = op_count // 2
-    order = list(range(half, op_count)) + list(range(half - 1, -1, -1))
+    order = [2, 3, 1, 0]
     swap = [(0, 1), (1, 0)]
     f32 = jnp.float32
     shape = jax.ShapeDtypeStruct
@@ -148,8 +151,10 @@
     table_other = lax.ppermute(slot_table, "blk", swap)
     wave_pair = lax.ppermute(wavefunction, "rep", swap)
     acc_shape = shape((tiles + 1, op_count * rows, width), f32)
+    caps = slot_table.shape[-1]
+    early, late = caps // 4, caps // 2
     left_rows, right_t, wave, own_table, acc = call(
-        functools.partial(first_kernel, order),
+        functools.partial(load_kernel, order, early),
         (
             shape((terms, op_count * rows, width), left_env.dtype),
             shape(right_env.shape, right_env.dtype),
@@ -165,13 +170,15 @@
             pltpu.SemaphoreType.DMA((3 + op_count,)),
         ],
     )
-    blocks = (block, (op_count - 2,) + block, block)
-    first, middle, last = call(
-        other_kernel,
-        tuple(shape(b, LINK) for b in blocks),
-        (table_other, left_rows, right_t, wave, wave_pair),
-        [ANY] + [VMEM] * 4,
-        (VMEM,) * 3,
+    blocks = (block,) * (op_count - 2) + ((2,) + block,)
+    operands = (own_table, left_rows, right_t, wave, wave_pair)
+    acc, *sends = call(
+        functools.partial(other_kernel, early, late),
+        (acc_shape,) + tuple(shape(b, LINK) for b in blocks),
+        (table_other, *operands, acc),
+        [ANY, SMEM] + [VMEM] * 5,
+        (VMEM,) * (1 + len(blocks)),
+        input_output_aliases={6: 0},
         scratch_shapes=[
             pltpu.VMEM(acc_shape.shape, f32),
             pltpu.SMEM(slot_table.shape, slot_table.dtype),
@@ -185,42 +192,46 @@
     def to_op(x, s):
         return lax.ppermute(x, "op", [(i, i ^ s) for i in range(op_count)])
 
-    got_first = to_blk(first)
-    _, middle, kept_first, kept_middle, kept_last = call(
-        own_kernel,
-        (acc_shape, shape(middle.shape, LINK)) + tuple(shape(b, f32) for b in blocks),
-        (own_table, left_rows, right_t, wave_pair, acc, middle),
-        [SMEM] + [VMEM] * 4 + [ANY],
-        (VMEM, ANY) + (VMEM,) * 3,
-        input_output_aliases={4: 0, 5: 1},
-        cost_estimate=COSTLY,
-    )
-    got_middle = to_blk(middle)
-    total, last = call(
-        sum_kernel,
-        (shape(block, LINK),) * 2,
-        (kept_first, got_first, last),
+    *far, rest = sends
+    got = [to_blk(x) for x in far]
+    _, rest, *kept, kept_rest = call(
+        functools.partial(own_kernel, late),
+        (acc_shape, shape(blocks[-1], LINK)) + tuple(shape(b, f32) for b in blocks),
+        (*operands, acc, rest),
+        [SMEM] + [VMEM] * 5 + [ANY],
+        (VMEM, ANY) + (VMEM,) * len(blocks),
+        input_output_aliases={5: 0, 6: 1},
+        cost_estimate=COST_K,
+    )
+    got_rest = to_blk(rest)
+    arrived, before = [], ()
+    for g, s in enumerate(order[:-2]):
+        total = call(
+            sum_kernel,
+            shape(block, LINK),
+            (kept[g], got[g], *before),
+            [VMEM] * 2 + [ANY] * len(before),
+            VMEM,
+            cost_estimate=COST_S[g],
+        )
+        arrived.append(to_op(total, s))
+        before = (total,)
+    near, own = call(
+        last_sum_kernel,
+        (shape(block, LINK), shape(block, f32)),
+        (kept_rest, got_rest, *before),
         [VMEM] * 2 + [ANY],
-        (VMEM, ANY),
-        input_output_aliases={2: 1},
-        cost_estimate=COSTLY,
-    )
-    arrived = [to_op(total, order[0])]
-    last, *totals = call(
-        sums_kernel,
-        (shape(block, LINK),) * (op_count - 1),
-        (kept_middle, got_middle, last),
-        [VMEM] * 2 + [ANY],
-        (ANY,) + (VMEM,) * (op_count - 2),
-        input_output_aliases={2: 0},
-    )
-    arrived += [to_op(x, s) for x, s in zip(totals, order[1:])]
+        (VMEM,) * 2,
+        cost_estimate=COST_S[2],
+    )
+    arrived.append(to_op(near, order[-2]))
     return call(
         final_kernel,
         shape((rows, tiles, width), f32),
-        (kept_last, to_blk(last), *arrived),
-        [VMEM] * (op_count + 1),
+        (own, *arrived),
+        [VMEM] * op_count,
         VMEM,
+        cost_estimate=COST_F,
     )
 
 

time: 29.3 us -> 26.6 us (0.908)
  waiting for transfers between devices: 7.74 us -> 4.14 us
  starting transfers between devices: 12.4 us -> 13.9 us
  Pallas kernels: 9.01 us -> 8.33 us
    ppermute x3, waiting for transfers between devices: 3.13 us -> 0.01 us  [to_blk(): return lax.ppermute(x, 'blk', swap)]
    ppermute x3, starting transfers between devices: 6.06 us -> 7.16 us  [to_op(): return lax.ppermute(x, 'op', [(i, i ^ s) for i in range(op_count)])]
    pallas_call x6 -> x7, Pallas kernels: 9.01 us -> 8.33 us  [call(): pl.pallas_call(kernel, out_shape=out_shape, in_specs=ins, out_specs=outs,...]
    ppermute x3, waiting for transfers between devices: 4.61 us -> 4.13 us  [to_op(): return lax.ppermute(x, 'op', [(i, i ^ s) for i in range(op_count)])]
    ppermute x3, starting transfers between devices: 3.37 us -> 3.83 us  [to_blk(): return lax.ppermute(x, 'blk', swap)]
  transfers between devices with their start and end apart: 8 -> 8, of which waited for: 4 -> 3; matrix products, arithmetic and copies ran while one was open for 0% -> 0% of each run, Pallas kernels for 16% -> 15%
where the time goes in v6:
time: 26.6 us; the launch traced here: 26.5 us
  starting transfers between devices  13.9 us (52%)
  Pallas kernels  8.33 us (31%)
  waiting for transfers between devices  4.14 us (16%)
    pallas_call x7, Pallas kernels, call(): pl.pallas_call(kernel, out_shape=out_shape, in_specs=ins, out_specs=outs,...  8.33 us
    ppermute x3, starting transfers between devices, to_op(): return lax.ppermute(x, 'op', [(i, i ^ s) for i in range(op_count)])  7.16 us
    ppermute x3, waiting for transfers between devices, to_op(): return lax.ppermute(x, 'op', [(i, i ^ s) for i in range(op_count)])  4.13 us
    ppermute x3, starting transfers between devices, to_blk(): return lax.ppermute(x, 'blk', swap)  3.83 us
    ppermute x1, starting transfers between devices, at_source(): table_other = lax.ppermute(slot_table, 'blk', swap)  2.49 us
  transfers between devices with their start and end apart: 8, of which 3 were waited for; matrix products, arithmetic and copies ran while one was open for 0% of the time, Pallas kernels for 15%

profile of v6, /device:TPU:0, one launch (start us, length us, event | category | flops | bytes accessed | tf_op | source)
XLA Modules:
  0.0 26.5 jit_solution(14536514830738479603)
XLA Ops:
  0.0 0.5 %collective-permute-start = (bf16[12,128,128]{2,1,0:T(8,128)(2,1)}, bf16[12,128,128]{2,1,0:T(8,128)(2,1)S(1)}, u32[]{:S(2)}, u32[]{:S(2)}) collective-permute-start(bf16[12,128,128]{2,1,0:T(8,128)(2,1)} %wave.1), channel_id=1, source_target_pairs={{0,1},{1,0},{2,3},{3,2},{4,5},{5,4},{6,7},{7,6},{8,9},{9,8},{10,11... | collective-permute-start | bytes 1179656 | tf_op jit(solution)/shard_map/ppermute | solution.py:152
  0.5 2.5 %collective-permute-start.1 = (s32[3,1,1,2,2,64]{5,4,3,2,1,0:T(2,128)}, s32[3,1,1,2,2,64]{5,4,3,2,1,0:T(2,128)S(1)}, u32[]{:S(2)}, u32[]{:S(2)}) collective-permute-start(s32[3,1,1,2,2,64]{5,4,3,2,1,0:T(2,128)} %table.1), channel_id=1, source_target_pairs={{0,2},{2,0},{1,3},{3,1},{4,6},{6,4},{5,7},{7,5},{8,10},{10,8},{9,1... | collective-permute-start | bytes 9224 | tf_op jit(solution)/shard_map/ppermute | solution.py:151
  2.9 2.1 %shard_map.46 = (bf16[32,64,128]{2,1,0:T(8,128)(2,1)S(1)}, bf16[32,128,128]{2,1,0:T(8,128)(2,1)S(1)}, bf16[12,128,128]{2,1,0:T(8,128)(2,1)S(1)}, s32[3,1,1,2,2,64]{5,4,3,2,1,0:T(2,128)S(4)}, f32[25,64,128]{2,1,0:T(8,128)S(1)}) custom-call(bf16[32,128,128]{2,1,0:T(8,128)(2,1)} %left.1, bf16[32,128,128]{2,1,0:T(8,128)(2,1)} %right.1, ...), custom_call_target="tpu_custom_call" | custom-call | tf_op jit(solution)/shard_map/pallas_call | solution.py:133
  5.1 0.0 collective-permute-done.1.other
  5.1 0.0 collective-permute-done.wave_pair
  5.1 3.4 %shard_map.47 = (f32[25,64,128]{2,1,0:T(8,128)S(1)}, bf16[24,16,128]{2,1,0:T(8,128)(2,1)S(1)}, bf16[24,16,128]{2,1,0:T(8,128)(2,1)S(1)}, bf16[2,24,16,128]{3,2,1,0:T(8,128)(2,1)S(1)}) custom-call(s32[3,1,1,2,2,64]{5,4,3,2,1,0:T(2,128)S(1)} %collective-permute-done.1.other, ...), custom_call_target="tpu_custom_call", output_to_operand_aliasing={{0}: (6, {})} | custom-call | tf_op jit(solution)/shard_map/pallas_call | solution.py:133
  8.6 1.7 %collective-permute-start.4 = (bf16[24,16,128]{2,1,0:T(8,128)(2,1)S(1)}, bf16[24,16,128]{2,1,0:T(8,128)(2,1)S(1)}, u32[]{:S(2)}, u32[]{:S(2)}) collective-permute-start(bf16[24,16,128]{2,1,0:T(8,128)(2,1)S(1)} %get-tuple-element.32), channel_id=1, source_target_pairs={{0,2},{2,0},{1,3},{3,1},{4,6},{6,4},{5,7},{7,5},{8,10},{10,8},{9,1... | collective-permute-start | bytes 294920 | tf_op jit(solution)/shard_map/ppermute | solution.py:190
  10.3 0.4 %collective-permute-start.3 = (bf16[24,16,128]{2,1,0:T(8,128)(2,1)S(1)}, bf16[24,16,128]{2,1,0:T(8,128)(2,1)S(1)}, u32[]{:S(2)}, u32[]{:S(2)}) collective-permute-start(bf16[24,16,128]{2,1,0:T(8,128)(2,1)S(1)} %get-tuple-element.30), channel_id=1, source_target_pairs={{0,2},{2,0},{1,3},{3,1},{4,6},{6,4},{5,7},{7,5},{8,10},{10,8},{9,1... | collective-permute-start | bytes 294920 | tf_op jit(solution)/shard_map/ppermute | solution.py:190
  10.7 1.9 %shard_map.48 = (f32[25,64,128]{2,1,0:T(8,128)S(1)}, bf16[2,24,16,128]{3,2,1,0:T(8,128)(2,1)S(1)}, f32[24,16,128]{2,1,0:T(8,128)S(1)}, f32[24,16,128]{2,1,0:T(8,128)S(1)}, f32[2,24,16,128]{3,2,1,0:T(8,128)S(1)}) custom-call(s32[3,1,1,2,2,64]{5,4,3,2,1,0:T(2,128)S(4)} %get-tuple-element.20.table, ...), custom_call_target="tpu_custom_call", output_to_operand_aliasing={{0}: (5, {}), {1}: (6, {})} | custom-call | tf_op jit(solution)/shard_map/pallas_call | solution.py:133
  12.5 1.7 %collective-permute-start.2 = (bf16[2,24,16,128]{3,2,1,0:T(8,128)(2,1)S(1)}, bf16[2,24,16,128]{3,2,1,0:T(8,128)(2,1)S(1)}, u32[]{:S(2)}, u32[]{:S(2)}) collective-permute-start(bf16[2,24,16,128]{3,2,1,0:T(8,128)(2,1)S(1)} %get-tuple-element.28), channel_id=1, source_target_pairs={{0,2},{2,0},{1,3},{3,1},{4,6},{6,4},{5,7},{7,5},{8,10},{10,8},{9,1... | collective-permute-start | bytes 589832 | tf_op jit(solution)/shard_map/ppermute | solution.py:190
  14.3 0.0 collective-permute-done.4.got
  14.3 2.8 %collective-permute-start.5 = (bf16[24,16,128]{2,1,0:T(8,128)(2,1)S(1)}, bf16[24,16,128]{2,1,0:T(8,128)(2,1)S(1)}, u32[]{:S(2)}, u32[]{:S(2)}) collective-permute-start(bf16[24,16,128]{2,1,0:T(8,128)(2,1)S(1)} %shard_map.49.refs_0_), channel_id=1, source_target_pairs={{0,8},{4,12},{8,0},{12,4},{1,9},{5,13},{9,1},{13,5},{2,10},{6,14},... | collective-permute-start | bytes 294920 | tf_op jit(solution)/shard_map/ppermute | solution.py:193
  17.1 0.0 collective-permute-done.3.got
  17.2 2.9 %collective-permute-start.6 = (bf16[24,16,128]{2,1,0:T(8,128)(2,1)S(1)}, bf16[24,16,128]{2,1,0:T(8,128)(2,1)S(1)}, u32[]{:S(2)}, u32[]{:S(2)}) collective-permute-start(bf16[24,16,128]{2,1,0:T(8,128)(2,1)S(1)} %shard_map.50.before), channel_id=1, source_target_pairs={{0,12},{4,8},{8,4},{12,0},{1,13},{5,9},{9,5},{13,1},{2,14},{6,10},... | collective-permute-start | bytes 294920 | tf_op jit(solution)/shard_map/ppermute | solution.py:193
  20.1 0.0 collective-permute-done.2.got
  20.1 1.4 %collective-permute-start.7 = (bf16[24,16,128]{2,1,0:T(8,128)(2,1)S(1)}, bf16[24,16,128]{2,1,0:T(8,128)(2,1)S(1)}, u32[]{:S(2)}, u32[]{:S(2)}) collective-permute-start(bf16[24,16,128]{2,1,0:T(8,128)(2,1)S(1)} %get-tuple-element.34), channel_id=1, source_target_pairs={{0,4},{4,0},{8,12},{12,8},{1,5},{5,1},{9,13},{13,9},{2,6},{6,2},{1... | collective-permute-start | bytes 294920 | tf_op jit(solution)/shard_map/ppermute | solution.py:193
  21.5 2.3 %collective-permute-done.6.rest_1_ = bf16[24,16,128]{2,1,0:T(8,128)(2,1)S(1)} collective-permute-done((bf16[24,16,128]{2,1,0:T(8,128)(2,1)S(1)}, bf16[24,16,128]{2,1,0:T(8,128)(2,1)S(1)}, u32[]{:S(2)}, u32[]{:S(2)}) %collective-permute-start.6) | collective-permute-done | bytes 98336 | tf_op jit(solution)/shard_map/ppermute | solution.py:193
  23.8 0.3 %collective-permute-done.5.rest_0_ = bf16[24,16,128]{2,1,0:T(8,128)(2,1)S(1)} collective-permute-done((bf16[24,16,128]{2,1,0:T(8,128)(2,1)S(1)}, bf16[24,16,128]{2,1,0:T(8,128)(2,1)S(1)}, u32[]{:S(2)}, u32[]{:S(2)}) %collective-permute-start.5) | collective-permute-done | bytes 98336 | tf_op jit(solution)/shard_map/ppermute | solution.py:193
  24.1 1.6 %collective-permute-done.7.rest_2_ = bf16[24,16,128]{2,1,0:T(8,128)(2,1)S(1)} collective-permute-done((bf16[24,16,128]{2,1,0:T(8,128)(2,1)S(1)}, bf16[24,16,128]{2,1,0:T(8,128)(2,1)S(1)}, u32[]{:S(2)}, u32[]{:S(2)}) %collective-permute-start.7) | collective-permute-done | bytes 98336 | tf_op jit(solution)/shard_map/ppermute | solution.py:193
  25.7 0.8 %shard_map.52 = f32[16,24,128]{2,1,0:T(8,128)} custom-call(f32[24,16,128]{2,1,0:T(8,128)S(1)} %get-tuple-element.33.own, bf16[24,16,128]{2,1,0:T(8,128)(2,1)S(1)} %collective-permute-done.5.rest_0_, bf16[24,16,128]{2,1,0:T(8,128)(2,1)S(1)} %collective-permute-done.6.rest_1_, bf16[24,16,128]{2,1,0:T(8,128)(2,1)S(1)} %collective-permute-done.7.rest_2_), custom_call_target="tpu_custom_call" | custom-call | tf_op jit(solution)/shard_map/pallas_call | solution.py:133
  (3 shorter events, 0.1 us)
Async XLA Ops:
  0.0 5.1 %collective-permute-start = (bf16[12,128,128]{2,1,0:T(8,128)(2,1)}, bf16[12,128,128]{2,1,0:T(8,128)(2,1)S(1)}, u32[]{:S(2)}, u32[]{:S(2)}) collective-permute-start(bf16[12,128,128]{2,1,0:T(8,128)(2,1)} %wave.1), channel_id=1, source_target_pairs={{0,1},{1,0},{2,3},{3,2},{4,5},{5,4},{6,7},{7,6},{8,9},{9,8},{10,11... | collective-permute-start | bytes 1179656 | tf_op jit(solution)/shard_map/ppermute | solution.py:152
  0.5 4.6 %collective-permute-start.1 = (s32[3,1,1,2,2,64]{5,4,3,2,1,0:T(2,128)}, s32[3,1,1,2,2,64]{5,4,3,2,1,0:T(2,128)S(1)}, u32[]{:S(2)}, u32[]{:S(2)}) collective-permute-start(s32[3,1,1,2,2,64]{5,4,3,2,1,0:T(2,128)} %table.1), channel_id=1, source_target_pairs={{0,2},{2,0},{1,3},{3,1},{4,6},{6,4},{5,7},{7,5},{8,10},{10,8},{9,1... | collective-permute-start | bytes 9224 | tf_op jit(solution)/shard_map/ppermute | solution.py:151
  8.6 5.7 %collective-permute-start.4 = (bf16[24,16,128]{2,1,0:T(8,128)(2,1)S(1)}, bf16[24,16,128]{2,1,0:T(8,128)(2,1)S(1)}, u32[]{:S(2)}, u32[]{:S(2)}) collective-permute-start(bf16[24,16,128]{2,1,0:T(8,128)(2,1)S(1)} %get-tuple-element.32), channel_id=1, source_target_pairs={{0,2},{2,0},{1,3},{3,1},{4,6},{6,4},{5,7},{7,5},{8,10},{10,8},{9,1... | collective-permute-start | bytes 294920 | tf_op jit(solution)/shard_map/ppermute | solution.py:190
  10.3 6.8 %collective-permute-start.3 = (bf16[24,16,128]{2,1,0:T(8,128)(2,1)S(1)}, bf16[24,16,128]{2,1,0:T(8,128)(2,1)S(1)}, u32[]{:S(2)}, u32[]{:S(2)}) collective-permute-start(bf16[24,16,128]{2,1,0:T(8,128)(2,1)S(1)} %get-tuple-element.30), channel_id=1, source_target_pairs={{0,2},{2,0},{1,3},{3,1},{4,6},{6,4},{5,7},{7,5},{8,10},{10,8},{9,1... | collective-permute-start | bytes 294920 | tf_op jit(solution)/shard_map/ppermute | solution.py:190
  12.5 7.5 %collective-permute-start.2 = (bf16[2,24,16,128]{3,2,1,0:T(8,128)(2,1)S(1)}, bf16[2,24,16,128]{3,2,1,0:T(8,128)(2,1)S(1)}, u32[]{:S(2)}, u32[]{:S(2)}) collective-permute-start(bf16[2,24,16,128]{3,2,1,0:T(8,128)(2,1)S(1)} %get-tuple-element.28), channel_id=1, source_target_pairs={{0,2},{2,0},{1,3},{3,1},{4,6},{6,4},{5,7},{7,5},{8,10},{10,8},{9,1... | collective-permute-start | bytes 589832 | tf_op jit(solution)/shard_map/ppermute | solution.py:190
  14.3 9.8 %collective-permute-start.5 = (bf16[24,16,128]{2,1,0:T(8,128)(2,1)S(1)}, bf16[24,16,128]{2,1,0:T(8,128)(2,1)S(1)}, u32[]{:S(2)}, u32[]{:S(2)}) collective-permute-start(bf16[24,16,128]{2,1,0:T(8,128)(2,1)S(1)} %shard_map.49.refs_0_), channel_id=1, source_target_pairs={{0,8},{4,12},{8,0},{12,4},{1,9},{5,13},{9,1},{13,5},{2,10},{6,14},... | collective-permute-start | bytes 294920 | tf_op jit(solution)/shard_map/ppermute | solution.py:193
  17.2 6.6 %collective-permute-start.6 = (bf16[24,16,128]{2,1,0:T(8,128)(2,1)S(1)}, bf16[24,16,128]{2,1,0:T(8,128)(2,1)S(1)}, u32[]{:S(2)}, u32[]{:S(2)}) collective-permute-start(bf16[24,16,128]{2,1,0:T(8,128)(2,1)S(1)} %shard_map.50.before), channel_id=1, source_target_pairs={{0,12},{4,8},{8,4},{12,0},{1,13},{5,9},{9,5},{13,1},{2,14},{6,10},... | collective-permute-start | bytes 294920 | tf_op jit(solution)/shard_map/ppermute | solution.py:193
  20.1 5.5 %collective-permute-start.7 = (bf16[24,16,128]{2,1,0:T(8,128)(2,1)S(1)}, bf16[24,16,128]{2,1,0:T(8,128)(2,1)S(1)}, u32[]{:S(2)}, u32[]{:S(2)}) collective-permute-start(bf16[24,16,128]{2,1,0:T(8,128)(2,1)S(1)} %get-tuple-element.34), channel_id=1, source_target_pairs={{0,4},{4,0},{8,12},{12,8},{1,5},{5,1},{9,13},{13,9},{2,6},{6,2},{1... | collective-permute-start | bytes 294920 | tf_op jit(solution)/shard_map/ppermute | solution.py:193

commit v7 on v6

--- a/solution.py
+++ b/solution.py
@@ -11,9 +11,7 @@
 SMEM = pl.BlockSpec(memory_space=pltpu.SMEM)
 ANY = pl.BlockSpec(memory_space=pl.ANY)
 LINK = jnp.bfloat16
-COST_K = None
-COST_S = (pl.CostEstimate(flops=int(10.0e9), bytes_accessed=int(10.0e6), transcendentals=0), pl.CostEstimate(flops=int(10.0e9), bytes_accessed=int(10.0e6), transcendentals=0), None)
-COST_F = None
+COSTLY = pl.CostEstimate(flops=10**10, bytes_accessed=10**7, transcendentals=0)
 
 
 def params():
@@ -25,7 +23,7 @@
 
 
 def unroll_of(caps, most):
-    return next((u for u in (64, 32, 16, 8, 4, 2, 1) if u <= min(most, caps) and caps % u == 0), 0)
+    return next((u for u in range(min(most, caps), 0, -1) if caps % u == 0), 0)
 
 
 def add_list(table, rep, src, left, right_t, wave, acc, begin=0, end=None):
@@ -56,24 +54,31 @@
 
 
 def load_kernel(
-    order, early, left, right, wave, table, left_rows, right_t, wave_here, table_here, acc, right_here, sems
+    order, left, right, wave, table,
+    left_rows, right_t, wave_here, table_here, acc, right_here, sems,
 ):
     rep, op = lax.axis_index("rep"), lax.axis_index("op")
     rows = left_rows.shape[1] // len(order)
-    moves = [(right, right_here), (wave, wave_here), (table, table_here)]
+    count = right_t.shape[0]
+    part = next(p for p in (8, 4, 2, 1) if count % p == 0)
+    moves = [(table, table_here)]
+    for k in range(0, count, part):
+        moves.append((right.at[pl.ds(k, part)], right_here.at[pl.ds(k, part)]))
     for g, s in enumerate(order):
         first = pl.multiple_of((jnp.bitwise_xor(op, s) * 2 + rep) * rows, rows)
         moves.append((left.at[:, pl.ds(first, rows), :], left_rows.at[:, pl.ds(g * rows, rows), :]))
+    moves.append((wave, wave_here))
     copies = [pltpu.make_async_copy(a, b, sems.at[i]) for i, (a, b) in enumerate(moves)]
     for copy in copies:
         copy.start()
     acc[...] = jnp.zeros_like(acc)
-    for copy in copies:
+    copies[0].wait()
+    for k in range(count):
+        if k % part == 0:
+            copies[1 + k // part].wait()
+        right_t[k] = right_here[k].T
+    for copy in copies[1 + count // part :]:
         copy.wait()
-    for k in range(right_t.shape[0]):
-        right_t[k] = right_here[k].T
-    blk = lax.axis_index("blk")
-    add_list(table_here, rep, blk, left_rows, right_t, wave_here, acc, 0, early)
 
 
 def split_rows(acc, outs):
@@ -86,38 +91,46 @@
 
 
 def other_kernel(
-    begin, end, other, table, left_rows, right_t, wave, wave_pair, start, own_acc, *refs
+    early, other, table, left_rows, right_t, wave, start, own_acc, other_here, acc, sem
 ):
     del start
-    *outs, acc, other_here, sem = refs
     rep, blk = lax.axis_index("rep"), lax.axis_index("blk")
     copy = pltpu.make_async_copy(other, other_here, sem)
     copy.start()
     acc[...] = jnp.zeros_like(acc)
-    add_list(table, rep, blk, left_rows, right_t, wave, own_acc, begin, end)
+    add_list(table, rep, blk, left_rows, right_t, wave, own_acc, 0, early)
     copy.wait()
     add_list(other_here, rep, blk, left_rows, right_t, wave, acc)
-    add_list(other_here, 1 - rep, blk, left_rows, right_t, wave_pair, acc)
-    split_rows(acc, outs)
-
-
-def own_kernel(begin, table, left_rows, right_t, wave, wave_pair, start, later, acc, handed_on, *outs):
-    del start, later, handed_on
+
+
+def pair_kernel(table, left_rows, right_t, wave_pair, start, acc, *outs):
+    del start
     rep, blk = lax.axis_index("rep"), lax.axis_index("blk")
-    add_list(table, rep, blk, left_rows, right_t, wave, acc, begin)
     add_list(table, 1 - rep, blk, left_rows, right_t, wave_pair, acc)
     split_rows(acc, outs)
 
 
-def sum_kernel(kept, got, *refs):
-    out = refs[-1]
-    out[...] = (kept[...] + got[...].astype(jnp.float32)).astype(out.dtype)
-
-
-def last_sum_kernel(kept, got, before, *outs):
+def own_kernel(early, table, left_rows, right_t, wave, wave_pair, start, acc):
+    del start
+    rep, blk = lax.axis_index("rep"), lax.axis_index("blk")
+    add_list(table, rep, blk, left_rows, right_t, wave, acc, early)
+    add_list(table, 1 - rep, blk, left_rows, right_t, wave_pair, acc)
+
+
+def add_block(acc, block, got, out):
+    tiles, rows, _ = out.shape
+    kept = acc[0:tiles, block * rows : (block + 1) * rows, :]
+    out[...] = (kept + got[...].astype(jnp.float32)).astype(out.dtype)
+
+
+def sum_kernel(block, acc, got, *refs):
+    add_block(acc, block, got, refs[-1])
+
+
+def last_sum_kernel(first, acc, got, before, *outs):
     del before
     for g, out in enumerate(outs):
-        out[...] = (kept[g] + got[g].astype(jnp.float32)).astype(out.dtype)
+        add_block(acc, first + g, got.at[g], out)
 
 
 def final_kernel(own, *rest):
@@ -141,22 +154,24 @@
     op_count = lax.axis_size("op")
     tiles = 2 * tiles_dev
     rows = row_total // (2 * op_count)
-    order = [2, 3, 1, 0]
+    order = [*range(op_count // 2, op_count), *range(op_count // 2 - 1, -1, -1)]
     swap = [(0, 1), (1, 0)]
     f32 = jnp.float32
     shape = jax.ShapeDtypeStruct
     table_spec = pltpu.SMEM(slot_table.shape, slot_table.dtype)
     block = (tiles, rows, width)
 
-    table_other = lax.ppermute(slot_table, "blk", swap)
+    across = [(0, 3), (1, 2), (2, 1), (3, 0)]
+    table_other = lax.ppermute(slot_table, ("blk", "rep"), across)
     wave_pair = lax.ppermute(wavefunction, "rep", swap)
     acc_shape = shape((tiles + 1, op_count * rows, width), f32)
     caps = slot_table.shape[-1]
-    early, late = caps // 4, caps // 2
+    early = caps // 8
+    left_shape = shape((terms, op_count * rows, width), left_env.dtype)
     left_rows, right_t, wave, own_table, acc = call(
-        functools.partial(load_kernel, order, early),
+        functools.partial(load_kernel, order),
         (
-            shape((terms, op_count * rows, width), left_env.dtype),
+            left_shape,
             shape(right_env.shape, right_env.dtype),
             shape(wavefunction.shape, wavefunction.dtype),
             table_spec,
@@ -167,23 +182,27 @@
         (VMEM, VMEM, VMEM, SMEM, VMEM),
         scratch_shapes=[
             pltpu.VMEM(right_env.shape, right_env.dtype),
-            pltpu.SemaphoreType.DMA((3 + op_count,)),
+            pltpu.SemaphoreType.DMA((2 + op_count + terms,)),
         ],
     )
     blocks = (block,) * (op_count - 2) + ((2,) + block,)
-    operands = (own_table, left_rows, right_t, wave, wave_pair)
-    acc, *sends = call(
-        functools.partial(other_kernel, early, late),
+    acc, other_table, acc_other = call(
+        functools.partial(other_kernel, early),
+        (acc_shape, table_spec, acc_shape),
+        (table_other, own_table, left_rows, right_t, wave, acc),
+        [ANY, SMEM] + [VMEM] * 4,
+        (VMEM, SMEM, VMEM),
+        input_output_aliases={5: 0},
+        scratch_shapes=[pltpu.SemaphoreType.DMA],
+        cost_estimate=COSTLY,
+    )
+    _, *sends = call(
+        pair_kernel,
         (acc_shape,) + tuple(shape(b, LINK) for b in blocks),
-        (table_other, *operands, acc),
-        [ANY, SMEM] + [VMEM] * 5,
+        (other_table, left_rows, right_t, wave_pair, acc_other),
+        [SMEM] + [VMEM] * 4,
         (VMEM,) * (1 + len(blocks)),
-        input_output_aliases={6: 0},
-        scratch_shapes=[
-            pltpu.VMEM(acc_shape.shape, f32),
-            pltpu.SMEM(slot_table.shape, slot_table.dtype),
-            pltpu.SemaphoreType.DMA,
-        ],
+        input_output_aliases={4: 0},
     )
 
     def to_blk(x):
@@ -194,35 +213,33 @@
 
     *far, rest = sends
     got = [to_blk(x) for x in far]
-    _, rest, *kept, kept_rest = call(
-        functools.partial(own_kernel, late),
-        (acc_shape, shape(blocks[-1], LINK)) + tuple(shape(b, f32) for b in blocks),
-        (*operands, acc, rest),
-        [SMEM] + [VMEM] * 5 + [ANY],
-        (VMEM, ANY) + (VMEM,) * len(blocks),
-        input_output_aliases={5: 0, 6: 1},
-        cost_estimate=COST_K,
+    acc = call(
+        functools.partial(own_kernel, early),
+        acc_shape,
+        (own_table, left_rows, right_t, wave, wave_pair, acc),
+        [SMEM] + [VMEM] * 5,
+        VMEM,
+        input_output_aliases={5: 0},
     )
     got_rest = to_blk(rest)
     arrived, before = [], ()
     for g, s in enumerate(order[:-2]):
         total = call(
-            sum_kernel,
+            functools.partial(sum_kernel, g),
             shape(block, LINK),
-            (kept[g], got[g], *before),
+            (acc, got[g], *before),
             [VMEM] * 2 + [ANY] * len(before),
             VMEM,
-            cost_estimate=COST_S[g],
+            cost_estimate=COSTLY,
         )
         arrived.append(to_op(total, s))
         before = (total,)
     near, own = call(
-        last_sum_kernel,
+        functools.partial(last_sum_kernel, op_count - 2),
         (shape(block, LINK), shape(block, f32)),
-        (kept_rest, got_rest, *before),
+        (acc, got_rest, *before),
         [VMEM] * 2 + [ANY],
         (VMEM,) * 2,
-        cost_estimate=COST_S[2],
     )
     arrived.append(to_op(near, order[-2]))
     return call(
@@ -231,7 +248,6 @@
         (own, *arrived),
         [VMEM] * op_count,
         VMEM,
-        cost_estimate=COST_F,
     )
 
 

time: 26.6 us -> 26.4 us (level)
  starting transfers between devices: 13.9 us -> 13.4 us
  waiting for transfers between devices: 4.14 us -> 4.43 us
    ppermute x3, starting transfers between devices: 3.83 us -> 3.43 us  [to_blk(): return lax.ppermute(x, 'blk', swap)]
    ppermute x3, waiting for transfers between devices: 4.13 us -> 4.42 us  [to_op(): return lax.ppermute(x, 'op', [(i, i ^ s) for i in range(op_count)])]
    pallas_call x7 -> x8, Pallas kernels: 8.33 us -> 8.38 us  [call(): pl.pallas_call(kernel, out_shape=out_shape, in_specs=ins, out_specs=outs,...]
  transfers between devices with their start and end apart: 8 -> 8, of which waited for: 3 -> 3; matrix products, arithmetic and copies ran while one was open for 0% -> 0% of each run, Pallas kernels for 15% -> 24%
where the time goes in v7:
time: 26.4 us; the launch traced here: 26.3 us
  starting transfers between devices  13.4 us (51%)
  Pallas kernels  8.38 us (32%)
  waiting for transfers between devices  4.43 us (17%)
    pallas_call x8, Pallas kernels, call(): pl.pallas_call(kernel, out_shape=out_shape, in_specs=ins, out_specs=outs,...  8.38 us
    ppermute x3, starting transfers between devices, to_op(): return lax.ppermute(x, 'op', [(i, i ^ s) for i in range(op_count)])  6.91 us
    ppermute x3, waiting for transfers between devices, to_op(): return lax.ppermute(x, 'op', [(i, i ^ s) for i in range(op_count)])  4.42 us
    ppermute x3, starting transfers between devices, to_blk(): return lax.ppermute(x, 'blk', swap)  3.43 us
    ppermute x1, starting transfers between devices, at_source(): table_other = lax.ppermute(slot_table, ('blk', 'rep'), across)  2.38 us
    ppermute x1, starting transfers between devices, at_source(): wave_pair = lax.ppermute(wavefunction, 'rep', swap)  0.68 us
  transfers between devices with their start and end apart: 8, of which 3 were waited for; matrix products, arithmetic and copies ran while one was open for 0% of the time, Pallas kernels for 24%

profile of v7, /device:TPU:0, one launch (start us, length us, event | category | flops | bytes accessed | tf_op | source)
XLA Modules:
  0.0 26.3 jit_solution(13873664121679253981)
XLA Ops:
  0.0 2.4 %collective-permute-start.1 = (s32[3,1,1,2,2,64]{5,4,3,2,1,0:T(2,128)}, s32[3,1,1,2,2,64]{5,4,3,2,1,0:T(2,128)S(1)}, u32[]{:S(2)}, u32[]{:S(2)}) collective-permute-start(s32[3,1,1,2,2,64]{5,4,3,2,1,0:T(2,128)} %table.1), channel_id=1, source_target_pairs={{0,3},{1,2},{2,1},{3,0},{4,7},{5,6},{6,5},{7,4},{8,11},{9,10},{10,... | collective-permute-start | bytes 9224 | tf_op jit(solution)/shard_map/ppermute | solution.py:165
  2.4 0.7 %collective-permute-start = (bf16[12,128,128]{2,1,0:T(8,128)(2,1)}, bf16[12,128,128]{2,1,0:T(8,128)(2,1)S(1)}, u32[]{:S(2)}, u32[]{:S(2)}) collective-permute-start(bf16[12,128,128]{2,1,0:T(8,128)(2,1)} %wave.1), channel_id=1, source_target_pairs={{0,1},{1,0},{2,3},{3,2},{4,5},{5,4},{6,7},{7,6},{8,9},{9,8},{10,11... | collective-permute-start | bytes 1179656 | tf_op jit(solution)/shard_map/ppermute | solution.py:166
  3.1 1.8 %shard_map.46 = (bf16[32,64,128]{2,1,0:T(8,128)(2,1)S(1)}, bf16[32,128,128]{2,1,0:T(8,128)(2,1)S(1)}, bf16[12,128,128]{2,1,0:T(8,128)(2,1)S(1)}, s32[3,1,1,2,2,64]{5,4,3,2,1,0:T(2,128)S(4)}, f32[25,64,128]{2,1,0:T(8,128)S(1)}) custom-call(bf16[32,128,128]{2,1,0:T(8,128)(2,1)} %left.1, bf16[32,128,128]{2,1,0:T(8,128)(2,1)} %right.1, ...), custom_call_target="tpu_custom_call" | custom-call | tf_op jit(solution)/shard_map/pallas_call | solution.py:146
  4.9 0.0 collective-permute-done.1.other
  4.9 2.0 %shard_map.47 = (f32[25,64,128]{2,1,0:T(8,128)S(1)}, s32[3,1,1,2,2,64]{5,4,3,2,1,0:T(2,128)S(4)}, f32[25,64,128]{2,1,0:T(8,128)S(1)}) custom-call(s32[3,1,1,2,2,64]{5,4,3,2,1,0:T(2,128)S(1)} %collective-permute-done.1.other, s32[3,1,1,2,2,64]{5,4,3,2,1,0:T(2,128)S(4)} %get-tuple-element.18.table, ...), custom_call_target="tpu_custom_call", output_to_operand_aliasing={{0}: (5, {})} | custom-call | flops 10000000000 | bytes 10000000 | tf_op jit(solution)/shard_map/pallas_call | solution.py:146
  6.9 0.0 collective-permute-done.wave_pair
  6.9 1.3 %shard_map.49 = (f32[25,64,128]{2,1,0:T(8,128)S(1)}, bf16[24,16,128]{2,1,0:T(8,128)(2,1)S(1)}, bf16[24,16,128]{2,1,0:T(8,128)(2,1)S(1)}, bf16[2,24,16,128]{3,2,1,0:T(8,128)(2,1)S(1)}) custom-call(s32[3,1,1,2,2,64]{5,4,3,2,1,0:T(2,128)S(4)} %get-tuple-element.24.table, ...), custom_call_target="tpu_custom_call", output_to_operand_aliasing={{0}: (4, {})} | custom-call | tf_op jit(solution)/shard_map/pallas_call | solution.py:146
  8.3 1.4 %collective-permute-start.4 = (bf16[24,16,128]{2,1,0:T(8,128)(2,1)S(1)}, bf16[24,16,128]{2,1,0:T(8,128)(2,1)S(1)}, u32[]{:S(2)}, u32[]{:S(2)}) collective-permute-start(bf16[24,16,128]{2,1,0:T(8,128)(2,1)S(1)} %get-tuple-element.28), channel_id=1, source_target_pairs={{0,2},{2,0},{1,3},{3,1},{4,6},{6,4},{5,7},{7,5},{8,10},{10,8},{9,1... | collective-permute-start | bytes 294920 | tf_op jit(solution)/shard_map/ppermute | solution.py:209
  9.7 0.7 %collective-permute-start.3 = (bf16[24,16,128]{2,1,0:T(8,128)(2,1)S(1)}, bf16[24,16,128]{2,1,0:T(8,128)(2,1)S(1)}, u32[]{:S(2)}, u32[]{:S(2)}) collective-permute-start(bf16[24,16,128]{2,1,0:T(8,128)(2,1)S(1)} %get-tuple-element.27), channel_id=1, source_target_pairs={{0,2},{2,0},{1,3},{3,1},{4,6},{6,4},{5,7},{7,5},{8,10},{10,8},{9,1... | collective-permute-start | bytes 294920 | tf_op jit(solution)/shard_map/ppermute | solution.py:209
  10.4 1.3 %collective-permute-start.2 = (bf16[2,24,16,128]{3,2,1,0:T(8,128)(2,1)S(1)}, bf16[2,24,16,128]{3,2,1,0:T(8,128)(2,1)S(1)}, u32[]{:S(2)}, u32[]{:S(2)}) collective-permute-start(bf16[2,24,16,128]{3,2,1,0:T(8,128)(2,1)S(1)} %get-tuple-element.26), channel_id=1, source_target_pairs={{0,2},{2,0},{1,3},{3,1},{4,6},{6,4},{5,7},{7,5},{8,10},{10,8},{9,1... | collective-permute-start | bytes 589832 | tf_op jit(solution)/shard_map/ppermute | solution.py:209
  11.7 2.3 %shard_map.48.acc = f32[25,64,128]{2,1,0:T(8,128)S(1)} custom-call(s32[3,1,1,2,2,64]{5,4,3,2,1,0:T(2,128)S(4)} %get-tuple-element.18.table, bf16[32,64,128]{2,1,0:T(8,128)(2,1)S(1)} %get-tuple-element.19.left_rows, bf16[32,128,128]{2,1,0:T(8,128)(2,1)S(1)} %get-tuple-element.20.right_t, ...), custom_call_target="tpu_custom_call", output_to_operand_aliasing={{}: (5, {})} | custom-call | tf_op jit(solution)/shard_map/pallas_call | solution.py:146
  14.0 0.0 collective-permute-done.4.got
  14.0 2.6 %collective-permute-start.5 = (bf16[24,16,128]{2,1,0:T(8,128)(2,1)S(1)}, bf16[24,16,128]{2,1,0:T(8,128)(2,1)S(1)}, u32[]{:S(2)}, u32[]{:S(2)}) collective-permute-start(bf16[24,16,128]{2,1,0:T(8,128)(2,1)S(1)} %shard_map.50.refs_0_), channel_id=1, source_target_pairs={{0,8},{4,12},{8,0},{12,4},{1,9},{5,13},{9,1},{13,5},{2,10},{6,14},... | collective-permute-start | bytes 294920 | tf_op jit(solution)/shard_map/ppermute | solution.py:212
  16.7 0.0 collective-permute-done.3.got
  16.7 3.1 %collective-permute-start.6 = (bf16[24,16,128]{2,1,0:T(8,128)(2,1)S(1)}, bf16[24,16,128]{2,1,0:T(8,128)(2,1)S(1)}, u32[]{:S(2)}, u32[]{:S(2)}) collective-permute-start(bf16[24,16,128]{2,1,0:T(8,128)(2,1)S(1)} %shard_map.51.before), channel_id=1, source_target_pairs={{0,12},{4,8},{8,4},{12,0},{1,13},{5,9},{9,5},{13,1},{2,14},{6,10},... | collective-permute-start | bytes 294920 | tf_op jit(solution)/shard_map/ppermute | solution.py:212
  19.8 0.0 collective-permute-done.2.got
  19.8 1.2 %collective-permute-start.7 = (bf16[24,16,128]{2,1,0:T(8,128)(2,1)S(1)}, bf16[24,16,128]{2,1,0:T(8,128)(2,1)S(1)}, u32[]{:S(2)}, u32[]{:S(2)}) collective-permute-start(bf16[24,16,128]{2,1,0:T(8,128)(2,1)S(1)} %get-tuple-element.30), channel_id=1, source_target_pairs={{0,4},{4,0},{8,12},{12,8},{1,5},{5,1},{9,13},{13,9},{2,6},{6,2},{1... | collective-permute-start | bytes 294920 | tf_op jit(solution)/shard_map/ppermute | solution.py:212
  21.0 2.2 %collective-permute-done.6.rest_1_ = bf16[24,16,128]{2,1,0:T(8,128)(2,1)S(1)} collective-permute-done((bf16[24,16,128]{2,1,0:T(8,128)(2,1)S(1)}, bf16[24,16,128]{2,1,0:T(8,128)(2,1)S(1)}, u32[]{:S(2)}, u32[]{:S(2)}) %collective-permute-start.6) | collective-permute-done | bytes 98336 | tf_op jit(solution)/shard_map/ppermute | solution.py:212
  23.2 0.7 %collective-permute-done.5.rest_0_ = bf16[24,16,128]{2,1,0:T(8,128)(2,1)S(1)} collective-permute-done((bf16[24,16,128]{2,1,0:T(8,128)(2,1)S(1)}, bf16[24,16,128]{2,1,0:T(8,128)(2,1)S(1)}, u32[]{:S(2)}, u32[]{:S(2)}) %collective-permute-start.5) | collective-permute-done | bytes 98336 | tf_op jit(solution)/shard_map/ppermute | solution.py:212
  23.9 1.6 %collective-permute-done.7.rest_2_ = bf16[24,16,128]{2,1,0:T(8,128)(2,1)S(1)} collective-permute-done((bf16[24,16,128]{2,1,0:T(8,128)(2,1)S(1)}, bf16[24,16,128]{2,1,0:T(8,128)(2,1)S(1)}, u32[]{:S(2)}, u32[]{:S(2)}) %collective-permute-start.7) | collective-permute-done | bytes 98336 | tf_op jit(solution)/shard_map/ppermute | solution.py:212
  25.5 0.8 %shard_map.53 = f32[16,24,128]{2,1,0:T(8,128)} custom-call(f32[24,16,128]{2,1,0:T(8,128)S(1)} %get-tuple-element.29.own, bf16[24,16,128]{2,1,0:T(8,128)(2,1)S(1)} %collective-permute-done.5.rest_0_, bf16[24,16,128]{2,1,0:T(8,128)(2,1)S(1)} %collective-permute-done.6.rest_1_, bf16[24,16,128]{2,1,0:T(8,128)(2,1)S(1)} %collective-permute-done.7.rest_2_), custom_call_target="tpu_custom_call" | custom-call | tf_op jit(solution)/shard_map/pallas_call | solution.py:146
  (3 shorter events, 0.1 us)
Async XLA Ops:
  0.0 4.9 %collective-permute-start.1 = (s32[3,1,1,2,2,64]{5,4,3,2,1,0:T(2,128)}, s32[3,1,1,2,2,64]{5,4,3,2,1,0:T(2,128)S(1)}, u32[]{:S(2)}, u32[]{:S(2)}) collective-permute-start(s32[3,1,1,2,2,64]{5,4,3,2,1,0:T(2,128)} %table.1), channel_id=1, source_target_pairs={{0,3},{1,2},{2,1},{3,0},{4,7},{5,6},{6,5},{7,4},{8,11},{9,10},{10,... | collective-permute-start | bytes 9224 | tf_op jit(solution)/shard_map/ppermute | solution.py:165
  2.4 4.5 %collective-permute-start = (bf16[12,128,128]{2,1,0:T(8,128)(2,1)}, bf16[12,128,128]{2,1,0:T(8,128)(2,1)S(1)}, u32[]{:S(2)}, u32[]{:S(2)}) collective-permute-start(bf16[12,128,128]{2,1,0:T(8,128)(2,1)} %wave.1), channel_id=1, source_target_pairs={{0,1},{1,0},{2,3},{3,2},{4,5},{5,4},{6,7},{7,6},{8,9},{9,8},{10,11... | collective-permute-start | bytes 1179656 | tf_op jit(solution)/shard_map/ppermute | solution.py:166
  8.3 5.7 %collective-permute-start.4 = (bf16[24,16,128]{2,1,0:T(8,128)(2,1)S(1)}, bf16[24,16,128]{2,1,0:T(8,128)(2,1)S(1)}, u32[]{:S(2)}, u32[]{:S(2)}) collective-permute-start(bf16[24,16,128]{2,1,0:T(8,128)(2,1)S(1)} %get-tuple-element.28), channel_id=1, source_target_pairs={{0,2},{2,0},{1,3},{3,1},{4,6},{6,4},{5,7},{7,5},{8,10},{10,8},{9,1... | collective-permute-start | bytes 294920 | tf_op jit(solution)/shard_map/ppermute | solution.py:209
  9.7 7.0 %collective-permute-start.3 = (bf16[24,16,128]{2,1,0:T(8,128)(2,1)S(1)}, bf16[24,16,128]{2,1,0:T(8,128)(2,1)S(1)}, u32[]{:S(2)}, u32[]{:S(2)}) collective-permute-start(bf16[24,16,128]{2,1,0:T(8,128)(2,1)S(1)} %get-tuple-element.27), channel_id=1, source_target_pairs={{0,2},{2,0},{1,3},{3,1},{4,6},{6,4},{5,7},{7,5},{8,10},{10,8},{9,1... | collective-permute-start | bytes 294920 | tf_op jit(solution)/shard_map/ppermute | solution.py:209
  10.4 9.4 %collective-permute-start.2 = (bf16[2,24,16,128]{3,2,1,0:T(8,128)(2,1)S(1)}, bf16[2,24,16,128]{3,2,1,0:T(8,128)(2,1)S(1)}, u32[]{:S(2)}, u32[]{:S(2)}) collective-permute-start(bf16[2,24,16,128]{3,2,1,0:T(8,128)(2,1)S(1)} %get-tuple-element.26), channel_id=1, source_target_pairs={{0,2},{2,0},{1,3},{3,1},{4,6},{6,4},{5,7},{7,5},{8,10},{10,8},{9,1... | collective-permute-start | bytes 589832 | tf_op jit(solution)/shard_map/ppermute | solution.py:209
  14.0 9.9 %collective-permute-start.5 = (bf16[24,16,128]{2,1,0:T(8,128)(2,1)S(1)}, bf16[24,16,128]{2,1,0:T(8,128)(2,1)S(1)}, u32[]{:S(2)}, u32[]{:S(2)}) collective-permute-start(bf16[24,16,128]{2,1,0:T(8,128)(2,1)S(1)} %shard_map.50.refs_0_), channel_id=1, source_target_pairs={{0,8},{4,12},{8,0},{12,4},{1,9},{5,13},{9,1},{13,5},{2,10},{6,14},... | collective-permute-start | bytes 294920 | tf_op jit(solution)/shard_map/ppermute | solution.py:212
  16.7 6.5 %collective-permute-start.6 = (bf16[24,16,128]{2,1,0:T(8,128)(2,1)S(1)}, bf16[24,16,128]{2,1,0:T(8,128)(2,1)S(1)}, u32[]{:S(2)}, u32[]{:S(2)}) collective-permute-start(bf16[24,16,128]{2,1,0:T(8,128)(2,1)S(1)} %shard_map.51.before), channel_id=1, source_target_pairs={{0,12},{4,8},{8,4},{12,0},{1,13},{5,9},{9,5},{13,1},{2,14},{6,10},... | collective-permute-start | bytes 294920 | tf_op jit(solution)/shard_map/ppermute | solution.py:212
  19.8 5.6 %collective-permute-start.7 = (bf16[24,16,128]{2,1,0:T(8,128)(2,1)S(1)}, bf16[24,16,128]{2,1,0:T(8,128)(2,1)S(1)}, u32[]{:S(2)}, u32[]{:S(2)}) collective-permute-start(bf16[24,16,128]{2,1,0:T(8,128)(2,1)S(1)} %get-tuple-element.30), channel_id=1, source_target_pairs={{0,4},{4,0},{8,12},{12,8},{1,5},{5,1},{9,13},{13,9},{2,6},{6,2},{1... | collective-permute-start | bytes 294920 | tf_op jit(solution)/shard_map/ppermute | solution.py:212

commit v8 on v7

--- a/solution.py
+++ b/solution.py
@@ -55,7 +55,7 @@
 
 def load_kernel(
     order, left, right, wave, table,
-    left_rows, right_t, wave_here, table_here, acc, right_here, sems,
+    left_rows, right_t, wave_here, table_here, right_here, sems,
 ):
     rep, op = lax.axis_index("rep"), lax.axis_index("op")
     rows = left_rows.shape[1] // len(order)
@@ -71,7 +71,6 @@
     copies = [pltpu.make_async_copy(a, b, sems.at[i]) for i, (a, b) in enumerate(moves)]
     for copy in copies:
         copy.start()
-    acc[...] = jnp.zeros_like(acc)
     copies[0].wait()
     for k in range(count):
         if k % part == 0:
@@ -91,27 +90,28 @@
 
 
 def other_kernel(
-    early, other, table, left_rows, right_t, wave, start, own_acc, other_here, acc, sem
+    early, other, table, left_rows, right_t, wave, own_acc, other_here, acc, sem
 ):
-    del start
     rep, blk = lax.axis_index("rep"), lax.axis_index("blk")
     copy = pltpu.make_async_copy(other, other_here, sem)
     copy.start()
+    own_acc[...] = jnp.zeros_like(own_acc)
     acc[...] = jnp.zeros_like(acc)
     add_list(table, rep, blk, left_rows, right_t, wave, own_acc, 0, early)
     copy.wait()
     add_list(other_here, rep, blk, left_rows, right_t, wave, acc)
 
 
-def pair_kernel(table, left_rows, right_t, wave_pair, start, acc, *outs):
-    del start
+def pair_kernel(table, left_rows, right_t, wave_pair, start, *refs):
+    *outs, acc = refs
+    acc[...] = start[...]
     rep, blk = lax.axis_index("rep"), lax.axis_index("blk")
     add_list(table, 1 - rep, blk, left_rows, right_t, wave_pair, acc)
     split_rows(acc, outs)
 
 
 def own_kernel(early, table, left_rows, right_t, wave, wave_pair, start, acc):
-    del start
+    acc[...] = start[...]
     rep, blk = lax.axis_index("rep"), lax.axis_index("blk")
     add_list(table, rep, blk, left_rows, right_t, wave, acc, early)
     add_list(table, 1 - rep, blk, left_rows, right_t, wave_pair, acc)
@@ -168,18 +168,17 @@
     caps = slot_table.shape[-1]
     early = caps // 8
     left_shape = shape((terms, op_count * rows, width), left_env.dtype)
-    left_rows, right_t, wave, own_table, acc = call(
+    left_rows, right_t, wave, own_table = call(
         functools.partial(load_kernel, order),
         (
             left_shape,
             shape(right_env.shape, right_env.dtype),
             shape(wavefunction.shape, wavefunction.dtype),
             table_spec,
-            acc_shape,
         ),
         [in_hbm(x) for x in (left_env, right_env, wavefunction, slot_table)],
         [ANY] * 4,
-        (VMEM, VMEM, VMEM, SMEM, VMEM),
+        (VMEM, VMEM, VMEM, SMEM),
         scratch_shapes=[
             pltpu.VMEM(right_env.shape, right_env.dtype),
             pltpu.SemaphoreType.DMA((2 + op_count + terms,)),
@@ -189,20 +188,19 @@
     acc, other_table, acc_other = call(
         functools.partial(other_kernel, early),
         (acc_shape, table_spec, acc_shape),
-        (table_other, own_table, left_rows, right_t, wave, acc),
-        [ANY, SMEM] + [VMEM] * 4,
+        (table_other, own_table, left_rows, right_t, wave),
+        [ANY, SMEM] + [VMEM] * 3,
         (VMEM, SMEM, VMEM),
-        input_output_aliases={5: 0},
         scratch_shapes=[pltpu.SemaphoreType.DMA],
         cost_estimate=COSTLY,
     )
-    _, *sends = call(
+    sends = call(
         pair_kernel,
-        (acc_shape,) + tuple(shape(b, LINK) for b in blocks),
+        tuple(shape(b, LINK) for b in blocks),
         (other_table, left_rows, right_t, wave_pair, acc_other),
         [SMEM] + [VMEM] * 4,
-        (VMEM,) * (1 + len(blocks)),
-        input_output_aliases={4: 0},
+        (VMEM,) * len(blocks),
+        scratch_shapes=[pltpu.VMEM(acc_shape.shape, f32)],
     )
 
     def to_blk(x):
@@ -219,7 +217,6 @@
         (own_table, left_rows, right_t, wave, wave_pair, acc),
         [SMEM] + [VMEM] * 5,
         VMEM,
-        input_output_aliases={5: 0},
     )
     got_rest = to_blk(rest)
     arrived, before = [], ()

time: 26.4 us -> 26.4 us (level)
  transfers between devices with their start and end apart: 8 -> 8, of which waited for: 3 -> 3; matrix products, arithmetic and copies ran while one was open for 0% -> 0% of each run, Pallas kernels for 24% -> 23%
where the time goes in v8:
time: 26.4 us; the launch traced here: 26.1 us
  starting transfers between devices  13.5 us (51%)
  Pallas kernels  8.21 us (31%)
  waiting for transfers between devices  4.37 us (17%)
    pallas_call x8, Pallas kernels, call(): pl.pallas_call(kernel, out_shape=out_shape, in_specs=ins, out_specs=outs,...  8.21 us
    ppermute x3, starting transfers between devices, to_op(): return lax.ppermute(x, 'op', [(i, i ^ s) for i in range(op_count)])  6.97 us
    ppermute x3, waiting for transfers between devices, to_op(): return lax.ppermute(x, 'op', [(i, i ^ s) for i in range(op_count)])  4.36 us
    ppermute x3, starting transfers between devices, to_blk(): return lax.ppermute(x, 'blk', swap)  3.44 us
    ppermute x1, starting transfers between devices, at_source(): table_other = lax.ppermute(slot_table, ('blk', 'rep'), across)  2.38 us
    ppermute x1, starting transfers between devices, at_source(): wave_pair = lax.ppermute(wavefunction, 'rep', swap)  0.68 us
  transfers between devices with their start and end apart: 8, of which 3 were waited for; matrix products, arithmetic and copies ran while one was open for 0% of the time, Pallas kernels for 23%

profile of v8, /device:TPU:0, one launch (start us, length us, event | category | flops | bytes accessed | tf_op | source)
XLA Modules:
  0.0 26.1 jit_solution(9460562606456082113)
XLA Ops:
  0.0 2.4 %collective-permute-start.1 = (s32[3,1,1,2,2,64]{5,4,3,2,1,0:T(2,128)}, s32[3,1,1,2,2,64]{5,4,3,2,1,0:T(2,128)S(1)}, u32[]{:S(2)}, u32[]{:S(2)}) collective-permute-start(s32[3,1,1,2,2,64]{5,4,3,2,1,0:T(2,128)} %table.1), channel_id=1, source_target_pairs={{0,3},{1,2},{2,1},{3,0},{4,7},{5,6},{6,5},{7,4},{8,11},{9,10},{10,... | collective-permute-start | bytes 9224 | tf_op jit(solution)/shard_map/ppermute | solution.py:165
  2.4 0.7 %collective-permute-start = (bf16[12,128,128]{2,1,0:T(8,128)(2,1)}, bf16[12,128,128]{2,1,0:T(8,128)(2,1)S(1)}, u32[]{:S(2)}, u32[]{:S(2)}) collective-permute-start(bf16[12,128,128]{2,1,0:T(8,128)(2,1)} %wave.1), channel_id=1, source_target_pairs={{0,1},{1,0},{2,3},{3,2},{4,5},{5,4},{6,7},{7,6},{8,9},{9,8},{10,11... | collective-permute-start | bytes 1179656 | tf_op jit(solution)/shard_map/ppermute | solution.py:166
  3.1 1.8 %shard_map.46 = (bf16[32,64,128]{2,1,0:T(8,128)(2,1)S(1)}, bf16[32,128,128]{2,1,0:T(8,128)(2,1)S(1)}, bf16[12,128,128]{2,1,0:T(8,128)(2,1)S(1)}, s32[3,1,1,2,2,64]{5,4,3,2,1,0:T(2,128)S(4)}) custom-call(bf16[32,128,128]{2,1,0:T(8,128)(2,1)} %left.1, bf16[32,128,128]{2,1,0:T(8,128)(2,1)} %right.1, bf16[12,128,128]{2,1,0:T(8,128)(2,1)} %wave.1, ...), custom_call_target="tpu_custom_call" | custom-call | tf_op jit(solution)/shard_map/pallas_call | solution.py:146
  4.9 0.0 collective-permute-done.1.other
  4.9 1.9 %shard_map.47 = (f32[25,64,128]{2,1,0:T(8,128)S(1)}, s32[3,1,1,2,2,64]{5,4,3,2,1,0:T(2,128)S(4)}, f32[25,64,128]{2,1,0:T(8,128)S(1)}) custom-call(s32[3,1,1,2,2,64]{5,4,3,2,1,0:T(2,128)S(1)} %collective-permute-done.1.other, s32[3,1,1,2,2,64]{5,4,3,2,1,0:T(2,128)S(4)} %get-tuple-element.17.table, bf16[32,64,128]{2,1,0:T(8,128)(2,1)S(1)} %get-tuple-element.18.left_rows, ...), custom_call_target="tpu_custom_call" | custom-call | flops 10000000000 | bytes 10000000 | tf_op jit(solution)/shard_map/pallas_call | solution.py:146
  6.8 0.0 collective-permute-done.wave_pair
  6.9 1.3 %shard_map.49 = (bf16[24,16,128]{2,1,0:T(8,128)(2,1)S(1)}, bf16[24,16,128]{2,1,0:T(8,128)(2,1)S(1)}, bf16[2,24,16,128]{3,2,1,0:T(8,128)(2,1)S(1)}) custom-call(s32[3,1,1,2,2,64]{5,4,3,2,1,0:T(2,128)S(4)} %get-tuple-element.22.table, bf16[32,64,128]{2,1,0:T(8,128)(2,1)S(1)} %get-tuple-element.18.left_rows, ...), custom_call_target="tpu_custom_call" | custom-call | tf_op jit(solution)/shard_map/pallas_call | solution.py:146
  8.2 1.4 %collective-permute-start.4 = (bf16[24,16,128]{2,1,0:T(8,128)(2,1)S(1)}, bf16[24,16,128]{2,1,0:T(8,128)(2,1)S(1)}, u32[]{:S(2)}, u32[]{:S(2)}) collective-permute-start(bf16[24,16,128]{2,1,0:T(8,128)(2,1)S(1)} %get-tuple-element.26), channel_id=1, source_target_pairs={{0,2},{2,0},{1,3},{3,1},{4,6},{6,4},{5,7},{7,5},{8,10},{10,8},{9,1... | collective-permute-start | bytes 294920 | tf_op jit(solution)/shard_map/ppermute | solution.py:207
  9.6 0.7 %collective-permute-start.3 = (bf16[24,16,128]{2,1,0:T(8,128)(2,1)S(1)}, bf16[24,16,128]{2,1,0:T(8,128)(2,1)S(1)}, u32[]{:S(2)}, u32[]{:S(2)}) collective-permute-start(bf16[24,16,128]{2,1,0:T(8,128)(2,1)S(1)} %get-tuple-element.25), channel_id=1, source_target_pairs={{0,2},{2,0},{1,3},{3,1},{4,6},{6,4},{5,7},{7,5},{8,10},{10,8},{9,1... | collective-permute-start | bytes 294920 | tf_op jit(solution)/shard_map/ppermute | solution.py:207
  10.3 1.3 %collective-permute-start.2 = (bf16[2,24,16,128]{3,2,1,0:T(8,128)(2,1)S(1)}, bf16[2,24,16,128]{3,2,1,0:T(8,128)(2,1)S(1)}, u32[]{:S(2)}, u32[]{:S(2)}) collective-permute-start(bf16[2,24,16,128]{3,2,1,0:T(8,128)(2,1)S(1)} %get-tuple-element.24), channel_id=1, source_target_pairs={{0,2},{2,0},{1,3},{3,1},{4,6},{6,4},{5,7},{7,5},{8,10},{10,8},{9,1... | collective-permute-start | bytes 589832 | tf_op jit(solution)/shard_map/ppermute | solution.py:207
  11.6 2.2 %shard_map.48.acc = f32[25,64,128]{2,1,0:T(8,128)S(1)} custom-call(s32[3,1,1,2,2,64]{5,4,3,2,1,0:T(2,128)S(4)} %get-tuple-element.17.table, bf16[32,64,128]{2,1,0:T(8,128)(2,1)S(1)} %get-tuple-element.18.left_rows, bf16[32,128,128]{2,1,0:T(8,128)(2,1)S(1)} %get-tuple-element.19.right_t, bf16[12,128,128]{2,1,0:T(8,128)(2,1)S(1)} %get-tuple-element.20.wave, ...), custom_call_target="tpu_custom_call" | custom-call | tf_op jit(solution)/shard_map/pallas_call | solution.py:146
  13.9 0.0 collective-permute-done.4.got
  13.9 2.7 %collective-permute-start.5 = (bf16[24,16,128]{2,1,0:T(8,128)(2,1)S(1)}, bf16[24,16,128]{2,1,0:T(8,128)(2,1)S(1)}, u32[]{:S(2)}, u32[]{:S(2)}) collective-permute-start(bf16[24,16,128]{2,1,0:T(8,128)(2,1)S(1)} %shard_map.50.refs_0_), channel_id=1, source_target_pairs={{0,8},{4,12},{8,0},{12,4},{1,9},{5,13},{9,1},{13,5},{2,10},{6,14},... | collective-permute-start | bytes 294920 | tf_op jit(solution)/shard_map/ppermute | solution.py:210
  16.6 0.0 collective-permute-done.3.got
  16.6 3.1 %collective-permute-start.6 = (bf16[24,16,128]{2,1,0:T(8,128)(2,1)S(1)}, bf16[24,16,128]{2,1,0:T(8,128)(2,1)S(1)}, u32[]{:S(2)}, u32[]{:S(2)}) collective-permute-start(bf16[24,16,128]{2,1,0:T(8,128)(2,1)S(1)} %shard_map.51.before), channel_id=1, source_target_pairs={{0,12},{4,8},{8,4},{12,0},{1,13},{5,9},{9,5},{13,1},{2,14},{6,10},... | collective-permute-start | bytes 294920 | tf_op jit(solution)/shard_map/ppermute | solution.py:210
  19.7 0.0 collective-permute-done.2.got
  19.8 1.2 %collective-permute-start.7 = (bf16[24,16,128]{2,1,0:T(8,128)(2,1)S(1)}, bf16[24,16,128]{2,1,0:T(8,128)(2,1)S(1)}, u32[]{:S(2)}, u32[]{:S(2)}) collective-permute-start(bf16[24,16,128]{2,1,0:T(8,128)(2,1)S(1)} %get-tuple-element.28), channel_id=1, source_target_pairs={{0,4},{4,0},{8,12},{12,8},{1,5},{5,1},{9,13},{13,9},{2,6},{6,2},{1... | collective-permute-start | bytes 294920 | tf_op jit(solution)/shard_map/ppermute | solution.py:210
  21.0 2.2 %collective-permute-done.6.rest_1_ = bf16[24,16,128]{2,1,0:T(8,128)(2,1)S(1)} collective-permute-done((bf16[24,16,128]{2,1,0:T(8,128)(2,1)S(1)}, bf16[24,16,128]{2,1,0:T(8,128)(2,1)S(1)}, u32[]{:S(2)}, u32[]{:S(2)}) %collective-permute-start.6) | collective-permute-done | bytes 98336 | tf_op jit(solution)/shard_map/ppermute | solution.py:210
  23.1 0.6 %collective-permute-done.5.rest_0_ = bf16[24,16,128]{2,1,0:T(8,128)(2,1)S(1)} collective-permute-done((bf16[24,16,128]{2,1,0:T(8,128)(2,1)S(1)}, bf16[24,16,128]{2,1,0:T(8,128)(2,1)S(1)}, u32[]{:S(2)}, u32[]{:S(2)}) %collective-permute-start.5) | collective-permute-done | bytes 98336 | tf_op jit(solution)/shard_map/ppermute | solution.py:210
  23.7 1.6 %collective-permute-done.7.rest_2_ = bf16[24,16,128]{2,1,0:T(8,128)(2,1)S(1)} collective-permute-done((bf16[24,16,128]{2,1,0:T(8,128)(2,1)S(1)}, bf16[24,16,128]{2,1,0:T(8,128)(2,1)S(1)}, u32[]{:S(2)}, u32[]{:S(2)}) %collective-permute-start.7) | collective-permute-done | bytes 98336 | tf_op jit(solution)/shard_map/ppermute | solution.py:210
  25.3 0.8 %shard_map.53 = f32[16,24,128]{2,1,0:T(8,128)} custom-call(f32[24,16,128]{2,1,0:T(8,128)S(1)} %get-tuple-element.27.own, bf16[24,16,128]{2,1,0:T(8,128)(2,1)S(1)} %collective-permute-done.5.rest_0_, bf16[24,16,128]{2,1,0:T(8,128)(2,1)S(1)} %collective-permute-done.6.rest_1_, bf16[24,16,128]{2,1,0:T(8,128)(2,1)S(1)} %collective-permute-done.7.rest_2_), custom_call_target="tpu_custom_call" | custom-call | tf_op jit(solution)/shard_map/pallas_call | solution.py:146
  (3 shorter events, 0.1 us)
Async XLA Ops:
  0.0 4.9 %collective-permute-start.1 = (s32[3,1,1,2,2,64]{5,4,3,2,1,0:T(2,128)}, s32[3,1,1,2,2,64]{5,4,3,2,1,0:T(2,128)S(1)}, u32[]{:S(2)}, u32[]{:S(2)}) collective-permute-start(s32[3,1,1,2,2,64]{5,4,3,2,1,0:T(2,128)} %table.1), channel_id=1, source_target_pairs={{0,3},{1,2},{2,1},{3,0},{4,7},{5,6},{6,5},{7,4},{8,11},{9,10},{10,... | collective-permute-start | bytes 9224 | tf_op jit(solution)/shard_map/ppermute | solution.py:165
  2.4 4.5 %collective-permute-start = (bf16[12,128,128]{2,1,0:T(8,128)(2,1)}, bf16[12,128,128]{2,1,0:T(8,128)(2,1)S(1)}, u32[]{:S(2)}, u32[]{:S(2)}) collective-permute-start(bf16[12,128,128]{2,1,0:T(8,128)(2,1)} %wave.1), channel_id=1, source_target_pairs={{0,1},{1,0},{2,3},{3,2},{4,5},{5,4},{6,7},{7,6},{8,9},{9,8},{10,11... | collective-permute-start | bytes 1179656 | tf_op jit(solution)/shard_map/ppermute | solution.py:166
  8.2 5.7 %collective-permute-start.4 = (bf16[24,16,128]{2,1,0:T(8,128)(2,1)S(1)}, bf16[24,16,128]{2,1,0:T(8,128)(2,1)S(1)}, u32[]{:S(2)}, u32[]{:S(2)}) collective-permute-start(bf16[24,16,128]{2,1,0:T(8,128)(2,1)S(1)} %get-tuple-element.26), channel_id=1, source_target_pairs={{0,2},{2,0},{1,3},{3,1},{4,6},{6,4},{5,7},{7,5},{8,10},{10,8},{9,1... | collective-permute-start | bytes 294920 | tf_op jit(solution)/shard_map/ppermute | solution.py:207
  9.6 7.0 %collective-permute-start.3 = (bf16[24,16,128]{2,1,0:T(8,128)(2,1)S(1)}, bf16[24,16,128]{2,1,0:T(8,128)(2,1)S(1)}, u32[]{:S(2)}, u32[]{:S(2)}) collective-permute-start(bf16[24,16,128]{2,1,0:T(8,128)(2,1)S(1)} %get-tuple-element.25), channel_id=1, source_target_pairs={{0,2},{2,0},{1,3},{3,1},{4,6},{6,4},{5,7},{7,5},{8,10},{10,8},{9,1... | collective-permute-start | bytes 294920 | tf_op jit(solution)/shard_map/ppermute | solution.py:207
  10.3 9.4 %collective-permute-start.2 = (bf16[2,24,16,128]{3,2,1,0:T(8,128)(2,1)S(1)}, bf16[2,24,16,128]{3,2,1,0:T(8,128)(2,1)S(1)}, u32[]{:S(2)}, u32[]{:S(2)}) collective-permute-start(bf16[2,24,16,128]{3,2,1,0:T(8,128)(2,1)S(1)} %get-tuple-element.24), channel_id=1, source_target_pairs={{0,2},{2,0},{1,3},{3,1},{4,6},{6,4},{5,7},{7,5},{8,10},{10,8},{9,1... | collective-permute-start | bytes 589832 | tf_op jit(solution)/shard_map/ppermute | solution.py:207
  13.9 9.8 %collective-permute-start.5 = (bf16[24,16,128]{2,1,0:T(8,128)(2,1)S(1)}, bf16[24,16,128]{2,1,0:T(8,128)(2,1)S(1)}, u32[]{:S(2)}, u32[]{:S(2)}) collective-permute-start(bf16[24,16,128]{2,1,0:T(8,128)(2,1)S(1)} %shard_map.50.refs_0_), channel_id=1, source_target_pairs={{0,8},{4,12},{8,0},{12,4},{1,9},{5,13},{9,1},{13,5},{2,10},{6,14},... | collective-permute-start | bytes 294920 | tf_op jit(solution)/shard_map/ppermute | solution.py:210
  16.6 6.5 %collective-permute-start.6 = (bf16[24,16,128]{2,1,0:T(8,128)(2,1)S(1)}, bf16[24,16,128]{2,1,0:T(8,128)(2,1)S(1)}, u32[]{:S(2)}, u32[]{:S(2)}) collective-permute-start(bf16[24,16,128]{2,1,0:T(8,128)(2,1)S(1)} %shard_map.51.before), channel_id=1, source_target_pairs={{0,12},{4,8},{8,4},{12,0},{1,13},{5,9},{9,5},{13,1},{2,14},{6,10},... | collective-permute-start | bytes 294920 | tf_op jit(solution)/shard_map/ppermute | solution.py:210
  19.8 5.6 %collective-permute-start.7 = (bf16[24,16,128]{2,1,0:T(8,128)(2,1)S(1)}, bf16[24,16,128]{2,1,0:T(8,128)(2,1)S(1)}, u32[]{:S(2)}, u32[]{:S(2)}) collective-permute-start(bf16[24,16,128]{2,1,0:T(8,128)(2,1)S(1)} %get-tuple-element.28), channel_id=1, source_target_pairs={{0,4},{4,0},{8,12},{12,8},{1,5},{5,1},{9,13},{13,9},{2,6},{6,2},{1... | collective-permute-start | bytes 294920 | tf_op jit(solution)/shard_map/ppermute | solution.py:210

commit v9 on v8

--- a/solution.py
+++ b/solution.py
@@ -11,6 +11,7 @@
 SMEM = pl.BlockSpec(memory_space=pltpu.SMEM)
 ANY = pl.BlockSpec(memory_space=pl.ANY)
 LINK = jnp.bfloat16
+STEP = pl.CostEstimate(flops=3 * 10**9, bytes_accessed=3 * 10**6, transcendentals=0)
 COSTLY = pl.CostEstimate(flops=10**10, bytes_accessed=10**7, transcendentals=0)
 
 
@@ -127,17 +128,23 @@
     add_block(acc, block, got, refs[-1])
 
 
-def last_sum_kernel(first, acc, got, before, *outs):
+def cut_kernel(block, acc, before, out):
     del before
-    for g, out in enumerate(outs):
-        add_block(acc, first + g, got.at[g], out)
-
-
-def final_kernel(own, *rest):
-    got, out = rest[:-1], rest[-1]
-    total = own[...]
-    for g in got:
-        total = total + g[...].astype(jnp.float32)
+    tiles, rows, _ = out.shape
+    out[...] = acc[0:tiles, block * rows : (block + 1) * rows, :].astype(out.dtype)
+
+
+def pair_sum_kernel(kept, got, before, out):
+    del before
+    out[...] = (kept[...] + got[...].astype(jnp.float32)).astype(out.dtype)
+
+
+def more_kernel(so_far, got, out):
+    out[...] = so_far[...] + got[...].astype(jnp.float32)
+
+
+def final_kernel(so_far, got, out):
+    total = so_far[...] + got[...].astype(jnp.float32)
     for t in range(total.shape[0]):
         out[:, t, :] = total[t]
 
@@ -184,7 +191,6 @@
             pltpu.SemaphoreType.DMA((2 + op_count + terms,)),
         ],
     )
-    blocks = (block,) * (op_count - 2) + ((2,) + block,)
     acc, other_table, acc_other = call(
         functools.partial(other_kernel, early),
         (acc_shape, table_spec, acc_shape),
@@ -196,10 +202,10 @@
     )
     sends = call(
         pair_kernel,
-        tuple(shape(b, LINK) for b in blocks),
+        (shape(block, LINK),) * (op_count - 1) + (shape(block, f32),),
         (other_table, left_rows, right_t, wave_pair, acc_other),
         [SMEM] + [VMEM] * 4,
-        (VMEM,) * len(blocks),
+        (VMEM,) * op_count,
         scratch_shapes=[pltpu.VMEM(acc_shape.shape, f32)],
     )
 
@@ -209,8 +215,9 @@
     def to_op(x, s):
         return lax.ppermute(x, "op", [(i, i ^ s) for i in range(op_count)])
 
-    *far, rest = sends
+    *far, near, own = sends
     got = [to_blk(x) for x in far]
+    got_near = to_op(near, order[-2])
     acc = call(
         functools.partial(own_kernel, early),
         acc_shape,
@@ -218,32 +225,55 @@
         [SMEM] + [VMEM] * 5,
         VMEM,
     )
-    got_rest = to_blk(rest)
-    arrived, before = [], ()
-    for g, s in enumerate(order[:-2]):
-        total = call(
-            functools.partial(sum_kernel, g),
-            shape(block, LINK),
-            (acc, got[g], *before),
-            [VMEM] * 2 + [ANY] * len(before),
-            VMEM,
-            cost_estimate=COSTLY,
+    total = call(
+        functools.partial(sum_kernel, 0),
+        shape(block, LINK),
+        (acc, got[0]),
+        [VMEM] * 2,
+        VMEM,
+    )
+    arrived = [to_op(total, order[0])]
+    near = call(
+        functools.partial(cut_kernel, op_count - 2),
+        shape(block, LINK),
+        (acc, total),
+        [VMEM, ANY],
+        VMEM,
+    )
+    arrived.append(to_op(near, order[-2]))
+    total = call(
+        functools.partial(sum_kernel, 1),
+        shape(block, LINK),
+        (acc, got[1], near),
+        [VMEM] * 2 + [ANY],
+        VMEM,
+    )
+    arrived.append(to_op(total, order[1]))
+    own = call(
+        pair_sum_kernel,
+        shape(block, LINK),
+        (own, got_near, total),
+        [VMEM] * 2 + [ANY],
+        VMEM,
+    )
+    here = to_blk(own)
+    so_far = call(
+        functools.partial(sum_kernel, op_count - 1),
+        shape(block, f32),
+        (acc, arrived[0]),
+        [VMEM] * 2,
+        VMEM,
+        cost_estimate=STEP,
+    )
+    for x in arrived[1:]:
+        so_far = call(
+            more_kernel, shape(block, f32), (so_far, x), [VMEM] * 2, VMEM, cost_estimate=STEP
         )
-        arrived.append(to_op(total, s))
-        before = (total,)
-    near, own = call(
-        functools.partial(last_sum_kernel, op_count - 2),
-        (shape(block, LINK), shape(block, f32)),
-        (acc, got_rest, *before),
-        [VMEM] * 2 + [ANY],
-        (VMEM,) * 2,
-    )
-    arrived.append(to_op(near, order[-2]))
     return call(
         final_kernel,
         shape((rows, tiles, width), f32),
-        (own, *arrived),
-        [VMEM] * op_count,
+        (so_far, here),
+        [VMEM] * 2,
         VMEM,
     )
 

time: 26.4 us -> 25.9 us (0.981)
  starting transfers between devices: 13.5 us -> 12.8 us
    ppermute x3 -> x4, starting transfers between devices: 6.97 us -> 6.16 us  [to_op(): return lax.ppermute(x, 'op', [(i, i ^ s) for i in range(op_count)])]
    ppermute x3 -> x4, waiting for transfers between devices: 4.36 us -> 4.48 us  [to_op(): return lax.ppermute(x, 'op', [(i, i ^ s) for i in range(op_count)])]
    pallas_call x8 -> x12, Pallas kernels: 8.21 us -> 8.27 us  [call(): pl.pallas_call(kernel, out_shape=out_shape, in_specs=ins, out_specs=outs,...]
  transfers between devices with their start and end apart: 8 -> 9, of which waited for: 3 -> 3; matrix products, arithmetic and copies ran while one was open for 0% -> 0% of each run, Pallas kernels for 23% -> 24%
where the time goes in v9:
time: 25.9 us; the launch traced here: 25.7 us
  starting transfers between devices  12.8 us (49%)
  Pallas kernels  8.27 us (32%)
  waiting for transfers between devices  4.49 us (17%)
    pallas_call x12, Pallas kernels, call(): pl.pallas_call(kernel, out_shape=out_shape, in_specs=ins, out_specs=outs,...  8.27 us
    ppermute x4, starting transfers between devices, to_op(): return lax.ppermute(x, 'op', [(i, i ^ s) for i in range(op_count)])  6.16 us
    ppermute x4, waiting for transfers between devices, to_op(): return lax.ppermute(x, 'op', [(i, i ^ s) for i in range(op_count)])  4.48 us
    ppermute x3, starting transfers between devices, to_blk(): return lax.ppermute(x, 'blk', swap)  3.62 us
    ppermute x1, starting transfers between devices, at_source(): table_other = lax.ppermute(slot_table, ('blk', 'rep'), across)  2.38 us
    ppermute x1, starting transfers between devices, at_source(): wave_pair = lax.ppermute(wavefunction, 'rep', swap)  0.68 us
  transfers between devices with their start and end apart: 9, of which 3 were waited for; matrix products, arithmetic and copies ran while one was open for 0% of the time, Pallas kernels for 24%

profile of v9, /device:TPU:0, one launch (start us, length us, event | category | flops | bytes accessed | tf_op | source)
XLA Modules:
  0.0 25.7 jit_solution(7470322831275731576)
XLA Ops:
  0.0 2.4 %collective-permute-start.1 = (s32[3,1,1,2,2,64]{5,4,3,2,1,0:T(2,128)}, s32[3,1,1,2,2,64]{5,4,3,2,1,0:T(2,128)S(1)}, u32[]{:S(2)}, u32[]{:S(2)}) collective-permute-start(s32[3,1,1,2,2,64]{5,4,3,2,1,0:T(2,128)} %table.1), channel_id=1, source_target_pairs={{0,3},{1,2},{2,1},{3,0},{4,7},{5,6},{6,5},{7,4},{8,11},{9,10},{10,... | collective-permute-start | bytes 9224 | tf_op jit(solution)/shard_map/ppermute | solution.py:172
  2.4 0.7 %collective-permute-start = (bf16[12,128,128]{2,1,0:T(8,128)(2,1)}, bf16[12,128,128]{2,1,0:T(8,128)(2,1)S(1)}, u32[]{:S(2)}, u32[]{:S(2)}) collective-permute-start(bf16[12,128,128]{2,1,0:T(8,128)(2,1)} %wave.1), channel_id=1, source_target_pairs={{0,1},{1,0},{2,3},{3,2},{4,5},{5,4},{6,7},{7,6},{8,9},{9,8},{10,11... | collective-permute-start | bytes 1179656 | tf_op jit(solution)/shard_map/ppermute | solution.py:173
  3.1 1.8 %shard_map.46 = (bf16[32,64,128]{2,1,0:T(8,128)(2,1)S(1)}, bf16[32,128,128]{2,1,0:T(8,128)(2,1)S(1)}, bf16[12,128,128]{2,1,0:T(8,128)(2,1)S(1)}, s32[3,1,1,2,2,64]{5,4,3,2,1,0:T(2,128)S(4)}) custom-call(bf16[32,128,128]{2,1,0:T(8,128)(2,1)} %left.1, bf16[32,128,128]{2,1,0:T(8,128)(2,1)} %right.1, bf16[12,128,128]{2,1,0:T(8,128)(2,1)} %wave.1, ...), custom_call_target="tpu_custom_call" | custom-call | tf_op jit(solution)/shard_map/pallas_call | solution.py:153
  4.9 0.0 collective-permute-done.1.other
  4.9 1.9 %shard_map.47 = (f32[25,64,128]{2,1,0:T(8,128)S(1)}, s32[3,1,1,2,2,64]{5,4,3,2,1,0:T(2,128)S(4)}, f32[25,64,128]{2,1,0:T(8,128)S(1)}) custom-call(s32[3,1,1,2,2,64]{5,4,3,2,1,0:T(2,128)S(1)} %collective-permute-done.1.other, s32[3,1,1,2,2,64]{5,4,3,2,1,0:T(2,128)S(4)} %get-tuple-element.16.table, bf16[32,64,128]{2,1,0:T(8,128)(2,1)S(1)} %get-tuple-element.17.left_rows, ...), custom_call_target="tpu_custom_call" | custom-call | flops 10000000000 | bytes 10000000 | tf_op jit(solution)/shard_map/pallas_call | solution.py:153
  6.8 0.0 collective-permute-done.wave_pair
  6.9 1.3 %shard_map.49 = (bf16[24,16,128]{2,1,0:T(8,128)(2,1)S(1)}, bf16[24,16,128]{2,1,0:T(8,128)(2,1)S(1)}, bf16[24,16,128]{2,1,0:T(8,128)(2,1)S(1)}, f32[24,16,128]{2,1,0:T(8,128)S(1)}) custom-call(s32[3,1,1,2,2,64]{5,4,3,2,1,0:T(2,128)S(4)} %get-tuple-element.21.table, bf16[32,64,128]{2,1,0:T(8,128)(2,1)S(1)} %get-tuple-element.17.left_rows, ...), custom_call_target="tpu_custom_call" | custom-call | tf_op jit(solution)/shard_map/pallas_call | solution.py:153
  8.2 1.4 %collective-permute-start.2 = (bf16[24,16,128]{2,1,0:T(8,128)(2,1)S(1)}, bf16[24,16,128]{2,1,0:T(8,128)(2,1)S(1)}, u32[]{:S(2)}, u32[]{:S(2)}) collective-permute-start(bf16[24,16,128]{2,1,0:T(8,128)(2,1)S(1)} %get-tuple-element.23), channel_id=1, source_target_pairs={{0,2},{2,0},{1,3},{3,1},{4,6},{6,4},{5,7},{7,5},{8,10},{10,8},{9,1... | collective-permute-start | bytes 294920 | tf_op jit(solution)/shard_map/ppermute | solution.py:213
  9.6 0.7 %collective-permute-start.5 = (bf16[24,16,128]{2,1,0:T(8,128)(2,1)S(1)}, bf16[24,16,128]{2,1,0:T(8,128)(2,1)S(1)}, u32[]{:S(2)}, u32[]{:S(2)}) collective-permute-start(bf16[24,16,128]{2,1,0:T(8,128)(2,1)S(1)} %get-tuple-element.24), channel_id=1, source_target_pairs={{0,2},{2,0},{1,3},{3,1},{4,6},{6,4},{5,7},{7,5},{8,10},{10,8},{9,1... | collective-permute-start | bytes 294920 | tf_op jit(solution)/shard_map/ppermute | solution.py:213
  10.3 1.6 %collective-permute-start.7 = (bf16[24,16,128]{2,1,0:T(8,128)(2,1)S(1)}, bf16[24,16,128]{2,1,0:T(8,128)(2,1)S(1)}, u32[]{:S(2)}, u32[]{:S(2)}) collective-permute-start(bf16[24,16,128]{2,1,0:T(8,128)(2,1)S(1)} %get-tuple-element.26), channel_id=1, source_target_pairs={{0,4},{4,0},{8,12},{12,8},{1,5},{5,1},{9,13},{13,9},{2,6},{6,2},{1... | collective-permute-start | bytes 294920 | tf_op jit(solution)/shard_map/ppermute | solution.py:216
  11.9 2.2 %shard_map.48.acc = f32[25,64,128]{2,1,0:T(8,128)S(1)} custom-call(s32[3,1,1,2,2,64]{5,4,3,2,1,0:T(2,128)S(4)} %get-tuple-element.16.table, bf16[32,64,128]{2,1,0:T(8,128)(2,1)S(1)} %get-tuple-element.17.left_rows, bf16[32,128,128]{2,1,0:T(8,128)(2,1)S(1)} %get-tuple-element.18.right_t, bf16[12,128,128]{2,1,0:T(8,128)(2,1)S(1)} %get-tuple-element.19.wave, ...), custom_call_target="tpu_custom_call" | custom-call | tf_op jit(solution)/shard_map/pallas_call | solution.py:153
  14.1 0.0 collective-permute-done.2.got
  14.1 2.7 %collective-permute-start.3 = (bf16[24,16,128]{2,1,0:T(8,128)(2,1)S(1)}, bf16[24,16,128]{2,1,0:T(8,128)(2,1)S(1)}, u32[]{:S(2)}, u32[]{:S(2)}) collective-permute-start(bf16[24,16,128]{2,1,0:T(8,128)(2,1)S(1)} %shard_map.50.before), channel_id=1, source_target_pairs={{0,8},{4,12},{8,0},{12,4},{1,9},{5,13},{9,1},{13,5},{2,10},{6,14},... | collective-permute-start | bytes 294920 | tf_op jit(solution)/shard_map/ppermute | solution.py:216
  16.8 1.4 %collective-permute-start.4 = (bf16[24,16,128]{2,1,0:T(8,128)(2,1)S(1)}, bf16[24,16,128]{2,1,0:T(8,128)(2,1)S(1)}, u32[]{:S(2)}, u32[]{:S(2)}) collective-permute-start(bf16[24,16,128]{2,1,0:T(8,128)(2,1)S(1)} %shard_map.52.refs_0_), channel_id=1, source_target_pairs={{0,4},{4,0},{8,12},{12,8},{1,5},{5,1},{9,13},{13,9},{2,6},{6,2},{1... | collective-permute-start | bytes 294920 | tf_op jit(solution)/shard_map/ppermute | solution.py:216
  18.2 0.0 collective-permute-done.5.got
  18.3 0.5 %collective-permute-start.6 = (bf16[24,16,128]{2,1,0:T(8,128)(2,1)S(1)}, bf16[24,16,128]{2,1,0:T(8,128)(2,1)S(1)}, u32[]{:S(2)}, u32[]{:S(2)}) collective-permute-start(bf16[24,16,128]{2,1,0:T(8,128)(2,1)S(1)} %shard_map.54.before), channel_id=1, source_target_pairs={{0,12},{4,8},{8,4},{12,0},{1,13},{5,9},{9,5},{13,1},{2,14},{6,10},... | collective-permute-start | bytes 294920 | tf_op jit(solution)/shard_map/ppermute | solution.py:216
  18.8 0.0 collective-permute-done.7.got
  18.8 1.5 %collective-permute-start.8 = (bf16[24,16,128]{2,1,0:T(8,128)(2,1)S(1)}, bf16[24,16,128]{2,1,0:T(8,128)(2,1)S(1)}, u32[]{:S(2)}, u32[]{:S(2)}) collective-permute-start(bf16[24,16,128]{2,1,0:T(8,128)(2,1)S(1)} %shard_map.56), channel_id=1, source_target_pairs={{0,2},{2,0},{1,3},{3,1},{4,6},{6,4},{5,7},{7,5},{8,10},{10,8},{9,1... | collective-permute-start | bytes 294920 | tf_op jit(solution)/shard_map/ppermute | solution.py:213
  20.3 2.2 %collective-permute-done.3.got = bf16[24,16,128]{2,1,0:T(8,128)(2,1)S(1)} collective-permute-done((bf16[24,16,128]{2,1,0:T(8,128)(2,1)S(1)}, bf16[24,16,128]{2,1,0:T(8,128)(2,1)S(1)}, u32[]{:S(2)}, u32[]{:S(2)}) %collective-permute-start.3) | collective-permute-done | bytes 98336 | tf_op jit(solution)/shard_map/ppermute | solution.py:216
  22.5 0.6 %collective-permute-done.4.got = bf16[24,16,128]{2,1,0:T(8,128)(2,1)S(1)} collective-permute-done((bf16[24,16,128]{2,1,0:T(8,128)(2,1)S(1)}, bf16[24,16,128]{2,1,0:T(8,128)(2,1)S(1)}, u32[]{:S(2)}, u32[]{:S(2)}) %collective-permute-start.4) | collective-permute-done | bytes 98336 | tf_op jit(solution)/shard_map/ppermute | solution.py:216
  23.2 1.7 %collective-permute-done.6.got = bf16[24,16,128]{2,1,0:T(8,128)(2,1)S(1)} collective-permute-done((bf16[24,16,128]{2,1,0:T(8,128)(2,1)S(1)}, bf16[24,16,128]{2,1,0:T(8,128)(2,1)S(1)}, u32[]{:S(2)}, u32[]{:S(2)}) %collective-permute-start.6) | collective-permute-done | bytes 98336 | tf_op jit(solution)/shard_map/ppermute | solution.py:216
  24.9 0.0 collective-permute-done.8.got
  24.9 0.8 %shard_map.57 = f32[16,24,128]{2,1,0:T(8,128)} custom-call(f32[24,16,128]{2,1,0:T(8,128)S(1)} %shard_map.55.so_far, bf16[24,16,128]{2,1,0:T(8,128)(2,1)S(1)} %collective-permute-done.8.got), custom_call_target="tpu_custom_call" | custom-call | tf_op jit(solution)/shard_map/pallas_call | solution.py:153
  (7 shorter events, 0.1 us)
Async XLA Ops:
  0.0 4.9 %collective-permute-start.1 = (s32[3,1,1,2,2,64]{5,4,3,2,1,0:T(2,128)}, s32[3,1,1,2,2,64]{5,4,3,2,1,0:T(2,128)S(1)}, u32[]{:S(2)}, u32[]{:S(2)}) collective-permute-start(s32[3,1,1,2,2,64]{5,4,3,2,1,0:T(2,128)} %table.1), channel_id=1, source_target_pairs={{0,3},{1,2},{2,1},{3,0},{4,7},{5,6},{6,5},{7,4},{8,11},{9,10},{10,... | collective-permute-start | bytes 9224 | tf_op jit(solution)/shard_map/ppermute | solution.py:172
  2.4 4.5 %collective-permute-start = (bf16[12,128,128]{2,1,0:T(8,128)(2,1)}, bf16[12,128,128]{2,1,0:T(8,128)(2,1)S(1)}, u32[]{:S(2)}, u32[]{:S(2)}) collective-permute-start(bf16[12,128,128]{2,1,0:T(8,128)(2,1)} %wave.1), channel_id=1, source_target_pairs={{0,1},{1,0},{2,3},{3,2},{4,5},{5,4},{6,7},{7,6},{8,9},{9,8},{10,11... | collective-permute-start | bytes 1179656 | tf_op jit(solution)/shard_map/ppermute | solution.py:173
  8.2 5.9 %collective-permute-start.2 = (bf16[24,16,128]{2,1,0:T(8,128)(2,1)S(1)}, bf16[24,16,128]{2,1,0:T(8,128)(2,1)S(1)}, u32[]{:S(2)}, u32[]{:S(2)}) collective-permute-start(bf16[24,16,128]{2,1,0:T(8,128)(2,1)S(1)} %get-tuple-element.23), channel_id=1, source_target_pairs={{0,2},{2,0},{1,3},{3,1},{4,6},{6,4},{5,7},{7,5},{8,10},{10,8},{9,1... | collective-permute-start | bytes 294920 | tf_op jit(solution)/shard_map/ppermute | solution.py:213
  9.6 8.6 %collective-permute-start.5 = (bf16[24,16,128]{2,1,0:T(8,128)(2,1)S(1)}, bf16[24,16,128]{2,1,0:T(8,128)(2,1)S(1)}, u32[]{:S(2)}, u32[]{:S(2)}) collective-permute-start(bf16[24,16,128]{2,1,0:T(8,128)(2,1)S(1)} %get-tuple-element.24), channel_id=1, source_target_pairs={{0,2},{2,0},{1,3},{3,1},{4,6},{6,4},{5,7},{7,5},{8,10},{10,8},{9,1... | collective-permute-start | bytes 294920 | tf_op jit(solution)/shard_map/ppermute | solution.py:213
  10.3 8.5 %collective-permute-start.7 = (bf16[24,16,128]{2,1,0:T(8,128)(2,1)S(1)}, bf16[24,16,128]{2,1,0:T(8,128)(2,1)S(1)}, u32[]{:S(2)}, u32[]{:S(2)}) collective-permute-start(bf16[24,16,128]{2,1,0:T(8,128)(2,1)S(1)} %get-tuple-element.26), channel_id=1, source_target_pairs={{0,4},{4,0},{8,12},{12,8},{1,5},{5,1},{9,13},{13,9},{2,6},{6,2},{1... | collective-permute-start | bytes 294920 | tf_op jit(solution)/shard_map/ppermute | solution.py:216
  14.1 8.4 %collective-permute-start.3 = (bf16[24,16,128]{2,1,0:T(8,128)(2,1)S(1)}, bf16[24,16,128]{2,1,0:T(8,128)(2,1)S(1)}, u32[]{:S(2)}, u32[]{:S(2)}) collective-permute-start(bf16[24,16,128]{2,1,0:T(8,128)(2,1)S(1)} %shard_map.50.before), channel_id=1, source_target_pairs={{0,8},{4,12},{8,0},{12,4},{1,9},{5,13},{9,1},{13,5},{2,10},{6,14},... | collective-permute-start | bytes 294920 | tf_op jit(solution)/shard_map/ppermute | solution.py:216
  16.8 6.3 %collective-permute-start.4 = (bf16[24,16,128]{2,1,0:T(8,128)(2,1)S(1)}, bf16[24,16,128]{2,1,0:T(8,128)(2,1)S(1)}, u32[]{:S(2)}, u32[]{:S(2)}) collective-permute-start(bf16[24,16,128]{2,1,0:T(8,128)(2,1)S(1)} %shard_map.52.refs_0_), channel_id=1, source_target_pairs={{0,4},{4,0},{8,12},{12,8},{1,5},{5,1},{9,13},{13,9},{2,6},{6,2},{1... | collective-permute-start | bytes 294920 | tf_op jit(solution)/shard_map/ppermute | solution.py:216
  18.3 6.6 %collective-permute-start.6 = (bf16[24,16,128]{2,1,0:T(8,128)(2,1)S(1)}, bf16[24,16,128]{2,1,0:T(8,128)(2,1)S(1)}, u32[]{:S(2)}, u32[]{:S(2)}) collective-permute-start(bf16[24,16,128]{2,1,0:T(8,128)(2,1)S(1)} %shard_map.54.before), channel_id=1, source_target_pairs={{0,12},{4,8},{8,4},{12,0},{1,13},{5,9},{9,5},{13,1},{2,14},{6,10},... | collective-permute-start | bytes 294920 | tf_op jit(solution)/shard_map/ppermute | solution.py:216
  18.8 6.1 %collective-permute-start.8 = (bf16[24,16,128]{2,1,0:T(8,128)(2,1)S(1)}, bf16[24,16,128]{2,1,0:T(8,128)(2,1)S(1)}, u32[]{:S(2)}, u32[]{:S(2)}) collective-permute-start(bf16[24,16,128]{2,1,0:T(8,128)(2,1)S(1)} %shard_map.56), channel_id=1, source_target_pairs={{0,2},{2,0},{1,3},{3,1},{4,6},{6,4},{5,7},{7,5},{8,10},{10,8},{9,1... | collective-permute-start | bytes 294920 | tf_op jit(solution)/shard_map/ppermute | solution.py:213

commit v10 on v9

--- a/solution.py
+++ b/solution.py
@@ -91,14 +91,12 @@
 
 
 def other_kernel(
-    early, other, table, left_rows, right_t, wave, own_acc, other_here, acc, sem
+    other, left_rows, right_t, wave, other_here, acc, sem
 ):
     rep, blk = lax.axis_index("rep"), lax.axis_index("blk")
     copy = pltpu.make_async_copy(other, other_here, sem)
     copy.start()
-    own_acc[...] = jnp.zeros_like(own_acc)
     acc[...] = jnp.zeros_like(acc)
-    add_list(table, rep, blk, left_rows, right_t, wave, own_acc, 0, early)
     copy.wait()
     add_list(other_here, rep, blk, left_rows, right_t, wave, acc)
 
@@ -111,10 +109,10 @@
     split_rows(acc, outs)
 
 
-def own_kernel(early, table, left_rows, right_t, wave, wave_pair, start, acc):
-    acc[...] = start[...]
+def own_kernel(table, left_rows, right_t, wave, wave_pair, acc):
+    acc[...] = jnp.zeros_like(acc)
     rep, blk = lax.axis_index("rep"), lax.axis_index("blk")
-    add_list(table, rep, blk, left_rows, right_t, wave, acc, early)
+    add_list(table, rep, blk, left_rows, right_t, wave, acc)
     add_list(table, 1 - rep, blk, left_rows, right_t, wave_pair, acc)
 
 
@@ -172,8 +170,6 @@
     table_other = lax.ppermute(slot_table, ("blk", "rep"), across)
     wave_pair = lax.ppermute(wavefunction, "rep", swap)
     acc_shape = shape((tiles + 1, op_count * rows, width), f32)
-    caps = slot_table.shape[-1]
-    early = caps // 8
     left_shape = shape((terms, op_count * rows, width), left_env.dtype)
     left_rows, right_t, wave, own_table = call(
         functools.partial(load_kernel, order),
@@ -191,12 +187,12 @@
             pltpu.SemaphoreType.DMA((2 + op_count + terms,)),
         ],
     )
-    acc, other_table, acc_other = call(
-        functools.partial(other_kernel, early),
-        (acc_shape, table_spec, acc_shape),
-        (table_other, own_table, left_rows, right_t, wave),
-        [ANY, SMEM] + [VMEM] * 3,
-        (VMEM, SMEM, VMEM),
+    other_table, acc_other = call(
+        other_kernel,
+        (table_spec, acc_shape),
+        (table_other, left_rows, right_t, wave),
+        [ANY] + [VMEM] * 3,
+        (SMEM, VMEM),
         scratch_shapes=[pltpu.SemaphoreType.DMA],
         cost_estimate=COSTLY,
     )
@@ -219,10 +215,10 @@
     got = [to_blk(x) for x in far]
     got_near = to_op(near, order[-2])
     acc = call(
-        functools.partial(own_kernel, early),
+        own_kernel,
         acc_shape,
-        (own_table, left_rows, right_t, wave, wave_pair, acc),
-        [SMEM] + [VMEM] * 5,
+        (own_table, left_rows, right_t, wave, wave_pair),
+        [SMEM] + [VMEM] * 4,
         VMEM,
     )
     total = call(

time: 25.9 us -> 25.8 us (level)
  no operation moved by 1% of the time
where the time goes in v10:
time: 25.8 us; the launch traced here: 25.6 us
  starting transfers between devices  12.8 us (50%)
  Pallas kernels  8.38 us (32%)
  waiting for transfers between devices  4.36 us (17%)
    pallas_call x12, Pallas kernels, call(): pl.pallas_call(kernel, out_shape=out_shape, in_specs=ins, out_specs=outs,...  8.38 us
    ppermute x4, starting transfers between devices, to_op(): return lax.ppermute(x, 'op', [(i, i ^ s) for i in range(op_count)])  6.16 us
    ppermute x4, waiting for transfers between devices, to_op(): return lax.ppermute(x, 'op', [(i, i ^ s) for i in range(op_count)])  4.35 us
    ppermute x3, starting transfers between devices, to_blk(): return lax.ppermute(x, 'blk', swap)  3.54 us
    ppermute x1, starting transfers between devices, at_source(): table_other = lax.ppermute(slot_table, ('blk', 'rep'), across)  2.38 us
    ppermute x1, starting transfers between devices, at_source(): wave_pair = lax.ppermute(wavefunction, 'rep', swap)  0.68 us
  transfers between devices with their start and end apart: 9, of which 3 were waited for; matrix products, arithmetic and copies ran while one was open for 0% of the time, Pallas kernels for 24%

profile of v10, /device:TPU:0, one launch (start us, length us, event | category | flops | bytes accessed | tf_op | source)
XLA Modules:
  0.0 25.6 jit_solution(14329537647315464814)
XLA Ops:
  0.0 2.4 %collective-permute-start.1 = (s32[3,1,1,2,2,64]{5,4,3,2,1,0:T(2,128)}, s32[3,1,1,2,2,64]{5,4,3,2,1,0:T(2,128)S(1)}, u32[]{:S(2)}, u32[]{:S(2)}) collective-permute-start(s32[3,1,1,2,2,64]{5,4,3,2,1,0:T(2,128)} %table.1), channel_id=1, source_target_pairs={{0,3},{1,2},{2,1},{3,0},{4,7},{5,6},{6,5},{7,4},{8,11},{9,10},{10,... | collective-permute-start | bytes 9224 | tf_op jit(solution)/shard_map/ppermute | solution.py:170
  2.4 0.7 %collective-permute-start = (bf16[12,128,128]{2,1,0:T(8,128)(2,1)}, bf16[12,128,128]{2,1,0:T(8,128)(2,1)S(1)}, u32[]{:S(2)}, u32[]{:S(2)}) collective-permute-start(bf16[12,128,128]{2,1,0:T(8,128)(2,1)} %wave.1), channel_id=1, source_target_pairs={{0,1},{1,0},{2,3},{3,2},{4,5},{5,4},{6,7},{7,6},{8,9},{9,8},{10,11... | collective-permute-start | bytes 1179656 | tf_op jit(solution)/shard_map/ppermute | solution.py:171
  3.1 1.8 %shard_map.46 = (bf16[32,64,128]{2,1,0:T(8,128)(2,1)S(1)}, bf16[32,128,128]{2,1,0:T(8,128)(2,1)S(1)}, bf16[12,128,128]{2,1,0:T(8,128)(2,1)S(1)}, s32[3,1,1,2,2,64]{5,4,3,2,1,0:T(2,128)S(4)}) custom-call(bf16[32,128,128]{2,1,0:T(8,128)(2,1)} %left.1, bf16[32,128,128]{2,1,0:T(8,128)(2,1)} %right.1, bf16[12,128,128]{2,1,0:T(8,128)(2,1)} %wave.1, ...), custom_call_target="tpu_custom_call" | custom-call | tf_op jit(solution)/shard_map/pallas_call | solution.py:151
  4.9 0.0 collective-permute-done.1.other
  4.9 1.9 %shard_map.48 = (s32[3,1,1,2,2,64]{5,4,3,2,1,0:T(2,128)S(4)}, f32[25,64,128]{2,1,0:T(8,128)S(1)}) custom-call(s32[3,1,1,2,2,64]{5,4,3,2,1,0:T(2,128)S(1)} %collective-permute-done.1.other, bf16[32,64,128]{2,1,0:T(8,128)(2,1)S(1)} %get-tuple-element.16.left_rows, bf16[32,128,128]{2,1,0:T(8,128)(2,1)S(1)} %get-tuple-element.17.right_t, ...), custom_call_target="tpu_custom_call" | custom-call | flops 10000000000 | bytes 10000000 | tf_op jit(solution)/shard_map/pallas_call | solution.py:151
  6.8 0.0 collective-permute-done.wave_pair
  6.8 1.3 %shard_map.49 = (bf16[24,16,128]{2,1,0:T(8,128)(2,1)S(1)}, bf16[24,16,128]{2,1,0:T(8,128)(2,1)S(1)}, bf16[24,16,128]{2,1,0:T(8,128)(2,1)S(1)}, f32[24,16,128]{2,1,0:T(8,128)S(1)}) custom-call(s32[3,1,1,2,2,64]{5,4,3,2,1,0:T(2,128)S(4)} %get-tuple-element.19.table, bf16[32,64,128]{2,1,0:T(8,128)(2,1)S(1)} %get-tuple-element.16.left_rows, ...), custom_call_target="tpu_custom_call" | custom-call | tf_op jit(solution)/shard_map/pallas_call | solution.py:151
  8.1 1.5 %collective-permute-start.2 = (bf16[24,16,128]{2,1,0:T(8,128)(2,1)S(1)}, bf16[24,16,128]{2,1,0:T(8,128)(2,1)S(1)}, u32[]{:S(2)}, u32[]{:S(2)}) collective-permute-start(bf16[24,16,128]{2,1,0:T(8,128)(2,1)S(1)} %get-tuple-element.21), channel_id=1, source_target_pairs={{0,2},{2,0},{1,3},{3,1},{4,6},{6,4},{5,7},{7,5},{8,10},{10,8},{9,1... | collective-permute-start | bytes 294920 | tf_op jit(solution)/shard_map/ppermute | solution.py:209
  9.6 0.6 %collective-permute-start.5 = (bf16[24,16,128]{2,1,0:T(8,128)(2,1)S(1)}, bf16[24,16,128]{2,1,0:T(8,128)(2,1)S(1)}, u32[]{:S(2)}, u32[]{:S(2)}) collective-permute-start(bf16[24,16,128]{2,1,0:T(8,128)(2,1)S(1)} %get-tuple-element.22), channel_id=1, source_target_pairs={{0,2},{2,0},{1,3},{3,1},{4,6},{6,4},{5,7},{7,5},{8,10},{10,8},{9,1... | collective-permute-start | bytes 294920 | tf_op jit(solution)/shard_map/ppermute | solution.py:209
  10.2 1.6 %collective-permute-start.7 = (bf16[24,16,128]{2,1,0:T(8,128)(2,1)S(1)}, bf16[24,16,128]{2,1,0:T(8,128)(2,1)S(1)}, u32[]{:S(2)}, u32[]{:S(2)}) collective-permute-start(bf16[24,16,128]{2,1,0:T(8,128)(2,1)S(1)} %get-tuple-element.24), channel_id=1, source_target_pairs={{0,4},{4,0},{8,12},{12,8},{1,5},{5,1},{9,13},{13,9},{2,6},{6,2},{1... | collective-permute-start | bytes 294920 | tf_op jit(solution)/shard_map/ppermute | solution.py:212
  11.8 2.4 %shard_map.47.acc = f32[25,64,128]{2,1,0:T(8,128)S(1)} custom-call(s32[3,1,1,2,2,64]{5,4,3,2,1,0:T(2,128)S(4)} %get-tuple-element.15.table, bf16[32,64,128]{2,1,0:T(8,128)(2,1)S(1)} %get-tuple-element.16.left_rows, bf16[32,128,128]{2,1,0:T(8,128)(2,1)S(1)} %get-tuple-element.17.right_t, bf16[12,128,128]{2,1,0:T(8,128)(2,1)S(1)} %get-tuple-element.18.wave, ...), custom_call_target="tpu_custom_call" | custom-call | tf_op jit(solution)/shard_map/pallas_call | solution.py:151
  14.2 0.0 collective-permute-done.2.got
  14.3 2.7 %collective-permute-start.3 = (bf16[24,16,128]{2,1,0:T(8,128)(2,1)S(1)}, bf16[24,16,128]{2,1,0:T(8,128)(2,1)S(1)}, u32[]{:S(2)}, u32[]{:S(2)}) collective-permute-start(bf16[24,16,128]{2,1,0:T(8,128)(2,1)S(1)} %shard_map.50.before), channel_id=1, source_target_pairs={{0,8},{4,12},{8,0},{12,4},{1,9},{5,13},{9,1},{13,5},{2,10},{6,14},... | collective-permute-start | bytes 294920 | tf_op jit(solution)/shard_map/ppermute | solution.py:212
  17.0 1.2 %collective-permute-start.4 = (bf16[24,16,128]{2,1,0:T(8,128)(2,1)S(1)}, bf16[24,16,128]{2,1,0:T(8,128)(2,1)S(1)}, u32[]{:S(2)}, u32[]{:S(2)}) collective-permute-start(bf16[24,16,128]{2,1,0:T(8,128)(2,1)S(1)} %shard_map.52.refs_0_), channel_id=1, source_target_pairs={{0,4},{4,0},{8,12},{12,8},{1,5},{5,1},{9,13},{13,9},{2,6},{6,2},{1... | collective-permute-start | bytes 294920 | tf_op jit(solution)/shard_map/ppermute | solution.py:212
  18.2 0.0 collective-permute-done.5.got
  18.2 0.7 %collective-permute-start.6 = (bf16[24,16,128]{2,1,0:T(8,128)(2,1)S(1)}, bf16[24,16,128]{2,1,0:T(8,128)(2,1)S(1)}, u32[]{:S(2)}, u32[]{:S(2)}) collective-permute-start(bf16[24,16,128]{2,1,0:T(8,128)(2,1)S(1)} %shard_map.54.before), channel_id=1, source_target_pairs={{0,12},{4,8},{8,4},{12,0},{1,13},{5,9},{9,5},{13,1},{2,14},{6,10},... | collective-permute-start | bytes 294920 | tf_op jit(solution)/shard_map/ppermute | solution.py:212
  18.9 0.0 collective-permute-done.7.got
  18.9 1.5 %collective-permute-start.8 = (bf16[24,16,128]{2,1,0:T(8,128)(2,1)S(1)}, bf16[24,16,128]{2,1,0:T(8,128)(2,1)S(1)}, u32[]{:S(2)}, u32[]{:S(2)}) collective-permute-start(bf16[24,16,128]{2,1,0:T(8,128)(2,1)S(1)} %shard_map.56), channel_id=1, source_target_pairs={{0,2},{2,0},{1,3},{3,1},{4,6},{6,4},{5,7},{7,5},{8,10},{10,8},{9,1... | collective-permute-start | bytes 294920 | tf_op jit(solution)/shard_map/ppermute | solution.py:209
  20.4 2.3 %collective-permute-done.3.got = bf16[24,16,128]{2,1,0:T(8,128)(2,1)S(1)} collective-permute-done((bf16[24,16,128]{2,1,0:T(8,128)(2,1)S(1)}, bf16[24,16,128]{2,1,0:T(8,128)(2,1)S(1)}, u32[]{:S(2)}, u32[]{:S(2)}) %collective-permute-start.3) | collective-permute-done | bytes 98336 | tf_op jit(solution)/shard_map/ppermute | solution.py:212
  22.7 0.5 %collective-permute-done.4.got = bf16[24,16,128]{2,1,0:T(8,128)(2,1)S(1)} collective-permute-done((bf16[24,16,128]{2,1,0:T(8,128)(2,1)S(1)}, bf16[24,16,128]{2,1,0:T(8,128)(2,1)S(1)}, u32[]{:S(2)}, u32[]{:S(2)}) %collective-permute-start.4) | collective-permute-done | bytes 98336 | tf_op jit(solution)/shard_map/ppermute | solution.py:212
  23.2 1.5 %collective-permute-done.6.got = bf16[24,16,128]{2,1,0:T(8,128)(2,1)S(1)} collective-permute-done((bf16[24,16,128]{2,1,0:T(8,128)(2,1)S(1)}, bf16[24,16,128]{2,1,0:T(8,128)(2,1)S(1)}, u32[]{:S(2)}, u32[]{:S(2)}) %collective-permute-start.6) | collective-permute-done | bytes 98336 | tf_op jit(solution)/shard_map/ppermute | solution.py:212
  24.8 0.0 collective-permute-done.8.got
  24.8 0.8 %shard_map.57 = f32[16,24,128]{2,1,0:T(8,128)} custom-call(f32[24,16,128]{2,1,0:T(8,128)S(1)} %shard_map.55.so_far, bf16[24,16,128]{2,1,0:T(8,128)(2,1)S(1)} %collective-permute-done.8.got), custom_call_target="tpu_custom_call" | custom-call | tf_op jit(solution)/shard_map/pallas_call | solution.py:151
  (7 shorter events, 0.1 us)
Async XLA Ops:
  0.0 4.9 %collective-permute-start.1 = (s32[3,1,1,2,2,64]{5,4,3,2,1,0:T(2,128)}, s32[3,1,1,2,2,64]{5,4,3,2,1,0:T(2,128)S(1)}, u32[]{:S(2)}, u32[]{:S(2)}) collective-permute-start(s32[3,1,1,2,2,64]{5,4,3,2,1,0:T(2,128)} %table.1), channel_id=1, source_target_pairs={{0,3},{1,2},{2,1},{3,0},{4,7},{5,6},{6,5},{7,4},{8,11},{9,10},{10,... | collective-permute-start | bytes 9224 | tf_op jit(solution)/shard_map/ppermute | solution.py:170
  2.4 4.4 %collective-permute-start = (bf16[12,128,128]{2,1,0:T(8,128)(2,1)}, bf16[12,128,128]{2,1,0:T(8,128)(2,1)S(1)}, u32[]{:S(2)}, u32[]{:S(2)}) collective-permute-start(bf16[12,128,128]{2,1,0:T(8,128)(2,1)} %wave.1), channel_id=1, source_target_pairs={{0,1},{1,0},{2,3},{3,2},{4,5},{5,4},{6,7},{7,6},{8,9},{9,8},{10,11... | collective-permute-start | bytes 1179656 | tf_op jit(solution)/shard_map/ppermute | solution.py:171
  8.1 6.1 %collective-permute-start.2 = (bf16[24,16,128]{2,1,0:T(8,128)(2,1)S(1)}, bf16[24,16,128]{2,1,0:T(8,128)(2,1)S(1)}, u32[]{:S(2)}, u32[]{:S(2)}) collective-permute-start(bf16[24,16,128]{2,1,0:T(8,128)(2,1)S(1)} %get-tuple-element.21), channel_id=1, source_target_pairs={{0,2},{2,0},{1,3},{3,1},{4,6},{6,4},{5,7},{7,5},{8,10},{10,8},{9,1... | collective-permute-start | bytes 294920 | tf_op jit(solution)/shard_map/ppermute | solution.py:209
  9.6 8.6 %collective-permute-start.5 = (bf16[24,16,128]{2,1,0:T(8,128)(2,1)S(1)}, bf16[24,16,128]{2,1,0:T(8,128)(2,1)S(1)}, u32[]{:S(2)}, u32[]{:S(2)}) collective-permute-start(bf16[24,16,128]{2,1,0:T(8,128)(2,1)S(1)} %get-tuple-element.22), channel_id=1, source_target_pairs={{0,2},{2,0},{1,3},{3,1},{4,6},{6,4},{5,7},{7,5},{8,10},{10,8},{9,1... | collective-permute-start | bytes 294920 | tf_op jit(solution)/shard_map/ppermute | solution.py:209
  10.2 8.7 %collective-permute-start.7 = (bf16[24,16,128]{2,1,0:T(8,128)(2,1)S(1)}, bf16[24,16,128]{2,1,0:T(8,128)(2,1)S(1)}, u32[]{:S(2)}, u32[]{:S(2)}) collective-permute-start(bf16[24,16,128]{2,1,0:T(8,128)(2,1)S(1)} %get-tuple-element.24), channel_id=1, source_target_pairs={{0,4},{4,0},{8,12},{12,8},{1,5},{5,1},{9,13},{13,9},{2,6},{6,2},{1... | collective-permute-start | bytes 294920 | tf_op jit(solution)/shard_map/ppermute | solution.py:212
  14.3 8.4 %collective-permute-start.3 = (bf16[24,16,128]{2,1,0:T(8,128)(2,1)S(1)}, bf16[24,16,128]{2,1,0:T(8,128)(2,1)S(1)}, u32[]{:S(2)}, u32[]{:S(2)}) collective-permute-start(bf16[24,16,128]{2,1,0:T(8,128)(2,1)S(1)} %shard_map.50.before), channel_id=1, source_target_pairs={{0,8},{4,12},{8,0},{12,4},{1,9},{5,13},{9,1},{13,5},{2,10},{6,14},... | collective-permute-start | bytes 294920 | tf_op jit(solution)/shard_map/ppermute | solution.py:212
  17.0 6.3 %collective-permute-start.4 = (bf16[24,16,128]{2,1,0:T(8,128)(2,1)S(1)}, bf16[24,16,128]{2,1,0:T(8,128)(2,1)S(1)}, u32[]{:S(2)}, u32[]{:S(2)}) collective-permute-start(bf16[24,16,128]{2,1,0:T(8,128)(2,1)S(1)} %shard_map.52.refs_0_), channel_id=1, source_target_pairs={{0,4},{4,0},{8,12},{12,8},{1,5},{5,1},{9,13},{13,9},{2,6},{6,2},{1... | collective-permute-start | bytes 294920 | tf_op jit(solution)/shard_map/ppermute | solution.py:212
  18.2 6.6 %collective-permute-start.6 = (bf16[24,16,128]{2,1,0:T(8,128)(2,1)S(1)}, bf16[24,16,128]{2,1,0:T(8,128)(2,1)S(1)}, u32[]{:S(2)}, u32[]{:S(2)}) collective-permute-start(bf16[24,16,128]{2,1,0:T(8,128)(2,1)S(1)} %shard_map.54.before), channel_id=1, source_target_pairs={{0,12},{4,8},{8,4},{12,0},{1,13},{5,9},{9,5},{13,1},{2,14},{6,10},... | collective-permute-start | bytes 294920 | tf_op jit(solution)/shard_map/ppermute | solution.py:212
  18.9 5.9 %collective-permute-start.8 = (bf16[24,16,128]{2,1,0:T(8,128)(2,1)S(1)}, bf16[24,16,128]{2,1,0:T(8,128)(2,1)S(1)}, u32[]{:S(2)}, u32[]{:S(2)}) collective-permute-start(bf16[24,16,128]{2,1,0:T(8,128)(2,1)S(1)} %shard_map.56), channel_id=1, source_target_pairs={{0,2},{2,0},{1,3},{3,1},{4,6},{6,4},{5,7},{7,5},{8,10},{10,8},{9,1... | collective-permute-start | bytes 294920 | tf_op jit(solution)/shard_map/ppermute | solution.py:209

commit v11 on v10

--- a/solution.py
+++ b/solution.py
@@ -11,6 +11,7 @@
 SMEM = pl.BlockSpec(memory_space=pltpu.SMEM)
 ANY = pl.BlockSpec(memory_space=pl.ANY)
 LINK = jnp.bfloat16
+BEHIND = 16
 STEP = pl.CostEstimate(flops=3 * 10**9, bytes_accessed=3 * 10**6, transcendentals=0)
 COSTLY = pl.CostEstimate(flops=10**10, bytes_accessed=10**7, transcendentals=0)
 
@@ -34,20 +35,19 @@
     def body(step, carry):
         slots = [begin + step * unroll + q for q in range(unroll)]
         terms = [table[0, 0, 0, rep, src, c] for c in slots]
-        inner = [
-            jnp.dot(
-                left[terms[q]],
-                wave[table[2, 0, 0, rep, src, slots[q]]],
-                preferred_element_type=jnp.float32,
-            ).astype(jnp.bfloat16)
-            for q in range(unroll)
-        ]
-        outer = [
-            jnp.dot(inner[q], right_t[terms[q]], preferred_element_type=jnp.float32)
-            for q in range(unroll)
-        ]
-        for q in range(unroll):
-            acc[table[1, 0, 0, rep, src, slots[q]]] += outer[q]
+        inner = {}
+        for q in range(unroll + BEHIND):
+            if q < unroll:
+                inner[q] = jnp.dot(
+                    left[terms[q]],
+                    wave[table[2, 0, 0, rep, src, slots[q]]],
+                    preferred_element_type=jnp.float32,
+                ).astype(jnp.bfloat16)
+            p = q - BEHIND
+            if p >= 0:
+                acc[table[1, 0, 0, rep, src, slots[p]]] += jnp.dot(
+                    inner.pop(p), right_t[terms[p]], preferred_element_type=jnp.float32
+                )
         return carry
 
     if unroll:

time: 25.8 us -> 25.8 us (level)
  no operation moved by 1% of the time
where the time goes in v11:
time: 25.8 us; the launch traced here: 25.6 us
  starting transfers between devices  12.8 us (50%)
  Pallas kernels  8.29 us (32%)
  waiting for transfers between devices  4.43 us (17%)
    pallas_call x12, Pallas kernels, call(): pl.pallas_call(kernel, out_shape=out_shape, in_specs=ins, out_specs=outs,...  8.29 us
    ppermute x4, starting transfers between devices, to_op(): return lax.ppermute(x, 'op', [(i, i ^ s) for i in range(op_count)])  6.16 us
    ppermute x4, waiting for transfers between devices, to_op(): return lax.ppermute(x, 'op', [(i, i ^ s) for i in range(op_count)])  4.42 us
    ppermute x3, starting transfers between devices, to_blk(): return lax.ppermute(x, 'blk', swap)  3.54 us
    ppermute x1, starting transfers between devices, at_source(): table_other = lax.ppermute(slot_table, ('blk', 'rep'), across)  2.38 us
    ppermute x1, starting transfers between devices, at_source(): wave_pair = lax.ppermute(wavefunction, 'rep', swap)  0.68 us
  transfers between devices with their start and end apart: 9, of which 3 were waited for; matrix products, arithmetic and copies ran while one was open for 0% of the time, Pallas kernels for 24%

profile of v11, /device:TPU:0, one launch (start us, length us, event | category | flops | bytes accessed | tf_op | source)
XLA Modules:
  0.0 25.6 jit_solution(12715264147838465659)
XLA Ops:
  0.0 2.4 %collective-permute-start.1 = (s32[3,1,1,2,2,64]{5,4,3,2,1,0:T(2,128)}, s32[3,1,1,2,2,64]{5,4,3,2,1,0:T(2,128)S(1)}, u32[]{:S(2)}, u32[]{:S(2)}) collective-permute-start(s32[3,1,1,2,2,64]{5,4,3,2,1,0:T(2,128)} %table.1), channel_id=1, source_target_pairs={{0,3},{1,2},{2,1},{3,0},{4,7},{5,6},{6,5},{7,4},{8,11},{9,10},{10,... | collective-permute-start | bytes 9224 | tf_op jit(solution)/shard_map/ppermute | solution.py:170
  2.4 0.7 %collective-permute-start = (bf16[12,128,128]{2,1,0:T(8,128)(2,1)}, bf16[12,128,128]{2,1,0:T(8,128)(2,1)S(1)}, u32[]{:S(2)}, u32[]{:S(2)}) collective-permute-start(bf16[12,128,128]{2,1,0:T(8,128)(2,1)} %wave.1), channel_id=1, source_target_pairs={{0,1},{1,0},{2,3},{3,2},{4,5},{5,4},{6,7},{7,6},{8,9},{9,8},{10,11... | collective-permute-start | bytes 1179656 | tf_op jit(solution)/shard_map/ppermute | solution.py:171
  3.1 1.8 %shard_map.46 = (bf16[32,64,128]{2,1,0:T(8,128)(2,1)S(1)}, bf16[32,128,128]{2,1,0:T(8,128)(2,1)S(1)}, bf16[12,128,128]{2,1,0:T(8,128)(2,1)S(1)}, s32[3,1,1,2,2,64]{5,4,3,2,1,0:T(2,128)S(4)}) custom-call(bf16[32,128,128]{2,1,0:T(8,128)(2,1)} %left.1, bf16[32,128,128]{2,1,0:T(8,128)(2,1)} %right.1, bf16[12,128,128]{2,1,0:T(8,128)(2,1)} %wave.1, ...), custom_call_target="tpu_custom_call" | custom-call | tf_op jit(solution)/shard_map/pallas_call | solution.py:151
  4.9 0.0 collective-permute-done.1.other
  4.9 1.9 %shard_map.48 = (s32[3,1,1,2,2,64]{5,4,3,2,1,0:T(2,128)S(4)}, f32[25,64,128]{2,1,0:T(8,128)S(1)}) custom-call(s32[3,1,1,2,2,64]{5,4,3,2,1,0:T(2,128)S(1)} %collective-permute-done.1.other, bf16[32,64,128]{2,1,0:T(8,128)(2,1)S(1)} %get-tuple-element.16.left_rows, bf16[32,128,128]{2,1,0:T(8,128)(2,1)S(1)} %get-tuple-element.17.right_t, ...), custom_call_target="tpu_custom_call" | custom-call | flops 10000000000 | bytes 10000000 | tf_op jit(solution)/shard_map/pallas_call | solution.py:151
  6.8 0.0 collective-permute-done.wave_pair
  6.8 1.3 %shard_map.49 = (bf16[24,16,128]{2,1,0:T(8,128)(2,1)S(1)}, bf16[24,16,128]{2,1,0:T(8,128)(2,1)S(1)}, bf16[24,16,128]{2,1,0:T(8,128)(2,1)S(1)}, f32[24,16,128]{2,1,0:T(8,128)S(1)}) custom-call(s32[3,1,1,2,2,64]{5,4,3,2,1,0:T(2,128)S(4)} %get-tuple-element.19.table, bf16[32,64,128]{2,1,0:T(8,128)(2,1)S(1)} %get-tuple-element.16.left_rows, ...), custom_call_target="tpu_custom_call" | custom-call | tf_op jit(solution)/shard_map/pallas_call | solution.py:151
  8.1 1.5 %collective-permute-start.2 = (bf16[24,16,128]{2,1,0:T(8,128)(2,1)S(1)}, bf16[24,16,128]{2,1,0:T(8,128)(2,1)S(1)}, u32[]{:S(2)}, u32[]{:S(2)}) collective-permute-start(bf16[24,16,128]{2,1,0:T(8,128)(2,1)S(1)} %get-tuple-element.21), channel_id=1, source_target_pairs={{0,2},{2,0},{1,3},{3,1},{4,6},{6,4},{5,7},{7,5},{8,10},{10,8},{9,1... | collective-permute-start | bytes 294920 | tf_op jit(solution)/shard_map/ppermute | solution.py:209
  9.6 0.6 %collective-permute-start.5 = (bf16[24,16,128]{2,1,0:T(8,128)(2,1)S(1)}, bf16[24,16,128]{2,1,0:T(8,128)(2,1)S(1)}, u32[]{:S(2)}, u32[]{:S(2)}) collective-permute-start(bf16[24,16,128]{2,1,0:T(8,128)(2,1)S(1)} %get-tuple-element.22), channel_id=1, source_target_pairs={{0,2},{2,0},{1,3},{3,1},{4,6},{6,4},{5,7},{7,5},{8,10},{10,8},{9,1... | collective-permute-start | bytes 294920 | tf_op jit(solution)/shard_map/ppermute | solution.py:209
  10.2 1.6 %collective-permute-start.7 = (bf16[24,16,128]{2,1,0:T(8,128)(2,1)S(1)}, bf16[24,16,128]{2,1,0:T(8,128)(2,1)S(1)}, u32[]{:S(2)}, u32[]{:S(2)}) collective-permute-start(bf16[24,16,128]{2,1,0:T(8,128)(2,1)S(1)} %get-tuple-element.24), channel_id=1, source_target_pairs={{0,4},{4,0},{8,12},{12,8},{1,5},{5,1},{9,13},{13,9},{2,6},{6,2},{1... | collective-permute-start | bytes 294920 | tf_op jit(solution)/shard_map/ppermute | solution.py:212
  11.8 2.4 %shard_map.47.acc = f32[25,64,128]{2,1,0:T(8,128)S(1)} custom-call(s32[3,1,1,2,2,64]{5,4,3,2,1,0:T(2,128)S(4)} %get-tuple-element.15.table, bf16[32,64,128]{2,1,0:T(8,128)(2,1)S(1)} %get-tuple-element.16.left_rows, bf16[32,128,128]{2,1,0:T(8,128)(2,1)S(1)} %get-tuple-element.17.right_t, bf16[12,128,128]{2,1,0:T(8,128)(2,1)S(1)} %get-tuple-element.18.wave, ...), custom_call_target="tpu_custom_call" | custom-call | tf_op jit(solution)/shard_map/pallas_call | solution.py:151
  14.1 0.0 collective-permute-done.2.got
  14.2 2.7 %collective-permute-start.3 = (bf16[24,16,128]{2,1,0:T(8,128)(2,1)S(1)}, bf16[24,16,128]{2,1,0:T(8,128)(2,1)S(1)}, u32[]{:S(2)}, u32[]{:S(2)}) collective-permute-start(bf16[24,16,128]{2,1,0:T(8,128)(2,1)S(1)} %shard_map.50.before), channel_id=1, source_target_pairs={{0,8},{4,12},{8,0},{12,4},{1,9},{5,13},{9,1},{13,5},{2,10},{6,14},... | collective-permute-start | bytes 294920 | tf_op jit(solution)/shard_map/ppermute | solution.py:212
  16.9 1.3 %collective-permute-start.4 = (bf16[24,16,128]{2,1,0:T(8,128)(2,1)S(1)}, bf16[24,16,128]{2,1,0:T(8,128)(2,1)S(1)}, u32[]{:S(2)}, u32[]{:S(2)}) collective-permute-start(bf16[24,16,128]{2,1,0:T(8,128)(2,1)S(1)} %shard_map.52.refs_0_), channel_id=1, source_target_pairs={{0,4},{4,0},{8,12},{12,8},{1,5},{5,1},{9,13},{13,9},{2,6},{6,2},{1... | collective-permute-start | bytes 294920 | tf_op jit(solution)/shard_map/ppermute | solution.py:212
  18.1 0.0 collective-permute-done.5.got
  18.2 0.6 %collective-permute-start.6 = (bf16[24,16,128]{2,1,0:T(8,128)(2,1)S(1)}, bf16[24,16,128]{2,1,0:T(8,128)(2,1)S(1)}, u32[]{:S(2)}, u32[]{:S(2)}) collective-permute-start(bf16[24,16,128]{2,1,0:T(8,128)(2,1)S(1)} %shard_map.54.before), channel_id=1, source_target_pairs={{0,12},{4,8},{8,4},{12,0},{1,13},{5,9},{9,5},{13,1},{2,14},{6,10},... | collective-permute-start | bytes 294920 | tf_op jit(solution)/shard_map/ppermute | solution.py:212
  18.8 0.0 collective-permute-done.7.got
  18.8 1.5 %collective-permute-start.8 = (bf16[24,16,128]{2,1,0:T(8,128)(2,1)S(1)}, bf16[24,16,128]{2,1,0:T(8,128)(2,1)S(1)}, u32[]{:S(2)}, u32[]{:S(2)}) collective-permute-start(bf16[24,16,128]{2,1,0:T(8,128)(2,1)S(1)} %shard_map.56), channel_id=1, source_target_pairs={{0,2},{2,0},{1,3},{3,1},{4,6},{6,4},{5,7},{7,5},{8,10},{10,8},{9,1... | collective-permute-start | bytes 294920 | tf_op jit(solution)/shard_map/ppermute | solution.py:209
  20.3 2.4 %collective-permute-done.3.got = bf16[24,16,128]{2,1,0:T(8,128)(2,1)S(1)} collective-permute-done((bf16[24,16,128]{2,1,0:T(8,128)(2,1)S(1)}, bf16[24,16,128]{2,1,0:T(8,128)(2,1)S(1)}, u32[]{:S(2)}, u32[]{:S(2)}) %collective-permute-start.3) | collective-permute-done | bytes 98336 | tf_op jit(solution)/shard_map/ppermute | solution.py:212
  22.7 0.5 %collective-permute-done.4.got = bf16[24,16,128]{2,1,0:T(8,128)(2,1)S(1)} collective-permute-done((bf16[24,16,128]{2,1,0:T(8,128)(2,1)S(1)}, bf16[24,16,128]{2,1,0:T(8,128)(2,1)S(1)}, u32[]{:S(2)}, u32[]{:S(2)}) %collective-permute-start.4) | collective-permute-done | bytes 98336 | tf_op jit(solution)/shard_map/ppermute | solution.py:212
  23.2 1.6 %collective-permute-done.6.got = bf16[24,16,128]{2,1,0:T(8,128)(2,1)S(1)} collective-permute-done((bf16[24,16,128]{2,1,0:T(8,128)(2,1)S(1)}, bf16[24,16,128]{2,1,0:T(8,128)(2,1)S(1)}, u32[]{:S(2)}, u32[]{:S(2)}) %collective-permute-start.6) | collective-permute-done | bytes 98336 | tf_op jit(solution)/shard_map/ppermute | solution.py:212
  24.8 0.0 collective-permute-done.8.got
  24.8 0.8 %shard_map.57 = f32[16,24,128]{2,1,0:T(8,128)} custom-call(f32[24,16,128]{2,1,0:T(8,128)S(1)} %shard_map.55.so_far, bf16[24,16,128]{2,1,0:T(8,128)(2,1)S(1)} %collective-permute-done.8.got), custom_call_target="tpu_custom_call" | custom-call | tf_op jit(solution)/shard_map/pallas_call | solution.py:151
  (7 shorter events, 0.1 us)
Async XLA Ops:
  0.0 4.9 %collective-permute-start.1 = (s32[3,1,1,2,2,64]{5,4,3,2,1,0:T(2,128)}, s32[3,1,1,2,2,64]{5,4,3,2,1,0:T(2,128)S(1)}, u32[]{:S(2)}, u32[]{:S(2)}) collective-permute-start(s32[3,1,1,2,2,64]{5,4,3,2,1,0:T(2,128)} %table.1), channel_id=1, source_target_pairs={{0,3},{1,2},{2,1},{3,0},{4,7},{5,6},{6,5},{7,4},{8,11},{9,10},{10,... | collective-permute-start | bytes 9224 | tf_op jit(solution)/shard_map/ppermute | solution.py:170
  2.4 4.4 %collective-permute-start = (bf16[12,128,128]{2,1,0:T(8,128)(2,1)}, bf16[12,128,128]{2,1,0:T(8,128)(2,1)S(1)}, u32[]{:S(2)}, u32[]{:S(2)}) collective-permute-start(bf16[12,128,128]{2,1,0:T(8,128)(2,1)} %wave.1), channel_id=1, source_target_pairs={{0,1},{1,0},{2,3},{3,2},{4,5},{5,4},{6,7},{7,6},{8,9},{9,8},{10,11... | collective-permute-start | bytes 1179656 | tf_op jit(solution)/shard_map/ppermute | solution.py:171
  8.1 6.0 %collective-permute-start.2 = (bf16[24,16,128]{2,1,0:T(8,128)(2,1)S(1)}, bf16[24,16,128]{2,1,0:T(8,128)(2,1)S(1)}, u32[]{:S(2)}, u32[]{:S(2)}) collective-permute-start(bf16[24,16,128]{2,1,0:T(8,128)(2,1)S(1)} %get-tuple-element.21), channel_id=1, source_target_pairs={{0,2},{2,0},{1,3},{3,1},{4,6},{6,4},{5,7},{7,5},{8,10},{10,8},{9,1... | collective-permute-start | bytes 294920 | tf_op jit(solution)/shard_map/ppermute | solution.py:209
  9.6 8.6 %collective-permute-start.5 = (bf16[24,16,128]{2,1,0:T(8,128)(2,1)S(1)}, bf16[24,16,128]{2,1,0:T(8,128)(2,1)S(1)}, u32[]{:S(2)}, u32[]{:S(2)}) collective-permute-start(bf16[24,16,128]{2,1,0:T(8,128)(2,1)S(1)} %get-tuple-element.22), channel_id=1, source_target_pairs={{0,2},{2,0},{1,3},{3,1},{4,6},{6,4},{5,7},{7,5},{8,10},{10,8},{9,1... | collective-permute-start | bytes 294920 | tf_op jit(solution)/shard_map/ppermute | solution.py:209
  10.2 8.6 %collective-permute-start.7 = (bf16[24,16,128]{2,1,0:T(8,128)(2,1)S(1)}, bf16[24,16,128]{2,1,0:T(8,128)(2,1)S(1)}, u32[]{:S(2)}, u32[]{:S(2)}) collective-permute-start(bf16[24,16,128]{2,1,0:T(8,128)(2,1)S(1)} %get-tuple-element.24), channel_id=1, source_target_pairs={{0,4},{4,0},{8,12},{12,8},{1,5},{5,1},{9,13},{13,9},{2,6},{6,2},{1... | collective-permute-start | bytes 294920 | tf_op jit(solution)/shard_map/ppermute | solution.py:212
  14.2 8.5 %collective-permute-start.3 = (bf16[24,16,128]{2,1,0:T(8,128)(2,1)S(1)}, bf16[24,16,128]{2,1,0:T(8,128)(2,1)S(1)}, u32[]{:S(2)}, u32[]{:S(2)}) collective-permute-start(bf16[24,16,128]{2,1,0:T(8,128)(2,1)S(1)} %shard_map.50.before), channel_id=1, source_target_pairs={{0,8},{4,12},{8,0},{12,4},{1,9},{5,13},{9,1},{13,5},{2,10},{6,14},... | collective-permute-start | bytes 294920 | tf_op jit(solution)/shard_map/ppermute | solution.py:212
  16.9 6.3 %collective-permute-start.4 = (bf16[24,16,128]{2,1,0:T(8,128)(2,1)S(1)}, bf16[24,16,128]{2,1,0:T(8,128)(2,1)S(1)}, u32[]{:S(2)}, u32[]{:S(2)}) collective-permute-start(bf16[24,16,128]{2,1,0:T(8,128)(2,1)S(1)} %shard_map.52.refs_0_), channel_id=1, source_target_pairs={{0,4},{4,0},{8,12},{12,8},{1,5},{5,1},{9,13},{13,9},{2,6},{6,2},{1... | collective-permute-start | bytes 294920 | tf_op jit(solution)/shard_map/ppermute | solution.py:212
  18.2 6.6 %collective-permute-start.6 = (bf16[24,16,128]{2,1,0:T(8,128)(2,1)S(1)}, bf16[24,16,128]{2,1,0:T(8,128)(2,1)S(1)}, u32[]{:S(2)}, u32[]{:S(2)}) collective-permute-start(bf16[24,16,128]{2,1,0:T(8,128)(2,1)S(1)} %shard_map.54.before), channel_id=1, source_target_pairs={{0,12},{4,8},{8,4},{12,0},{1,13},{5,9},{9,5},{13,1},{2,14},{6,10},... | collective-permute-start | bytes 294920 | tf_op jit(solution)/shard_map/ppermute | solution.py:212
  18.8 5.9 %collective-permute-start.8 = (bf16[24,16,128]{2,1,0:T(8,128)(2,1)S(1)}, bf16[24,16,128]{2,1,0:T(8,128)(2,1)S(1)}, u32[]{:S(2)}, u32[]{:S(2)}) collective-permute-start(bf16[24,16,128]{2,1,0:T(8,128)(2,1)S(1)} %shard_map.56), channel_id=1, source_target_pairs={{0,2},{2,0},{1,3},{3,1},{4,6},{6,4},{5,7},{7,5},{8,10},{10,8},{9,1... | collective-permute-start | bytes 294920 | tf_op jit(solution)/shard_map/ppermute | solution.py:209

commit v12 on v11

--- a/solution.py
+++ b/solution.py
@@ -61,7 +61,7 @@
     rep, op = lax.axis_index("rep"), lax.axis_index("op")
     rows = left_rows.shape[1] // len(order)
     count = right_t.shape[0]
-    part = next(p for p in (8, 4, 2, 1) if count % p == 0)
+    part = next(p for p in (16, 8, 4, 2, 1) if count % p == 0)
     moves = [(table, table_here)]
     for k in range(0, count, part):
         moves.append((right.at[pl.ds(k, part)], right_here.at[pl.ds(k, part)]))

time: 25.8 us -> 25.8 us (level)
  no operation moved by 1% of the time
where the time goes in v12:
time: 25.8 us; the launch traced here: 25.6 us
  starting transfers between devices  12.8 us (50%)
  Pallas kernels  8.29 us (32%)
  waiting for transfers between devices  4.4 us (17%)
    pallas_call x12, Pallas kernels, call(): pl.pallas_call(kernel, out_shape=out_shape, in_specs=ins, out_specs=outs,...  8.29 us
    ppermute x4, starting transfers between devices, to_op(): return lax.ppermute(x, 'op', [(i, i ^ s) for i in range(op_count)])  6.17 us
    ppermute x4, waiting for transfers between devices, to_op(): return lax.ppermute(x, 'op', [(i, i ^ s) for i in range(op_count)])  4.38 us
    ppermute x3, starting transfers between devices, to_blk(): return lax.ppermute(x, 'blk', swap)  3.54 us
    ppermute x1, starting transfers between devices, at_source(): table_other = lax.ppermute(slot_table, ('blk', 'rep'), across)  2.38 us
    ppermute x1, starting transfers between devices, at_source(): wave_pair = lax.ppermute(wavefunction, 'rep', swap)  0.68 us
  transfers between devices with their start and end apart: 9, of which 3 were waited for; matrix products, arithmetic and copies ran while one was open for 0% of the time, Pallas kernels for 24%

profile of v12, /device:TPU:0, one launch (start us, length us, event | category | flops | bytes accessed | tf_op | source)
XLA Modules:
  0.0 25.6 jit_solution(159934680994935330)
XLA Ops:
  0.0 2.4 %collective-permute-start.1 = (s32[3,1,1,2,2,64]{5,4,3,2,1,0:T(2,128)}, s32[3,1,1,2,2,64]{5,4,3,2,1,0:T(2,128)S(1)}, u32[]{:S(2)}, u32[]{:S(2)}) collective-permute-start(s32[3,1,1,2,2,64]{5,4,3,2,1,0:T(2,128)} %table.1), channel_id=1, source_target_pairs={{0,3},{1,2},{2,1},{3,0},{4,7},{5,6},{6,5},{7,4},{8,11},{9,10},{10,... | collective-permute-start | bytes 9224 | tf_op jit(solution)/shard_map/ppermute | solution.py:170
  2.4 0.7 %collective-permute-start = (bf16[12,128,128]{2,1,0:T(8,128)(2,1)}, bf16[12,128,128]{2,1,0:T(8,128)(2,1)S(1)}, u32[]{:S(2)}, u32[]{:S(2)}) collective-permute-start(bf16[12,128,128]{2,1,0:T(8,128)(2,1)} %wave.1), channel_id=1, source_target_pairs={{0,1},{1,0},{2,3},{3,2},{4,5},{5,4},{6,7},{7,6},{8,9},{9,8},{10,11... | collective-permute-start | bytes 1179656 | tf_op jit(solution)/shard_map/ppermute | solution.py:171
  3.1 1.8 %shard_map.46 = (bf16[32,64,128]{2,1,0:T(8,128)(2,1)S(1)}, bf16[32,128,128]{2,1,0:T(8,128)(2,1)S(1)}, bf16[12,128,128]{2,1,0:T(8,128)(2,1)S(1)}, s32[3,1,1,2,2,64]{5,4,3,2,1,0:T(2,128)S(4)}) custom-call(bf16[32,128,128]{2,1,0:T(8,128)(2,1)} %left.1, bf16[32,128,128]{2,1,0:T(8,128)(2,1)} %right.1, bf16[12,128,128]{2,1,0:T(8,128)(2,1)} %wave.1, ...), custom_call_target="tpu_custom_call" | custom-call | tf_op jit(solution)/shard_map/pallas_call | solution.py:151
  4.9 0.0 collective-permute-done.1.other
  4.9 1.9 %shard_map.48 = (s32[3,1,1,2,2,64]{5,4,3,2,1,0:T(2,128)S(4)}, f32[25,64,128]{2,1,0:T(8,128)S(1)}) custom-call(s32[3,1,1,2,2,64]{5,4,3,2,1,0:T(2,128)S(1)} %collective-permute-done.1.other, bf16[32,64,128]{2,1,0:T(8,128)(2,1)S(1)} %get-tuple-element.16.left_rows, bf16[32,128,128]{2,1,0:T(8,128)(2,1)S(1)} %get-tuple-element.17.right_t, ...), custom_call_target="tpu_custom_call" | custom-call | flops 10000000000 | bytes 10000000 | tf_op jit(solution)/shard_map/pallas_call | solution.py:151
  6.8 0.0 collective-permute-done.wave_pair
  6.8 1.3 %shard_map.49 = (bf16[24,16,128]{2,1,0:T(8,128)(2,1)S(1)}, bf16[24,16,128]{2,1,0:T(8,128)(2,1)S(1)}, bf16[24,16,128]{2,1,0:T(8,128)(2,1)S(1)}, f32[24,16,128]{2,1,0:T(8,128)S(1)}) custom-call(s32[3,1,1,2,2,64]{5,4,3,2,1,0:T(2,128)S(4)} %get-tuple-element.19.table, bf16[32,64,128]{2,1,0:T(8,128)(2,1)S(1)} %get-tuple-element.16.left_rows, ...), custom_call_target="tpu_custom_call" | custom-call | tf_op jit(solution)/shard_map/pallas_call | solution.py:151
  8.1 1.5 %collective-permute-start.2 = (bf16[24,16,128]{2,1,0:T(8,128)(2,1)S(1)}, bf16[24,16,128]{2,1,0:T(8,128)(2,1)S(1)}, u32[]{:S(2)}, u32[]{:S(2)}) collective-permute-start(bf16[24,16,128]{2,1,0:T(8,128)(2,1)S(1)} %get-tuple-element.21), channel_id=1, source_target_pairs={{0,2},{2,0},{1,3},{3,1},{4,6},{6,4},{5,7},{7,5},{8,10},{10,8},{9,1... | collective-permute-start | bytes 294920 | tf_op jit(solution)/shard_map/ppermute | solution.py:209
  9.6 0.6 %collective-permute-start.5 = (bf16[24,16,128]{2,1,0:T(8,128)(2,1)S(1)}, bf16[24,16,128]{2,1,0:T(8,128)(2,1)S(1)}, u32[]{:S(2)}, u32[]{:S(2)}) collective-permute-start(bf16[24,16,128]{2,1,0:T(8,128)(2,1)S(1)} %get-tuple-element.22), channel_id=1, source_target_pairs={{0,2},{2,0},{1,3},{3,1},{4,6},{6,4},{5,7},{7,5},{8,10},{10,8},{9,1... | collective-permute-start | bytes 294920 | tf_op jit(solution)/shard_map/ppermute | solution.py:209
  10.2 1.6 %collective-permute-start.7 = (bf16[24,16,128]{2,1,0:T(8,128)(2,1)S(1)}, bf16[24,16,128]{2,1,0:T(8,128)(2,1)S(1)}, u32[]{:S(2)}, u32[]{:S(2)}) collective-permute-start(bf16[24,16,128]{2,1,0:T(8,128)(2,1)S(1)} %get-tuple-element.24), channel_id=1, source_target_pairs={{0,4},{4,0},{8,12},{12,8},{1,5},{5,1},{9,13},{13,9},{2,6},{6,2},{1... | collective-permute-start | bytes 294920 | tf_op jit(solution)/shard_map/ppermute | solution.py:212
  11.8 2.4 %shard_map.47.acc = f32[25,64,128]{2,1,0:T(8,128)S(1)} custom-call(s32[3,1,1,2,2,64]{5,4,3,2,1,0:T(2,128)S(4)} %get-tuple-element.15.table, bf16[32,64,128]{2,1,0:T(8,128)(2,1)S(1)} %get-tuple-element.16.left_rows, bf16[32,128,128]{2,1,0:T(8,128)(2,1)S(1)} %get-tuple-element.17.right_t, bf16[12,128,128]{2,1,0:T(8,128)(2,1)S(1)} %get-tuple-element.18.wave, ...), custom_call_target="tpu_custom_call" | custom-call | tf_op jit(solution)/shard_map/pallas_call | solution.py:151
  14.2 0.0 collective-permute-done.2.got
  14.2 2.6 %collective-permute-start.3 = (bf16[24,16,128]{2,1,0:T(8,128)(2,1)S(1)}, bf16[24,16,128]{2,1,0:T(8,128)(2,1)S(1)}, u32[]{:S(2)}, u32[]{:S(2)}) collective-permute-start(bf16[24,16,128]{2,1,0:T(8,128)(2,1)S(1)} %shard_map.50.before), channel_id=1, source_target_pairs={{0,8},{4,12},{8,0},{12,4},{1,9},{5,13},{9,1},{13,5},{2,10},{6,14},... | collective-permute-start | bytes 294920 | tf_op jit(solution)/shard_map/ppermute | solution.py:212
  16.9 1.3 %collective-permute-start.4 = (bf16[24,16,128]{2,1,0:T(8,128)(2,1)S(1)}, bf16[24,16,128]{2,1,0:T(8,128)(2,1)S(1)}, u32[]{:S(2)}, u32[]{:S(2)}) collective-permute-start(bf16[24,16,128]{2,1,0:T(8,128)(2,1)S(1)} %shard_map.52.refs_0_), channel_id=1, source_target_pairs={{0,4},{4,0},{8,12},{12,8},{1,5},{5,1},{9,13},{13,9},{2,6},{6,2},{1... | collective-permute-start | bytes 294920 | tf_op jit(solution)/shard_map/ppermute | solution.py:212
  18.1 0.0 collective-permute-done.5.got
  18.2 0.7 %collective-permute-start.6 = (bf16[24,16,128]{2,1,0:T(8,128)(2,1)S(1)}, bf16[24,16,128]{2,1,0:T(8,128)(2,1)S(1)}, u32[]{:S(2)}, u32[]{:S(2)}) collective-permute-start(bf16[24,16,128]{2,1,0:T(8,128)(2,1)S(1)} %shard_map.54.before), channel_id=1, source_target_pairs={{0,12},{4,8},{8,4},{12,0},{1,13},{5,9},{9,5},{13,1},{2,14},{6,10},... | collective-permute-start | bytes 294920 | tf_op jit(solution)/shard_map/ppermute | solution.py:212
  18.8 0.0 collective-permute-done.7.got
  18.9 1.5 %collective-permute-start.8 = (bf16[24,16,128]{2,1,0:T(8,128)(2,1)S(1)}, bf16[24,16,128]{2,1,0:T(8,128)(2,1)S(1)}, u32[]{:S(2)}, u32[]{:S(2)}) collective-permute-start(bf16[24,16,128]{2,1,0:T(8,128)(2,1)S(1)} %shard_map.56), channel_id=1, source_target_pairs={{0,2},{2,0},{1,3},{3,1},{4,6},{6,4},{5,7},{7,5},{8,10},{10,8},{9,1... | collective-permute-start | bytes 294920 | tf_op jit(solution)/shard_map/ppermute | solution.py:209
  20.3 2.4 %collective-permute-done.3.got = bf16[24,16,128]{2,1,0:T(8,128)(2,1)S(1)} collective-permute-done((bf16[24,16,128]{2,1,0:T(8,128)(2,1)S(1)}, bf16[24,16,128]{2,1,0:T(8,128)(2,1)S(1)}, u32[]{:S(2)}, u32[]{:S(2)}) %collective-permute-start.3) | collective-permute-done | bytes 98336 | tf_op jit(solution)/shard_map/ppermute | solution.py:212
  22.7 0.5 %collective-permute-done.4.got = bf16[24,16,128]{2,1,0:T(8,128)(2,1)S(1)} collective-permute-done((bf16[24,16,128]{2,1,0:T(8,128)(2,1)S(1)}, bf16[24,16,128]{2,1,0:T(8,128)(2,1)S(1)}, u32[]{:S(2)}, u32[]{:S(2)}) %collective-permute-start.4) | collective-permute-done | bytes 98336 | tf_op jit(solution)/shard_map/ppermute | solution.py:212
  23.2 1.5 %collective-permute-done.6.got = bf16[24,16,128]{2,1,0:T(8,128)(2,1)S(1)} collective-permute-done((bf16[24,16,128]{2,1,0:T(8,128)(2,1)S(1)}, bf16[24,16,128]{2,1,0:T(8,128)(2,1)S(1)}, u32[]{:S(2)}, u32[]{:S(2)}) %collective-permute-start.6) | collective-permute-done | bytes 98336 | tf_op jit(solution)/shard_map/ppermute | solution.py:212
  24.8 0.0 collective-permute-done.8.got
  24.8 0.8 %shard_map.57 = f32[16,24,128]{2,1,0:T(8,128)} custom-call(f32[24,16,128]{2,1,0:T(8,128)S(1)} %shard_map.55.so_far, bf16[24,16,128]{2,1,0:T(8,128)(2,1)S(1)} %collective-permute-done.8.got), custom_call_target="tpu_custom_call" | custom-call | tf_op jit(solution)/shard_map/pallas_call | solution.py:151
  (7 shorter events, 0.1 us)
Async XLA Ops:
  0.0 4.9 %collective-permute-start.1 = (s32[3,1,1,2,2,64]{5,4,3,2,1,0:T(2,128)}, s32[3,1,1,2,2,64]{5,4,3,2,1,0:T(2,128)S(1)}, u32[]{:S(2)}, u32[]{:S(2)}) collective-permute-start(s32[3,1,1,2,2,64]{5,4,3,2,1,0:T(2,128)} %table.1), channel_id=1, source_target_pairs={{0,3},{1,2},{2,1},{3,0},{4,7},{5,6},{6,5},{7,4},{8,11},{9,10},{10,... | collective-permute-start | bytes 9224 | tf_op jit(solution)/shard_map/ppermute | solution.py:170
  2.4 4.4 %collective-permute-start = (bf16[12,128,128]{2,1,0:T(8,128)(2,1)}, bf16[12,128,128]{2,1,0:T(8,128)(2,1)S(1)}, u32[]{:S(2)}, u32[]{:S(2)}) collective-permute-start(bf16[12,128,128]{2,1,0:T(8,128)(2,1)} %wave.1), channel_id=1, source_target_pairs={{0,1},{1,0},{2,3},{3,2},{4,5},{5,4},{6,7},{7,6},{8,9},{9,8},{10,11... | collective-permute-start | bytes 1179656 | tf_op jit(solution)/shard_map/ppermute | solution.py:171
  8.1 6.0 %collective-permute-start.2 = (bf16[24,16,128]{2,1,0:T(8,128)(2,1)S(1)}, bf16[24,16,128]{2,1,0:T(8,128)(2,1)S(1)}, u32[]{:S(2)}, u32[]{:S(2)}) collective-permute-start(bf16[24,16,128]{2,1,0:T(8,128)(2,1)S(1)} %get-tuple-element.21), channel_id=1, source_target_pairs={{0,2},{2,0},{1,3},{3,1},{4,6},{6,4},{5,7},{7,5},{8,10},{10,8},{9,1... | collective-permute-start | bytes 294920 | tf_op jit(solution)/shard_map/ppermute | solution.py:209
  9.6 8.6 %collective-permute-start.5 = (bf16[24,16,128]{2,1,0:T(8,128)(2,1)S(1)}, bf16[24,16,128]{2,1,0:T(8,128)(2,1)S(1)}, u32[]{:S(2)}, u32[]{:S(2)}) collective-permute-start(bf16[24,16,128]{2,1,0:T(8,128)(2,1)S(1)} %get-tuple-element.22), channel_id=1, source_target_pairs={{0,2},{2,0},{1,3},{3,1},{4,6},{6,4},{5,7},{7,5},{8,10},{10,8},{9,1... | collective-permute-start | bytes 294920 | tf_op jit(solution)/shard_map/ppermute | solution.py:209
  10.2 8.6 %collective-permute-start.7 = (bf16[24,16,128]{2,1,0:T(8,128)(2,1)S(1)}, bf16[24,16,128]{2,1,0:T(8,128)(2,1)S(1)}, u32[]{:S(2)}, u32[]{:S(2)}) collective-permute-start(bf16[24,16,128]{2,1,0:T(8,128)(2,1)S(1)} %get-tuple-element.24), channel_id=1, source_target_pairs={{0,4},{4,0},{8,12},{12,8},{1,5},{5,1},{9,13},{13,9},{2,6},{6,2},{1... | collective-permute-start | bytes 294920 | tf_op jit(solution)/shard_map/ppermute | solution.py:212
  14.2 8.5 %collective-permute-start.3 = (bf16[24,16,128]{2,1,0:T(8,128)(2,1)S(1)}, bf16[24,16,128]{2,1,0:T(8,128)(2,1)S(1)}, u32[]{:S(2)}, u32[]{:S(2)}) collective-permute-start(bf16[24,16,128]{2,1,0:T(8,128)(2,1)S(1)} %shard_map.50.before), channel_id=1, source_target_pairs={{0,8},{4,12},{8,0},{12,4},{1,9},{5,13},{9,1},{13,5},{2,10},{6,14},... | collective-permute-start | bytes 294920 | tf_op jit(solution)/shard_map/ppermute | solution.py:212
  16.9 6.3 %collective-permute-start.4 = (bf16[24,16,128]{2,1,0:T(8,128)(2,1)S(1)}, bf16[24,16,128]{2,1,0:T(8,128)(2,1)S(1)}, u32[]{:S(2)}, u32[]{:S(2)}) collective-permute-start(bf16[24,16,128]{2,1,0:T(8,128)(2,1)S(1)} %shard_map.52.refs_0_), channel_id=1, source_target_pairs={{0,4},{4,0},{8,12},{12,8},{1,5},{5,1},{9,13},{13,9},{2,6},{6,2},{1... | collective-permute-start | bytes 294920 | tf_op jit(solution)/shard_map/ppermute | solution.py:212
  18.2 6.6 %collective-permute-start.6 = (bf16[24,16,128]{2,1,0:T(8,128)(2,1)S(1)}, bf16[24,16,128]{2,1,0:T(8,128)(2,1)S(1)}, u32[]{:S(2)}, u32[]{:S(2)}) collective-permute-start(bf16[24,16,128]{2,1,0:T(8,128)(2,1)S(1)} %shard_map.54.before), channel_id=1, source_target_pairs={{0,12},{4,8},{8,4},{12,0},{1,13},{5,9},{9,5},{13,1},{2,14},{6,10},... | collective-permute-start | bytes 294920 | tf_op jit(solution)/shard_map/ppermute | solution.py:212
  18.9 5.9 %collective-permute-start.8 = (bf16[24,16,128]{2,1,0:T(8,128)(2,1)S(1)}, bf16[24,16,128]{2,1,0:T(8,128)(2,1)S(1)}, u32[]{:S(2)}, u32[]{:S(2)}) collective-permute-start(bf16[24,16,128]{2,1,0:T(8,128)(2,1)S(1)} %shard_map.56), channel_id=1, source_target_pairs={{0,2},{2,0},{1,3},{3,1},{4,6},{6,4},{5,7},{7,5},{8,10},{10,8},{9,1... | collective-permute-start | bytes 294920 | tf_op jit(solution)/shard_map/ppermute | solution.py:209
